TPU v7x, 32 devices: a whole 2x2x4 slice. The times are simulated.
32 devices in a mesh: seq: 4 (over x, core), head: 8 (over z, y).
Axes of the slice: x: 2, y: 2, z: 4, core: 2. Of those that a mesh axis runs over, the one named last changes fastest.
Arguments:
- qk_in: bfloat16 [4, 4096, 2, 2048], P(None, 'seq', None, 'head'), may hold values from -6 to 6
- v_in: bfloat16 [4, 4096, 4096], P(None, 'seq', 'head'), may hold values from -6 to 6
- gate_z: bfloat16 [4, 4096, 4096], P(None, 'seq', 'head'), may hold values from -6 to 6
- conv_qk: bfloat16 [4, 2, 2048], P(None, None, 'head'), may hold values from -3 to 3
- conv_v: bfloat16 [4, 4096], P(None, 'head'), may hold values from -3 to 3
- log_decay: float32 [4, 32, 4096], P(None, 'head', 'seq'), may hold values from -0.7 to 0
- write_gain: float32 [4, 32, 4096], P(None, 'head', 'seq'), may hold values from 0 to 1
- norm_gain: float32 [128], replicated, may hold values from 0.5 to 1.5
- prompt_lengths: int32 [4], replicated, may hold values from 1 to 4096, 10240 in all
- placement: int32 [4, 8], P('seq'), may hold values from 0 to 3
Outputs:
- attended: bfloat16 [4, 4096, 4096], P(None, 'seq', 'head')
- rollout_state: float32 [4, 8, 32, 128, 128], P('seq', 'head')
Inputs may be any that keep to these rules, and one draw needn't show every extreme that they name: `prompt_lengths`: the largest length is exactly 4096; the lengths sum to 10240. Device (s, r) serves prompt placement[s, r]; the values 0 and 3 each occur at least once.
All inputs are finite; a program needn't handle non-finite values.
Results may differ from a plain program's by a relative error of at most 0.02.
Values may be sent and summed in bfloat16 or wider, within the bound.
No kernel may reach another device: no remote copies, remote signals or barrier semaphores. Data moves between devices by JAX's collectives and lax.ppermute only.
A program may use at most 128 MiB of HBM per device.

v0:
```python
import functools

import jax
import jax.numpy as jnp
from jax import lax
from jax.experimental import pallas as pl
from jax.experimental.pallas import tpu as pltpu
from jax.sharding import PartitionSpec as P

DK = 128
DV = 128
CONV = 4
BLOCK = 128
TINY = 16
EDGE = 8
EPSILON = 1e-06
VMEM_BYTES = 56 * 1024 * 1024
F32 = jnp.float32
BF16 = jnp.bfloat16


def dot(a, b):
    return lax.dot_general(a, b, (((1,), (0,)), ((), ())), preferred_element_type=F32)


def silu(x):
    half = 0.5 * x
    return half + half * jnp.tanh(half)


def load_padded(pad_ref, halo, raw_ref):
    rim = halo.shape[0]
    pad_ref[0:rim, :] = halo
    pad_ref[rim:, :] = raw_ref[0].astype(F32)


def mixed_rows(pad_ref, taps, rim, first, step, c):
    total = None
    for i in range(CONV):
        start = rim + first + step * (c * BLOCK + i - (CONV - 1))
        stride = None if step == 1 else step
        term = pad_ref[pl.ds(start, BLOCK, stride), :] * taps[i]
        total = term if total is None else total + term
    return silu(total)


def unit_rows(x):
    return x * lax.rsqrt(jnp.sum(x * x, axis=-1, keepdims=True) + EPSILON)


def heads_rows(ref, head, group):
    every = ref[0]
    rows = every[:group]
    for n in range(1, every.shape[0] // group):
        rows = jnp.where(head == n, every[n * group : (n + 1) * group], rows)
    return rows


def gates_of_heads(log_ref, gain_ref, used, head, group):
    log = heads_rows(log_ref, head, group)
    lane = lax.broadcasted_iota(jnp.int32, log.shape, 1)
    valid = lane < used
    cum = jnp.where(valid, log, 0.0)
    gain = jnp.where(valid, heads_rows(gain_ref, head, group), 0.0)
    shift = 1
    while shift < BLOCK:
        cum = cum + jnp.where(lane % BLOCK >= shift, pltpu.roll(cum, shift, 1), 0.0)
        shift *= 2
    return cum, gain


def as_columns(rows, chunks):
    parts = [rows[:, c * BLOCK : (c + 1) * BLOCK] for c in range(chunks)]
    short = BLOCK - 8 * chunks
    if short:
        parts.append(jnp.zeros((short, BLOCK), F32))
    return jnp.concatenate(parts, axis=0).T


def prepare_kernel(
    groups, group, chunks, key_heads,
    length_ref, qk_ref, v_ref, halo_ref, qk_taps_ref, v_taps_ref, log_ref, gain_ref,
    kn_ref, wu_ref, start_ref, state_ref, trans_ref,
    qk_pad, v_pad, halo_scr, taps_scr, m_scr, b_scr, fade_scr, st_scr, a_scr, x_scr,
):
    step = pl.program_id(0)
    now = jnp.minimum(step, groups - 1)
    prompt, head = now // key_heads, now % key_heads
    used = length_ref[prompt] - lax.axis_index("seq") * (chunks * BLOCK)
    units = [(h, c) for c in range(chunks) for h in range(group)]

    @pl.when(jnp.logical_and(step < groups, used <= 0))
    def _():
        kn_ref[...] = jnp.zeros_like(kn_ref)
        wu_ref[...] = jnp.zeros_like(wu_ref)
        for h, c in units:
            fade_scr[c, pl.ds(step * group + h, 1), :] = jnp.ones((1, BLOCK), F32)
            m_scr[c, step * group + h] = jnp.zeros((DK, DK), BF16)
            b_scr[c, step * group + h] = jnp.zeros((DK, DV), F32)

    @pl.when(jnp.logical_and(step < groups, used > 0))
    def _():
        @pl.when(head == 0)
        def _():
            halo = halo_ref[0].astype(F32)
            halo_scr[...] = halo
            taps_scr[...] = qk_taps_ref[...].astype(F32)
            load_padded(qk_pad, halo[: 2 * EDGE], qk_ref)

        v_pad[EDGE:, :] = v_ref[0].astype(F32)
        for i in range(CONV - 1):
            for h in range(group):
                source = 2 * EDGE + i * key_heads * group + head * group + h
                v_pad[EDGE - CONV + 1 + i : EDGE - CONV + 2 + i, h * DV : (h + 1) * DV] = halo_scr[
                    pl.ds(source, 1), :
                ]
        k_taps = [taps_scr[pl.ds(i * 2 * key_heads + 2 * head + 1, 1), :] for i in range(CONV)]
        v_all_taps = v_taps_ref[...].astype(F32)
        v_taps = [v_all_taps[i : i + 1] for i in range(CONV)]

        cum, gain = gates_of_heads(log_ref, gain_ref, used, head, group)
        faded = jnp.exp(cum)
        columns = as_columns(jnp.concatenate([cum, gain, gain * faded, faded], axis=0), chunks)

        def column(which, h, c):
            n = c * 8 + which * group + h
            return columns[:, n : n + 1]

        row = lax.broadcasted_iota(jnp.int32, (BLOCK, BLOCK), 0)
        lane = lax.broadcasted_iota(jnp.int32, (BLOCK, BLOCK), 1)
        below = row > lane
        small_row = lax.broadcasted_iota(jnp.int32, (TINY, BLOCK), 0)
        small_lane = lax.broadcasted_iota(jnp.int32, (TINY, BLOCK), 1)
        part_of = small_lane // TINY
        tiny_eye = jnp.where(small_row == small_lane % TINY, 1.0, 0.0).astype(F32)

        keys = []
        for c in range(chunks):
            kc = mixed_rows(qk_pad, k_taps, 2 * EDGE, 2 * head + 1, 2 * key_heads, c)
            kc = unit_rows(kc).astype(BF16)
            kn_ref[0, c * BLOCK : (c + 1) * BLOCK, :] = kc
            keys.append(kc)
        turned = [kc.T for kc in keys]

        compact = {}
        for c in range(chunks):
            kk = dot(keys[c], turned[c])
            for h in range(group):
                r = h * chunks + c
                span = slice(c * BLOCK, (c + 1) * BLOCK)
                ratio = jnp.exp(column(0, h, c) - cum[h : h + 1, span])
                strict = jnp.where(below, column(1, h, c) * ratio * kk, 0.0)
                a_scr[r] = strict.astype(BF16)
                tiny = strict[0:TINY]
                for b in range(1, BLOCK // TINY):
                    tiny = jnp.where(part_of == b, strict[b * TINY : (b + 1) * TINY], tiny)
                compact[r] = tiny

        solved = {r: tiny_eye for r in compact}
        for j in range(TINY - 1):
            pick = part_of * TINY + j
            for r in solved:
                factor = jnp.take_along_axis(compact[r], pick, axis=1, mode="promise_in_bounds")
                solved[r] = solved[r] - factor * solved[r][j : j + 1, :]
        for r in solved:
            for b in range(BLOCK // TINY):
                x_scr[r, b * TINY : (b + 1) * TINY, :] = jnp.where(
                    part_of == b, solved[r], 0.0
                ).astype(BF16)

        size = TINY
        while size < BLOCK:
            odd = [s for s in range(size, BLOCK, 2 * size)]
            half_lane = lax.broadcasted_iota(jnp.int32, (BLOCK // 2, BLOCK), 1)
            half_row = lax.broadcasted_iota(jnp.int32, (BLOCK // 2, BLOCK), 0)
            left = half_lane // size == 2 * (half_row // size)
            moved = {}
            for h, c in units:
                r = h * chunks + c
                lower = jnp.concatenate([a_scr[r, s : s + size, :] for s in odd], axis=0)
                lower = jnp.where(left, lower, jnp.zeros_like(lower))
                moved[r] = dot(lower, x_scr[r]).astype(BF16)
            for h, c in units:
                r = h * chunks + c
                spread = []
                for n in range(len(odd)):
                    spread.append(jnp.zeros((size, BLOCK), BF16))
                    spread.append(moved[r][n * size : (n + 1) * size])
                own = jnp.concatenate([x_scr[r, s : s + size, :] for s in odd], axis=0)
                update = own.astype(F32) - dot(own, jnp.concatenate(spread, axis=0))
                update = update.astype(BF16)
                for n, s in enumerate(odd):
                    x_scr[r, s : s + size, :] = update[n * size : (n + 1) * size]
            size *= 2

        for c in range(chunks):
            vc = mixed_rows(v_pad, v_taps, EDGE, 0, 1, c).astype(BF16).astype(F32)
            kc = keys[c].astype(F32)
            for h in range(group):
                r = h * chunks + c
                right = jnp.concatenate(
                    [
                        (kc * column(2, h, c)).astype(BF16),
                        (vc[:, h * DV : (h + 1) * DV] * column(1, h, c)).astype(BF16),
                    ],
                    axis=1,
                )
                wu_ref[0, r] = dot(x_scr[r], right).astype(BF16)
        for c in range(chunks):
            sums = cum[:, c * BLOCK : (c + 1) * BLOCK]
            last = sums[:, BLOCK - 1 : BLOCK]
            tail = jnp.exp(last - sums)
            fade = jnp.broadcast_to(jnp.exp(last), (group, BLOCK))
            for h in range(group):
                r = h * chunks + c
                fade_scr[c, pl.ds(step * group + h, 1), :] = fade[h : h + 1]
                scaled = (turned[c].astype(F32) * tail[h : h + 1, :]).astype(BF16)
                both = dot(scaled, wu_ref[0, r])
                m_scr[c, step * group + h] = (-both[:, :DK]).astype(BF16)
                b_scr[c, step * group + h] = both[:, DK:]

    @pl.when(step >= groups)
    def _():
        c = step - groups
        chains = groups * group

        @pl.when(c == 0)
        def _():
            row = lax.broadcasted_iota(jnp.int32, (DK, DV + DK), 0)
            lane = lax.broadcasted_iota(jnp.int32, (DK, DV + DK), 1)
            first = jnp.where(lane == row + DV, 1.0, 0.0).astype(F32)
            for n in range(chains):
                st_scr[n] = first

        fades = fade_scr[c]
        for low in range(0, chains, 4):
            some = range(low, low + 4)
            narrow = {}
            for n in some:
                narrow[n] = st_scr[n].astype(BF16)
                start_ref[0, n] = narrow[n]
            moved = {n: dot(m_scr[c, n], narrow[n]) for n in some}
            after = {}
            for n in some:
                fade = fades[n : n + 1, :]
                state = st_scr[n, :, :DV] * fade + (moved[n][:, :DV] + b_scr[c, n])
                trans = st_scr[n, :, DV:] * fade + moved[n][:, DV:]
                after[n] = state, trans
            for n in some:
                st_scr[n, :, :DV] = after[n][0]
                st_scr[n, :, DV:] = after[n][1]

        @pl.when(c == chunks - 1)
        def _():
            for n in range(chains):
                state_ref[n] = st_scr[n, :, :DV].astype(BF16)
                trans_ref[n] = st_scr[n, :, DV:].astype(BF16)


def prepare(lengths, qk_rows, v_in, halo, qk_taps, v_taps, log_decay, write_gain, key_heads):
    prompts, tok = v_in.shape[:2]
    value_heads = v_in.shape[2] // DV
    group = value_heads // key_heads
    groups = prompts * key_heads
    chunks = tok // BLOCK
    chains = groups * group
    rows = group * chunks
    wide = group * DV

    def prompt_of(i):
        return jnp.minimum(i, groups - 1) // key_heads

    def head_of(i):
        return jnp.minimum(i, groups - 1) % key_heads

    def rows_of(i, lengths):
        return (prompt_of(i), 0, head_of(i))

    def whole_of(i, lengths):
        return (prompt_of(i), 0, 0)

    return pl.pallas_call(
        functools.partial(prepare_kernel, groups, group, chunks, key_heads),
        grid_spec=pltpu.PrefetchScalarGridSpec(
            num_scalar_prefetch=1,
            grid=(groups + chunks,),
            in_specs=[
                pl.BlockSpec((1,) + qk_rows.shape[1:], whole_of),
                pl.BlockSpec((1, tok, wide), rows_of),
                pl.BlockSpec((1,) + halo.shape[1:], whole_of),
                pl.BlockSpec(qk_taps.shape, lambda i, lengths: (0, 0)),
                pl.BlockSpec((CONV, wide), lambda i, lengths: (0, head_of(i))),
                pl.BlockSpec((1, value_heads, tok), whole_of),
                pl.BlockSpec((1, value_heads, tok), whole_of),
            ],
            out_specs=[
                pl.BlockSpec((1, tok, DK), rows_of),
                pl.BlockSpec((1, rows, BLOCK, DK + DV), lambda i, lengths: (jnp.minimum(i, groups - 1), 0, 0, 0)),
                pl.BlockSpec((1, chains, DK, DV + DK), lambda i, lengths: (jnp.maximum(i - groups, 0), 0, 0, 0)),
                pl.BlockSpec((chains, DK, DV), lambda i, lengths: (0, 0, 0)),
                pl.BlockSpec((chains, DK, DK), lambda i, lengths: (0, 0, 0)),
            ],
            scratch_shapes=[
                pltpu.VMEM((qk_rows.shape[1] + 2 * EDGE, DK), F32),
                pltpu.VMEM((tok + EDGE, wide), F32),
                pltpu.VMEM(halo.shape[1:], F32),
                pltpu.VMEM(qk_taps.shape, F32),
                pltpu.VMEM((chunks, chains, DK, DK), BF16),
                pltpu.VMEM((chunks, chains, DK, DV), F32),
                pltpu.VMEM((chunks, chains, BLOCK), F32),
                pltpu.VMEM((chains, DK, DV + DK), F32),
                pltpu.VMEM((rows, BLOCK, BLOCK), BF16),
                pltpu.VMEM((rows, BLOCK, BLOCK), BF16),
            ],
        ),
        out_shape=[
            jax.ShapeDtypeStruct((prompts, tok, key_heads * DK), BF16),
            jax.ShapeDtypeStruct((groups, rows, BLOCK, DK + DV), BF16),
            jax.ShapeDtypeStruct((chunks, chains, DK, DV + DK), BF16),
            jax.ShapeDtypeStruct((chains, DK, DV), BF16),
            jax.ShapeDtypeStruct((chains, DK, DK), BF16),
        ],
        compiler_params=pltpu.CompilerParams(vmem_limit_bytes=VMEM_BYTES),
        cost_estimate=pl.CostEstimate(flops=40 * 10**9, bytes_accessed=28 * 2**20, transcendentals=10**7),
        name="prepare",
    )(lengths, qk_rows, v_in, halo, qk_taps, v_taps, log_decay, write_gain)


def outputs_kernel(
    groups, group, chunks, key_heads,
    length_ref, qk_ref, halo_ref, qk_taps_ref, kn_ref, wu_ref, start_ref, log_ref, gain_ref,
    own_ref, map_ref,
    qk_pad, taps_scr,
):
    step = pl.program_id(0)
    prompt, head = step // key_heads, step % key_heads
    used = length_ref[prompt] - lax.axis_index("seq") * (chunks * BLOCK)

    @pl.when(used <= 0)
    def _():
        own_ref[...] = jnp.zeros_like(own_ref)
        map_ref[...] = jnp.zeros_like(map_ref)

    @pl.when(used > 0)
    def _():
        @pl.when(head == 0)
        def _():
            taps_scr[...] = qk_taps_ref[...].astype(F32)
            load_padded(qk_pad, halo_ref[0].astype(F32)[: 2 * EDGE], qk_ref)

        q_taps = [taps_scr[pl.ds(i * 2 * key_heads + 2 * head, 1), :] for i in range(CONV)]
        cum, gain = gates_of_heads(log_ref, gain_ref, used, head, group)
        faded = jnp.exp(cum)
        columns = as_columns(jnp.concatenate([cum, faded, gain, gain], axis=0), chunks)

        def column(which, h, c):
            n = c * 8 + which * group + h
            return columns[:, n : n + 1]

        row = lax.broadcasted_iota(jnp.int32, (BLOCK, BLOCK), 0)
        lane = lax.broadcasted_iota(jnp.int32, (BLOCK, BLOCK), 1)
        upto = row >= lane
        for c in range(chunks):
            span = slice(c * BLOCK, (c + 1) * BLOCK)
            qc = mixed_rows(qk_pad, q_taps, 2 * EDGE, 2 * head, 2 * key_heads, c)
            qc = unit_rows(qc).astype(BF16)
            qk = dot(qc, kn_ref[0, span, :].T)
            q_wide = qc.astype(F32)
            for h in range(group):
                r = h * chunks + c
                ratio = jnp.exp(column(0, h, c) - cum[h : h + 1, span])
                scores = jnp.where(upto, ratio * qk, 0.0).astype(BF16)
                both = dot(scores, wu_ref[0, r])
                seen = (q_wide * column(1, h, c) - both[:, :DK]).astype(BF16)
                out = dot(seen, start_ref[c, h])
                cols = slice(h * DV, (h + 1) * DV)
                own_ref[0, span, cols] = (out[:, :DV] + both[:, DK:]).astype(BF16)
                map_ref[0, span, cols] = out[:, DV:].astype(BF16)


def local_outputs(lengths, qk_rows, halo, qk_taps, kn, wu, starts, log_decay, write_gain, key_heads):
    prompts, tok = kn.shape[:2]
    groups, rows = wu.shape[:2]
    chunks = tok // BLOCK
    group = rows // chunks
    wide = group * DV
    value_heads = key_heads * group

    def rows_of(i, lengths):
        return (i // key_heads, 0, i % key_heads)

    def whole_of(i, lengths):
        return (i // key_heads, 0, 0)

    return pl.pallas_call(
        functools.partial(outputs_kernel, groups, group, chunks, key_heads),
        grid_spec=pltpu.PrefetchScalarGridSpec(
            num_scalar_prefetch=1,
            grid=(groups,),
            in_specs=[
                pl.BlockSpec((1,) + qk_rows.shape[1:], whole_of),
                pl.BlockSpec((1,) + halo.shape[1:], whole_of),
                pl.BlockSpec(qk_taps.shape, lambda i, lengths: (0, 0)),
                pl.BlockSpec((1, tok, DK), rows_of),
                pl.BlockSpec((1, rows, BLOCK, DK + DV), lambda i, lengths: (i, 0, 0, 0)),
                pl.BlockSpec((chunks, group, DK, DV + DK), lambda i, lengths: (0, i, 0, 0)),
                pl.BlockSpec((1, value_heads, tok), whole_of),
                pl.BlockSpec((1, value_heads, tok), whole_of),
            ],
            out_specs=[
                pl.BlockSpec((1, tok, wide), rows_of),
                pl.BlockSpec((1, tok, wide), rows_of),
            ],
            scratch_shapes=[
                pltpu.VMEM((qk_rows.shape[1] + 2 * EDGE, DK), F32),
                pltpu.VMEM(qk_taps.shape, F32),
            ],
        ),
        out_shape=[
            jax.ShapeDtypeStruct((prompts, tok, value_heads * DV), BF16),
            jax.ShapeDtypeStruct((prompts, tok, value_heads * DV), BF16),
        ],
        compiler_params=pltpu.CompilerParams(vmem_limit_bytes=VMEM_BYTES),
        cost_estimate=pl.CostEstimate(flops=20 * 10**9, bytes_accessed=28 * 2**20, transcendentals=10**7),
        name="local_outputs",
    )(lengths, qk_rows, halo, qk_taps, kn, wu, starts, log_decay, write_gain)


def gate_kernel(group, chunks, key_heads, length_ref, own_ref, map_ref, enter_ref, z_ref, norm_ref, out_ref):
    used = length_ref[pl.program_id(0) // key_heads] - lax.axis_index("seq") * (chunks * BLOCK)

    @pl.when(used <= 0)
    def _():
        out_ref[...] = jnp.zeros_like(out_ref)

    @pl.when(used > 0)
    def _():
        row = lax.broadcasted_iota(jnp.int32, (BLOCK, DV), 0)
        norm_gain = norm_ref[...]
        for c in range(chunks):
            span = slice(c * BLOCK, (c + 1) * BLOCK)
            valid = row + c * BLOCK < used
            for h in range(group):
                cols = slice(h * DV, (h + 1) * DV)
                raw = own_ref[0, span, cols].astype(F32) + dot(map_ref[0, span, cols], enter_ref[h])
                mean = jnp.sum(raw * raw, axis=-1, keepdims=True) * (1.0 / DV)
                gated = raw * lax.rsqrt(mean + EPSILON) * norm_gain * silu(z_ref[0, span, cols].astype(F32))
                out_ref[0, span, cols] = jnp.where(valid, gated, 0.0).astype(BF16)


def gate(lengths, own, maps, enter, gate_z, norm_gain, key_heads):
    prompts, tok, width = own.shape
    value_heads = width // DV
    group = value_heads // key_heads
    groups = prompts * key_heads
    wide = group * DV

    def rows_of(i, lengths):
        return (i // key_heads, 0, i % key_heads)

    return pl.pallas_call(
        functools.partial(gate_kernel, group, tok // BLOCK, key_heads),
        grid_spec=pltpu.PrefetchScalarGridSpec(
            num_scalar_prefetch=1,
            grid=(groups,),
            in_specs=[
                pl.BlockSpec((1, tok, wide), rows_of),
                pl.BlockSpec((1, tok, wide), rows_of),
                pl.BlockSpec((group, DK, DV), lambda i, lengths: (i, 0, 0)),
                pl.BlockSpec((1, tok, wide), rows_of),
                pl.BlockSpec((1, DV), lambda i, lengths: (0, 0)),
            ],
            out_specs=pl.BlockSpec((1, tok, wide), rows_of),
        ),
        out_shape=jax.ShapeDtypeStruct((prompts, tok, width), BF16),
        compiler_params=pltpu.CompilerParams(vmem_limit_bytes=VMEM_BYTES),
        cost_estimate=pl.CostEstimate(flops=10 * 10**9, bytes_accessed=16 * 2**20, transcendentals=10**7),
        name="gate",
    )(lengths, own, maps, enter, gate_z, norm_gain.reshape(1, DV))


def apply_map(trans, state):
    return jnp.einsum("nij,njv->niv", trans, state, preferred_element_type=F32)


def pair_swap(block):
    count = lax.axis_size("seq")
    return lax.ppermute(block, "seq", [(i, i ^ 1) for i in range(count)])


def from_chip_behind(block, distance, skip_first):
    count = lax.axis_size("seq")
    chips = count // 2
    route = [
        (i, ((i // 2 + distance) % chips) * 2 + i % 2)
        for i in range(count)
        if not (skip_first and i < 2)
    ]
    return lax.ppermute(block, "seq", route)


def across_seq(state, trans, meanwhile):
    chips = lax.axis_size("seq") // 2
    core = lax.axis_index("seq") % 2
    chip = lax.axis_index("seq") // 2
    odd = core == 1
    half = state.shape[0] // 2
    state_other, trans_other = pair_swap(state), pair_swap(trans)
    state_early = jnp.where(odd, state_other, state)
    state_late = jnp.where(odd, state, state_other)
    trans_early = jnp.where(odd, trans_other, trans)
    trans_late = jnp.where(odd, trans, trans_other)

    def mine(x):
        return lax.dynamic_slice_in_dim(x, core * half, half, 0)

    chip_state = (apply_map(mine(trans_late), mine(state_early)) + mine(state_late).astype(F32)).astype(BF16)
    chip_trans = apply_map(mine(trans_late), mine(trans_early)).astype(BF16)
    states, transes = [chip_state], [chip_trans]
    for k in range(1, chips):
        states.append(from_chip_behind(chip_state, k, False))
        transes.append(from_chip_behind(chip_trans, k, True))
    beside = meanwhile(chip_state, chip_trans)
    states, transes, beside = lax.optimization_barrier((states, transes, beside))

    def of_chip(parts, j):
        value = parts[0]
        for k in range(1, chips):
            value = jnp.where((chip - k) % chips == j, parts[k], value)
        return value

    entering = jnp.zeros_like(chip_state)
    running = of_chip(states, 0).astype(F32)
    for j in range(1, chips):
        running_b = running.astype(BF16)
        entering = jnp.where(chip == j, running_b, entering)
        running = apply_map(of_chip(transes, j), running_b) + of_chip(states, j).astype(F32)
    both = jnp.stack([entering, running.astype(BF16)])
    other = pair_swap(both)
    both = jnp.concatenate([jnp.where(odd, other, both), jnp.where(odd, both, other)], axis=1)
    chip_enter, final = both[0], both[1]
    second = (apply_map(trans_early, chip_enter) + state_early.astype(F32)).astype(BF16)
    return jnp.where(odd, second, chip_enter), final, beside


def shards(
    qk_in, v_in, gate_z, conv_qk, conv_v, log_decay, write_gain, norm_gain, prompt_lengths, placement,
):
    prompts, tok = qk_in.shape[:2]
    key_heads = qk_in.shape[3] // DK
    value_heads = v_in.shape[2] // DV
    rim = CONV - 1
    seq_count = lax.axis_size("seq")
    head_count = lax.axis_size("head")

    def by_head(x):
        x = x.reshape(x.shape[0], x.shape[1], 2, key_heads, DK)
        return jnp.transpose(x, (0, 1, 3, 2, 4)).reshape(x.shape[0], -1, DK)

    qk_rows = by_head(qk_in)
    qk_taps = by_head(conv_qk[None])[0]
    qk_tail = qk_rows[:, (tok - rim) * 2 * key_heads :]
    v_tail = v_in[:, tok - rim :].reshape(prompts, rim * value_heads, DV)
    front = 2 * EDGE - qk_tail.shape[1]
    back = 2 * EDGE - v_tail.shape[1]
    tails = jnp.concatenate(
        [
            jnp.zeros((prompts, front, DK), BF16),
            qk_tail,
            v_tail,
            jnp.zeros((prompts, back, DK), BF16),
        ],
        axis=1,
    )
    halo = lax.ppermute(tails, "seq", [(i, i + 1) for i in range(seq_count - 1)])
    kn, wu, starts, state, trans = prepare(
        prompt_lengths, qk_rows, v_in, halo, qk_taps, conv_v, log_decay, write_gain, key_heads
    )

    def meanwhile(*ready):
        rows = lax.optimization_barrier((qk_rows, ready))[0]
        return local_outputs(
            prompt_lengths, rows, halo, qk_taps, kn, wu, starts, log_decay, write_gain, key_heads
        )

    enter, final, (own, maps) = across_seq(state, trans, meanwhile)
    attended = gate(prompt_lengths, own, maps, enter, gate_z, norm_gain, key_heads)
    final = final.reshape(prompts, value_heads, DK, DV)
    outgoing = jnp.take(final, placement[0], axis=0)
    rollout = lax.all_to_all(outgoing, "head", 0, 0).astype(F32)
    return attended, rollout.reshape(1, 1, head_count * value_heads, DK, DV)


def solution(mesh):
    return jax.shard_map(
        shards,
        mesh=mesh,
        in_specs=(
            P(None, "seq", None, "head"),
            P(None, "seq", "head"),
            P(None, "seq", "head"),
            P(None, None, "head"),
            P(None, "head"),
            P(None, "head", "seq"),
            P(None, "head", "seq"),
            P(),
            P(),
            P("seq", None),
        ),
        out_specs=(P(None, "seq", "head"), P("seq", "head", None, None, None)),
        check_vma=False,
    )
```

profile of v0, /device:TPU:0, one launch (start us, length us, event | category | flops | bytes accessed | tf_op | source)
XLA Modules:
  0.0 127.9 jit_solution(15229972335582987512)
XLA Ops:
  0.6 0.7 slice.18
  1.4 0.8 slice.13
  2.2 2.4 %collective-permute-start = (bf16[4,32,128]{2,1,0:T(8,128)(2,1)S(1)}, bf16[4,32,128]{2,1,0:T(8,128)(2,1)S(1)}, u32[]{:S(2)}, u32[]{:S(2)}) collective-permute-start(bf16[4,32,128]{2,1,0:T(8,128)(2,1)S(1)} %pad_maximum_fusion.2), channel_id=1, source_target_pairs={{0,8},{8,16},{16,24},{1,9},{9,17},{17,25},{2,10},{10,18},{18,26},{... | collective-permute-start | bytes 98312 | tf_op jit(solution)/shard_map/ppermute | solution.py:575
  4.6 0.8 collective-permute-done.halo_ref
  5.4 0.0 copy-start.3
  5.4 0.6 copy-done.3
  6.0 47.5 %prepare.1 = (bf16[4,1024,256]{2,1,0:T(8,128)(2,1)}, bf16[8,16,128,256]{3,2,1,0:T(8,128)(2,1)}, bf16[8,16,128,256]{3,2,1,0:T(8,128)(2,1)}, bf16[16,128,128]{2,1,0:T(8,128)(2,1)}, bf16[16,128,128]{2,1,0:T(8,128)(2,1)}) custom-call(s32[4]{0:T(128)} %length_ref.5, bf16[4,4096,128]{2,1,0:T(8,128)(2,1)} %bitcast.34, bf16[4,1024,512]{2,1,0:T(8,128)(2,1)} %v_ref.1, ...), custom_call_target="tpu_custom_call" | custom-call | flops 40000000000 | bytes 29360128 | tf_op jit(solution)/shard_map/prepare/pallas_call | solution.py:282
  53.5 0.0 copy-start
  53.5 0.0 copy-start.1
  53.5 2.8 %collective-permute-start.1 = (bf16[16,128,128]{2,1,0:T(8,128)(2,1)}, bf16[16,128,128]{2,1,0:T(8,128)(2,1)S(1)}, u32[]{:S(2)}, u32[]{:S(2)}) collective-permute-start(bf16[16,128,128]{2,1,0:T(8,128)(2,1)} %get-tuple-element.16), channel_id=1, source_target_pairs={{0,8},{8,0},{16,24},{24,16},{1,9},{9,1},{17,25},{25,17},{2,10},{10... | collective-permute-start | bytes 1572872 | tf_op jit(solution)/shard_map/ppermute | solution.py:488
  56.4 0.1 collective-permute-start.2
  56.4 1.7 %collective-permute-done.1 = bf16[16,128,128]{2,1,0:T(8,128)(2,1)S(1)} collective-permute-done((bf16[16,128,128]{2,1,0:T(8,128)(2,1)}, bf16[16,128,128]{2,1,0:T(8,128)(2,1)S(1)}, u32[]{:S(2)}, u32[]{:S(2)}) %collective-permute-start.1) | collective-permute-done | bytes 524320 | tf_op jit(solution)/shard_map/ppermute | solution.py:488
  58.1 1.1 broadcast_select_fusion.3
  59.2 1.2 convolution_convert_fusion
  60.4 1.3 %collective-permute-start.4 = (bf16[8,128,128]{2,1,0:T(8,128)(2,1)S(1)}, bf16[8,128,128]{2,1,0:T(8,128)(2,1)S(1)}, u32[]{:S(2)}, u32[]{:S(2)}) collective-permute-start(bf16[8,128,128]{2,1,0:T(8,128)(2,1)S(1)} %convolution_convert_fusion), channel_id=1, source_target_pairs={{16,0},{24,8},{17,1},{25,9},{18,2},{26,10},{19,3},{27,11},{20,4},{... | collective-permute-start | bytes 786440 | tf_op jit(solution)/shard_map/ppermute | solution.py:499
  61.7 0.0 collective-permute-done.2
  61.7 1.1 broadcast_select_fusion.4
  62.8 0.0 copy-done
  62.8 0.0 copy-done.1
  62.8 0.0 copy-start.2
  62.9 0.2 fusion.2
  63.1 2.7 %collective-permute-start.3 = (bf16[8,128,128]{2,1,0:T(8,128)(2,1)S(1)}, bf16[8,128,128]{2,1,0:T(8,128)(2,1)S(1)}, u32[]{:S(2)}, u32[]{:S(2)}) collective-permute-start(bf16[8,128,128]{2,1,0:T(8,128)(2,1)S(1)} %fusion.2), channel_id=1, source_target_pairs={{0,16},{8,24},{16,0},{24,8},{1,17},{9,25},{17,1},{25,9},{2,18},{10... | collective-permute-start | bytes 786440 | tf_op jit(solution)/shard_map/ppermute | solution.py:499
  65.8 0.0 copy-start.4
  65.8 24.2 %local_outputs.1 = (bf16[4,1024,512]{2,1,0:T(8,128)(2,1)}, bf16[4,1024,512]{2,1,0:T(8,128)(2,1)}) custom-call(s32[4]{0:T(128)} %length_ref.5, bf16[4,4096,128]{2,1,0:T(8,128)(2,1)} %bitcast.35, bf16[4,32,128]{2,1,0:T(8,128)(2,1)} %copy-done.3, bf16[16,128]{1,0:T(8,128)(2,1)} %bitcast.37, bf16[4,1024,256]{2,1,0:T(8,128)(2,1)} %get-tuple-element.19.kn_ref, ...), custom_call_target="tpu_custom_call" | custom-call | flops 20000000000 | bytes 29360128 | tf_op jit(solution)/shard_map/local_outputs/pallas_call | solution.py:395
  90.1 0.0 copy-done.2
  90.1 0.0 collective-permute-done.4
  90.1 0.0 collective-permute-done.3
  90.1 0.2 fusion.4
  90.4 0.1 pad_maximum_fusion.1
  90.4 0.1 collective-permute-start.5
  90.5 0.0 copy-done.4
  90.5 1.8 %collective-permute-done.5 = bf16[2,8,128,128]{3,2,1,0:T(8,128)(2,1)S(1)} collective-permute-done((bf16[2,8,128,128]{3,2,1,0:T(8,128)(2,1)S(1)}, bf16[2,8,128,128]{3,2,1,0:T(8,128)(2,1)S(1)}, u32[]{:S(2)}, u32[]{:S(2)}) %collective-permute-start.5) | collective-permute-done | bytes 524320 | tf_op jit(solution)/shard_map/ppermute | solution.py:488
  92.4 0.1 broadcast_select_fusion.1
  92.5 0.7 gather_fusion
  93.3 1.1 broadcast_select_fusion
  94.4 5.8 %all-to-all-start = ((bf16[8,4,128,128]{3,2,1,0:T(8,128)(2,1)}), bf16[8,4,128,128]{3,2,1,0:T(8,128)(2,1)S(1)}, u32[]{:S(2)}, u32[]{:S(2)}) async-start(bf16[8,4,128,128]{3,2,1,0:T(8,128)(2,1)} %broadcast_select_fusion), calls=%async_computation | async-start | bytes 2097152 | tf_op jit(solution)/shard_map/all_to_all | solution.py:590
  100.3 2.2 %fusion.1.enter_ref = bf16[16,128,128]{2,1,0:T(8,128)(2,1)} fusion(bf16[16,128,128]{2,1,0:T(8,128)(2,1)S(1)} %broadcast_select_fusion.3, bf16[16,128,128]{2,1,0:T(8,128)(2,1)} %copy-done.2, bf16[2,8,128,128]{3,2,1,0:T(8,128)(2,1)S(1)} %get-tuple-element.31, bf16[2,8,128,128]{3,2,1,0:T(8,128)(2,1)S(1)} %get-tuple-element.30, pred[]{:T(512)S(6)} %eq.18), kind=kOutput, calls=%fused_computation.3 | convolution fusion | flops 68681728 | bytes 3670017 | tf_op jit(solution)/shard_map/nij,njv->niv/dot_general | solution.py:483
  102.4 11.9 %gate.1 = bf16[4,1024,512]{2,1,0:T(8,128)(2,1)} custom-call(s32[4]{0:T(128)} %length_ref.5, bf16[4,1024,512]{2,1,0:T(8,128)(2,1)} %get-tuple-element.24.own_ref, bf16[4,1024,512]{2,1,0:T(8,128)(2,1)} %get-tuple-element.25.map_ref, bf16[16,128,128]{2,1,0:T(8,128)(2,1)} %fusion.1.enter_ref, bf16[4,1024,512]{2,1,0:T(8,128)(2,1)} %z_ref.1, f32[1,128]{1,0:T(1,128)} %bitcast.38), custom_call_target="tpu_custom_call" | custom-call | flops 10000000000 | bytes 16777216 | tf_op jit(solution)/shard_map/gate/pallas_call | solution.py:461
  114.3 12.0 %all-to-all-done = bf16[8,4,128,128]{3,2,1,0:T(8,128)(2,1)S(1)} async-done(((bf16[8,4,128,128]{3,2,1,0:T(8,128)(2,1)}), bf16[8,4,128,128]{3,2,1,0:T(8,128)(2,1)S(1)}, u32[]{:S(2)}, u32[]{:S(2)}) %all-to-all-start) | async-done | bytes 1048608 | tf_op jit(solution)/shard_map/all_to_all | solution.py:590
  126.3 1.6 %convert.1 = f32[1,1,32,128,128]{4,3,2,1,0:T(8,128)} convert(bf16[1,1,32,128,128]{4,3,2,1,0:T(8,128)(2,1)S(1)} %bitcast.32) | non-fusion elementwise | flops 524288 | bytes 3145728 | tf_op jit(solution)/shard_map/reshape | solution.py:591
  (8 shorter events, 0.1 us)
Async XLA Ops:
  2.2 3.2 %collective-permute-start = (bf16[4,32,128]{2,1,0:T(8,128)(2,1)S(1)}, bf16[4,32,128]{2,1,0:T(8,128)(2,1)S(1)}, u32[]{:S(2)}, u32[]{:S(2)}) collective-permute-start(bf16[4,32,128]{2,1,0:T(8,128)(2,1)S(1)} %pad_maximum_fusion.2), channel_id=1, source_target_pairs={{0,8},{8,16},{16,24},{1,9},{9,17},{17,25},{2,10},{10,18},{18,26},{... | collective-permute-start | bytes 98312 | tf_op jit(solution)/shard_map/ppermute | solution.py:575
  5.4 0.6 copy-start.3
  53.5 9.3 %copy-start = (bf16[16,128,128]{2,1,0:T(8,128)(2,1)S(1)}, bf16[16,128,128]{2,1,0:T(8,128)(2,1)}, u32[]{:S(2)}) copy-start(bf16[16,128,128]{2,1,0:T(8,128)(2,1)} %get-tuple-element.16) | copy-start | bytes 1572868
  53.5 9.3 %copy-start.1 = (bf16[16,128,128]{2,1,0:T(8,128)(2,1)S(1)}, bf16[16,128,128]{2,1,0:T(8,128)(2,1)}, u32[]{:S(2)}) copy-start(bf16[16,128,128]{2,1,0:T(8,128)(2,1)} %get-tuple-element.17) | copy-start | bytes 1572868
  53.5 4.6 %collective-permute-start.1 = (bf16[16,128,128]{2,1,0:T(8,128)(2,1)}, bf16[16,128,128]{2,1,0:T(8,128)(2,1)S(1)}, u32[]{:S(2)}, u32[]{:S(2)}) collective-permute-start(bf16[16,128,128]{2,1,0:T(8,128)(2,1)} %get-tuple-element.16), channel_id=1, source_target_pairs={{0,8},{8,0},{16,24},{24,16},{1,9},{9,1},{17,25},{25,17},{2,10},{10... | collective-permute-start | bytes 1572872 | tf_op jit(solution)/shard_map/ppermute | solution.py:488
  56.4 5.3 %collective-permute-start.2 = (bf16[16,128,128]{2,1,0:T(8,128)(2,1)}, bf16[16,128,128]{2,1,0:T(8,128)(2,1)S(1)}, u32[]{:S(2)}, u32[]{:S(2)}) collective-permute-start(bf16[16,128,128]{2,1,0:T(8,128)(2,1)} %get-tuple-element.17), channel_id=1, source_target_pairs={{0,8},{8,0},{16,24},{24,16},{1,9},{9,1},{17,25},{25,17},{2,10},{10... | collective-permute-start | bytes 1572872 | tf_op jit(solution)/shard_map/ppermute | solution.py:488
  60.4 29.7 %collective-permute-start.4 = (bf16[8,128,128]{2,1,0:T(8,128)(2,1)S(1)}, bf16[8,128,128]{2,1,0:T(8,128)(2,1)S(1)}, u32[]{:S(2)}, u32[]{:S(2)}) collective-permute-start(bf16[8,128,128]{2,1,0:T(8,128)(2,1)S(1)} %convolution_convert_fusion), channel_id=1, source_target_pairs={{16,0},{24,8},{17,1},{25,9},{18,2},{26,10},{19,3},{27,11},{20,4},{... | collective-permute-start | bytes 786440 | tf_op jit(solution)/shard_map/ppermute | solution.py:499
  62.8 27.2 %copy-start.2 = (bf16[16,128,128]{2,1,0:T(8,128)(2,1)}, bf16[16,128,128]{2,1,0:T(8,128)(2,1)S(1)}, u32[]{:S(2)}) copy-start(bf16[16,128,128]{2,1,0:T(8,128)(2,1)S(1)} %broadcast_select_fusion.4) | copy-start | bytes 1572868
  63.1 27.0 %collective-permute-start.3 = (bf16[8,128,128]{2,1,0:T(8,128)(2,1)S(1)}, bf16[8,128,128]{2,1,0:T(8,128)(2,1)S(1)}, u32[]{:S(2)}, u32[]{:S(2)}) collective-permute-start(bf16[8,128,128]{2,1,0:T(8,128)(2,1)S(1)} %fusion.2), channel_id=1, source_target_pairs={{0,16},{8,24},{16,0},{24,8},{1,17},{9,25},{17,1},{25,9},{2,18},{10... | collective-permute-start | bytes 786440 | tf_op jit(solution)/shard_map/ppermute | solution.py:499
  65.8 24.7 %copy-start.4 = (s32[1,8]{1,0:T(1,128)S(1)}, s32[1,8]{1,0:T(1,128)}, u32[]{:S(2)}) copy-start(s32[1,8]{1,0:T(1,128)} %param.19) | copy-start | bytes 100
  90.4 2.0 %collective-permute-start.5 = (bf16[2,8,128,128]{3,2,1,0:T(8,128)(2,1)S(1)}, bf16[2,8,128,128]{3,2,1,0:T(8,128)(2,1)S(1)}, u32[]{:S(2)}, u32[]{:S(2)}) collective-permute-start(bf16[2,8,128,128]{3,2,1,0:T(8,128)(2,1)S(1)} %pad_maximum_fusion.1), channel_id=1, source_target_pairs={{0,8},{8,0},{16,24},{24,16},{1,9},{9,1},{17,25},{25,17},{2,10},{10... | collective-permute-start | bytes 1572872 | tf_op jit(solution)/shard_map/ppermute | solution.py:488
  94.4 31.9 %all-to-all-start = ((bf16[8,4,128,128]{3,2,1,0:T(8,128)(2,1)}), bf16[8,4,128,128]{3,2,1,0:T(8,128)(2,1)S(1)}, u32[]{:S(2)}, u32[]{:S(2)}) async-start(bf16[8,4,128,128]{3,2,1,0:T(8,128)(2,1)} %broadcast_select_fusion), calls=%async_computation | async-start | bytes 2097152 | tf_op jit(solution)/shard_map/all_to_all | solution.py:590
where the time goes:
time: 128 us
  Pallas kernels  83.6 us (65%)
  waiting for transfers between devices  16.4 us (13%)
  starting transfers between devices  15.2 us (12%)
  other arithmetic  5.14 us (4%)
  matrix products  3.81 us (3%)
  local copies, waits for them, and re-layouts  2.9 us (2%)
    pallas_call x1, Pallas kernels, prepare(): pl.pallas_call(functools.partial(prepare_kernel, groups, group, chunks, k...  47.5 us
    pallas_call x1, Pallas kernels, local_outputs(): pl.pallas_call(functools.partial(outputs_kernel, groups, group, chunks, k...  24.2 us
    all_to_all x1, waiting for transfers between devices, shards(): rollout = lax.all_to_all(outgoing, 'head', 0, 0).astype(F32)  12 us
    pallas_call x1, Pallas kernels, gate(): pl.pallas_call(functools.partial(gate_kernel, group, tok // BLOCK, key_he...  11.9 us
    all_to_all x1, starting transfers between devices, shards(): rollout = lax.all_to_all(outgoing, 'head', 0, 0).astype(F32)  5.84 us
    ppermute x2, starting transfers between devices, from_chip_behind(): return lax.ppermute(block, 'seq', route)  4.01 us
    dot_general x4, matrix products, apply_map(): return jnp.einsum('nij,njv->niv', trans, state, preferred_element_type=F32)  3.81 us
    ppermute x3, waiting for transfers between devices, pair_swap(): return lax.ppermute(block, 'seq', [(i, i ^ 1) for i in range(count)])  3.52 us
  transfers between devices with their start and end apart: 7, of which 4 were waited for; matrix products, arithmetic and copies ran while one was open for 5% of the time, Pallas kernels for 28%

commit v1 on v0

v1 whole, which is shorter than its diff:
```python
import functools

import jax
import jax.numpy as jnp
from jax import lax
from jax.experimental import pallas as pl
from jax.experimental.pallas import tpu as pltpu
from jax.sharding import PartitionSpec as P

DK = 128
DV = 128
CONV = 4
BLOCK = 128
TINY = 16
EDGE = 8
EPSILON = 1e-06
VMEM_BYTES = 20 * 1024 * 1024
F32 = jnp.float32
BF16 = jnp.bfloat16


def dot(a, b):
    return lax.dot_general(a, b, (((1,), (0,)), ((), ())), preferred_element_type=F32)


def silu(x):
    half = 0.5 * x
    return half + half * jnp.tanh(half)


def load_padded(pad_ref, halo, raw_ref):
    rim = halo.shape[0]
    pad_ref[0:rim, :] = halo
    pad_ref[rim:, :] = raw_ref[0].astype(F32)


def mixed_rows(pad_ref, taps, rim, first, step, c):
    total = None
    for i in range(CONV):
        start = rim + first + step * (c * BLOCK + i - (CONV - 1))
        stride = None if step == 1 else step
        term = pad_ref[pl.ds(start, BLOCK, stride), :] * taps[i]
        total = term if total is None else total + term
    return silu(total)


def unit_rows(x):
    return x * lax.rsqrt(jnp.sum(x * x, axis=-1, keepdims=True) + EPSILON)


def heads_rows(ref, head, group):
    every = ref[0]
    rows = every[:group]
    for n in range(1, every.shape[0] // group):
        rows = jnp.where(head == n, every[n * group : (n + 1) * group], rows)
    return rows


def gates_of_heads(log_ref, gain_ref, used, head, group):
    log = heads_rows(log_ref, head, group)
    lane = lax.broadcasted_iota(jnp.int32, log.shape, 1)
    valid = lane < used
    cum = jnp.where(valid, log, 0.0)
    gain = jnp.where(valid, heads_rows(gain_ref, head, group), 0.0)
    shift = 1
    while shift < BLOCK:
        cum = cum + jnp.where(lane % BLOCK >= shift, pltpu.roll(cum, shift, 1), 0.0)
        shift *= 2
    return cum, gain


def as_columns(rows, chunks):
    parts = [rows[:, c * BLOCK : (c + 1) * BLOCK] for c in range(chunks)]
    short = BLOCK - 8 * chunks
    if short:
        parts.append(jnp.zeros((short, BLOCK), F32))
    return jnp.concatenate(parts, axis=0).T


def prepare_kernel(
    first, count, head, group, chunks, key_heads,
    length_ref, qk_ref, v_ref, halo_ref, qk_taps_ref, v_taps_ref, log_ref, gain_ref, after_ref,
    kn_ref, wu_ref, start_ref, state_ref, trans_ref,
    qk_pad, v_pad, halo_scr, m_scr, b_scr, fade_scr, st_scr, a_scr, x_scr,
):
    step = pl.program_id(0)
    used = length_ref[first + jnp.minimum(step, count - 1)] - lax.axis_index("seq") * (chunks * BLOCK)
    units = [(h, c) for c in range(chunks) for h in range(group)]
    slot = step % 2
    live = jnp.logical_and(step < count, used > 0)

    def begin():
        row = lax.broadcasted_iota(jnp.int32, (DK, DV + DK), 0)
        lane = lax.broadcasted_iota(jnp.int32, (DK, DV + DK), 1)
        for h in range(group):
            st_scr[h] = jnp.where(lane == row + DV, 1.0, 0.0).astype(F32)

    def advance(c):
        narrow, moved = [], []
        for h in range(group):
            narrow.append(st_scr[h].astype(BF16))
            start_ref[0, c, h] = narrow[h]
        for h in range(group):
            moved.append(dot(m_scr[1 - slot, c, h], narrow[h]))
        for h in range(group):
            fade = fade_scr[1 - slot, c, h : h + 1, :]
            state = st_scr[h, :, :DV] * fade + (moved[h][:, :DV] + b_scr[1 - slot, c, h])
            trans = st_scr[h, :, DV:] * fade + moved[h][:, DV:]
            if c < chunks - 1:
                st_scr[h, :, :DV] = state
                st_scr[h, :, DV:] = trans
            else:
                state_ref[h] = state.astype(BF16)
                trans_ref[h] = trans.astype(BF16)

    todo = [begin] + [functools.partial(advance, c) for c in range(chunks)]

    def run(n):
        for _ in range(min(n, len(todo))):
            todo.pop(0)()

    @pl.when(jnp.logical_not(live))
    def _():
        @pl.when(step > 0)
        def _():
            begin()
            for c in range(chunks):
                advance(c)

        @pl.when(step < count)
        def _():
            kn_ref[...] = jnp.zeros_like(kn_ref)
            wu_ref[...] = jnp.zeros_like(wu_ref)
            fade_scr[slot] = jnp.ones(fade_scr.shape[1:], F32)
            m_scr[slot] = jnp.zeros(m_scr.shape[1:], BF16)
            b_scr[slot] = jnp.zeros(b_scr.shape[1:], F32)

    @pl.when(live)
    def _():
        halo = halo_ref[0].astype(F32)
        halo_scr[...] = halo
        load_padded(qk_pad, halo[: 2 * EDGE], qk_ref)
        v_pad[EDGE:, :] = v_ref[0].astype(F32)
        for i in range(CONV - 1):
            for h in range(group):
                source = 2 * EDGE + (i * key_heads + head) * group + h
                v_pad[EDGE - CONV + 1 + i : EDGE - CONV + 2 + i, h * DV : (h + 1) * DV] = halo_scr[
                    source : source + 1, :
                ]
        all_taps = qk_taps_ref[...].astype(F32)
        k_taps = [all_taps[n : n + 1] for n in range(2 * head + 1, all_taps.shape[0], 2 * key_heads)]
        v_all_taps = v_taps_ref[...].astype(F32)
        v_taps = [v_all_taps[i : i + 1] for i in range(CONV)]
        run(1)

        cum, gain = gates_of_heads(log_ref, gain_ref, used, head, group)
        faded = jnp.exp(cum)
        columns = as_columns(jnp.concatenate([cum, gain, gain * faded, faded], axis=0), chunks)

        def column(which, h, c):
            n = c * 8 + which * group + h
            return columns[:, n : n + 1]

        row = lax.broadcasted_iota(jnp.int32, (BLOCK, BLOCK), 0)
        lane = lax.broadcasted_iota(jnp.int32, (BLOCK, BLOCK), 1)
        below = row > lane
        small_row = lax.broadcasted_iota(jnp.int32, (TINY, BLOCK), 0)
        small_lane = lax.broadcasted_iota(jnp.int32, (TINY, BLOCK), 1)
        part_of = small_lane // TINY
        tiny_eye = jnp.where(small_row == small_lane % TINY, 1.0, 0.0).astype(F32)

        keys = []
        for c in range(chunks):
            kc = mixed_rows(qk_pad, k_taps, 2 * EDGE, 2 * head + 1, 2 * key_heads, c)
            kc = unit_rows(kc).astype(BF16)
            kn_ref[0, c * BLOCK : (c + 1) * BLOCK, :] = kc
            keys.append(kc)
        turned = [kc.T for kc in keys]
        run(1)

        compact = {}
        for c in range(chunks):
            kk = dot(keys[c], turned[c])
            for h in range(group):
                r = h * chunks + c
                span = slice(c * BLOCK, (c + 1) * BLOCK)
                ratio = jnp.exp(column(0, h, c) - cum[h : h + 1, span])
                strict = jnp.where(below, column(1, h, c) * ratio * kk, 0.0)
                a_scr[r] = strict.astype(BF16)
                tiny = strict[0:TINY]
                for b in range(1, BLOCK // TINY):
                    tiny = jnp.where(part_of == b, strict[b * TINY : (b + 1) * TINY], tiny)
                compact[r] = tiny

        run(1)
        solved = {r: tiny_eye for r in compact}
        for j in range(TINY - 1):
            pick = part_of * TINY + j
            for r in solved:
                factor = jnp.take_along_axis(compact[r], pick, axis=1, mode="promise_in_bounds")
                solved[r] = solved[r] - factor * solved[r][j : j + 1, :]
        for r in solved:
            for b in range(BLOCK // TINY):
                x_scr[r, b * TINY : (b + 1) * TINY, :] = jnp.where(
                    part_of == b, solved[r], 0.0
                ).astype(BF16)

        run(1)
        size = TINY
        while size < BLOCK:
            odd = [s for s in range(size, BLOCK, 2 * size)]
            half_lane = lax.broadcasted_iota(jnp.int32, (BLOCK // 2, BLOCK), 1)
            half_row = lax.broadcasted_iota(jnp.int32, (BLOCK // 2, BLOCK), 0)
            left = half_lane // size == 2 * (half_row // size)
            moved = {}
            for h, c in units:
                r = h * chunks + c
                lower = jnp.concatenate([a_scr[r, s : s + size, :] for s in odd], axis=0)
                lower = jnp.where(left, lower, jnp.zeros_like(lower))
                moved[r] = dot(lower, x_scr[r]).astype(BF16)
            for h, c in units:
                r = h * chunks + c
                spread = []
                for n in range(len(odd)):
                    spread.append(jnp.zeros((size, BLOCK), BF16))
                    spread.append(moved[r][n * size : (n + 1) * size])
                own = jnp.concatenate([x_scr[r, s : s + size, :] for s in odd], axis=0)
                update = own.astype(F32) - dot(own, jnp.concatenate(spread, axis=0))
                update = update.astype(BF16)
                for n, s in enumerate(odd):
                    x_scr[r, s : s + size, :] = update[n * size : (n + 1) * size]
            run(1)
            size *= 2

        for c in range(chunks):
            vc = mixed_rows(v_pad, v_taps, EDGE, 0, 1, c).astype(BF16).astype(F32)
            kc = keys[c].astype(F32)
            for h in range(group):
                r = h * chunks + c
                right = jnp.concatenate(
                    [
                        (kc * column(2, h, c)).astype(BF16),
                        (vc[:, h * DV : (h + 1) * DV] * column(1, h, c)).astype(BF16),
                    ],
                    axis=1,
                )
                wu_ref[0, r] = dot(x_scr[r], right).astype(BF16)
            if c == chunks // 2:
                run(1)
        run(len(todo))
        for c in range(chunks):
            sums = cum[:, c * BLOCK : (c + 1) * BLOCK]
            last = sums[:, BLOCK - 1 : BLOCK]
            tail = jnp.exp(last - sums)
            fade = jnp.broadcast_to(jnp.exp(last), (group, BLOCK))
            for h in range(group):
                r = h * chunks + c
                fade_scr[slot, c, h : h + 1, :] = fade[h : h + 1]
                scaled = (turned[c].astype(F32) * tail[h : h + 1, :]).astype(BF16)
                both = dot(scaled, wu_ref[0, r])
                m_scr[slot, c, h] = (-both[:, :DK]).astype(BF16)
                b_scr[slot, c, h] = both[:, DK:]


def prepare(job, lengths, qk_rows, v_in, halo, qk_taps, v_taps, log_decay, write_gain, key_heads, after):
    head, first, count = job
    tok = v_in.shape[1]
    value_heads = v_in.shape[2] // DV
    group = value_heads // key_heads
    chunks = tok // BLOCK
    rows = group * chunks
    wide = group * DV

    def now(i):
        return jnp.minimum(i, count - 1)

    def before(i):
        return jnp.maximum(i - 1, 0)

    def whole_of(i, lengths):
        return (first + now(i), 0, 0)

    return pl.pallas_call(
        functools.partial(prepare_kernel, first, count, head, group, chunks, key_heads),
        grid_spec=pltpu.PrefetchScalarGridSpec(
            num_scalar_prefetch=1,
            grid=(count + 1,),
            in_specs=[
                pl.BlockSpec((1,) + qk_rows.shape[1:], whole_of),
                pl.BlockSpec((1, tok, wide), lambda i, lengths: (first + now(i), 0, head)),
                pl.BlockSpec((1,) + halo.shape[1:], whole_of),
                pl.BlockSpec(qk_taps.shape, lambda i, lengths: (0, 0)),
                pl.BlockSpec((CONV, wide), lambda i, lengths: (0, head)),
                pl.BlockSpec((1, value_heads, tok), whole_of),
                pl.BlockSpec((1, value_heads, tok), whole_of),
                pl.BlockSpec(memory_space=pl.ANY),
            ],
            out_specs=[
                pl.BlockSpec((1, tok, DK), lambda i, lengths: (now(i), 0, 0)),
                pl.BlockSpec((1, rows, BLOCK, DK + DV), lambda i, lengths: (now(i), 0, 0, 0)),
                pl.BlockSpec((1, chunks, group, DK, DV + DK), lambda i, lengths: (before(i), 0, 0, 0, 0)),
                pl.BlockSpec((group, DK, DV), lambda i, lengths: (before(i), 0, 0)),
                pl.BlockSpec((group, DK, DK), lambda i, lengths: (before(i), 0, 0)),
            ],
            scratch_shapes=[
                pltpu.VMEM((qk_rows.shape[1] + 2 * EDGE, DK), F32),
                pltpu.VMEM((tok + EDGE, wide), F32),
                pltpu.VMEM(halo.shape[1:], F32),
                pltpu.VMEM((2, chunks, group, DK, DK), BF16),
                pltpu.VMEM((2, chunks, group, DK, DV), F32),
                pltpu.VMEM((2, chunks, group, BLOCK), F32),
                pltpu.VMEM((group, DK, DV + DK), F32),
                pltpu.VMEM((rows, BLOCK, BLOCK), BF16),
                pltpu.VMEM((rows, BLOCK, BLOCK), BF16),
            ],
        ),
        out_shape=[
            jax.ShapeDtypeStruct((count, tok, DK), BF16),
            jax.ShapeDtypeStruct((count, rows, BLOCK, DK + DV), BF16),
            jax.ShapeDtypeStruct((count, chunks, group, DK, DV + DK), BF16),
            jax.ShapeDtypeStruct((count * group, DK, DV), BF16),
            jax.ShapeDtypeStruct((count * group, DK, DK), BF16),
        ],
        compiler_params=pltpu.CompilerParams(vmem_limit_bytes=VMEM_BYTES),
        cost_estimate=pl.CostEstimate(flops=5 * 10**9 * count, bytes_accessed=4 * 2**20 * count, transcendentals=10**6),
        name="prepare",
    )(lengths, qk_rows, v_in, halo, qk_taps, v_taps, log_decay, write_gain, after)


def outputs_kernel(
    first, head, group, chunks, key_heads,
    length_ref, qk_ref, halo_ref, qk_taps_ref, kn_ref, wu_ref, start_ref, log_ref, gain_ref,
    enter_ref, z_ref, norm_ref, held_ref, after_ref,
    out_ref,
    qk_pad,
):
    used = length_ref[first + pl.program_id(0)] - lax.axis_index("seq") * (chunks * BLOCK)

    @pl.when(used <= 0)
    def _():
        out_ref[...] = jnp.zeros_like(out_ref)

    @pl.when(used > 0)
    def _():
        load_padded(qk_pad, halo_ref[0].astype(F32)[: 2 * EDGE], qk_ref)
        all_taps = qk_taps_ref[...].astype(F32)
        q_taps = [all_taps[n : n + 1] for n in range(2 * head, all_taps.shape[0], 2 * key_heads)]
        cum, gain = gates_of_heads(log_ref, gain_ref, used, head, group)
        faded = jnp.exp(cum)
        columns = as_columns(jnp.concatenate([cum, faded, gain, gain], axis=0), chunks)

        def column(which, h, c):
            n = c * 8 + which * group + h
            return columns[:, n : n + 1]

        row = lax.broadcasted_iota(jnp.int32, (BLOCK, BLOCK), 0)
        lane = lax.broadcasted_iota(jnp.int32, (BLOCK, BLOCK), 1)
        upto = row >= lane
        norm_gain = norm_ref[...]
        for c in range(chunks):
            span = slice(c * BLOCK, (c + 1) * BLOCK)
            qc = mixed_rows(qk_pad, q_taps, 2 * EDGE, 2 * head, 2 * key_heads, c)
            qc = unit_rows(qc).astype(BF16)
            qk = dot(qc, kn_ref[0, span, :].T)
            q_wide = qc.astype(F32)
            valid = row + c * BLOCK < used
            for h in range(group):
                r = h * chunks + c
                cols = slice(h * DV, (h + 1) * DV)
                first_state = dot(start_ref[0, c, h, :, DV:], enter_ref[h])
                first_state = (first_state + start_ref[0, c, h, :, :DV].astype(F32)).astype(BF16)
                ratio = jnp.exp(column(0, h, c) - cum[h : h + 1, span])
                scores = jnp.where(upto, ratio * qk, 0.0).astype(BF16)
                both = dot(scores, wu_ref[0, r])
                seen = (q_wide * column(1, h, c) - both[:, :DK]).astype(BF16)
                raw = dot(seen, first_state) + both[:, DK:]
                mean = jnp.sum(raw * raw, axis=-1, keepdims=True) * (1.0 / DV)
                gated = raw * lax.rsqrt(mean + EPSILON) * norm_gain * silu(z_ref[0, span, cols].astype(F32))
                out_ref[0, span, cols] = jnp.where(valid, gated, 0.0).astype(BF16)


def outputs(
    job, piece, lengths, qk_rows, halo, qk_taps, kn, wu, starts, log_decay, write_gain, enter, gate_z, norm_gain,
    key_heads, held, after,
):
    head, first, _ = job
    begin, count = piece
    prompts, tok, width = gate_z.shape
    rows = wu.shape[1]
    chunks = tok // BLOCK
    group = rows // chunks
    wide = group * DV
    value_heads = key_heads * group
    shift = begin - first

    def whole_of(i, lengths):
        return (begin + i, 0, 0)

    def wide_of(i, lengths):
        return (begin + i, 0, head)

    empty = held is None
    return pl.pallas_call(
        functools.partial(outputs_kernel, begin, head, group, chunks, key_heads),
        grid_spec=pltpu.PrefetchScalarGridSpec(
            num_scalar_prefetch=1,
            grid=(count,),
            in_specs=[
                pl.BlockSpec((1,) + qk_rows.shape[1:], whole_of),
                pl.BlockSpec((1,) + halo.shape[1:], whole_of),
                pl.BlockSpec(qk_taps.shape, lambda i, lengths: (0, 0)),
                pl.BlockSpec((1, tok, DK), lambda i, lengths: (shift + i, 0, 0)),
                pl.BlockSpec((1, rows, BLOCK, DK + DV), lambda i, lengths: (shift + i, 0, 0, 0)),
                pl.BlockSpec((1, chunks, group, DK, DV + DK), lambda i, lengths: (shift + i, 0, 0, 0, 0)),
                pl.BlockSpec((1, value_heads, tok), whole_of),
                pl.BlockSpec((1, value_heads, tok), whole_of),
                pl.BlockSpec((group, DK, DV), lambda i, lengths: (shift + i, 0, 0)),
                pl.BlockSpec((1, tok, wide), wide_of),
                pl.BlockSpec((1, DV), lambda i, lengths: (0, 0)),
                pl.BlockSpec(memory_space=pl.ANY),
                pl.BlockSpec(memory_space=pl.ANY),
            ],
            out_specs=pl.BlockSpec((1, tok, wide), wide_of),
            scratch_shapes=[pltpu.VMEM((qk_rows.shape[1] + 2 * EDGE, DK), F32)],
        ),
        out_shape=jax.ShapeDtypeStruct((prompts, tok, width), BF16),
        input_output_aliases={} if empty else {12: 0},
        compiler_params=pltpu.CompilerParams(vmem_limit_bytes=VMEM_BYTES),
        cost_estimate=pl.CostEstimate(flops=3 * 10**9 * count, bytes_accessed=4 * 2**20 * count, transcendentals=10**6),
        name="outputs",
    )(
        lengths, qk_rows, halo, qk_taps, kn, wu, starts, log_decay, write_gain, enter, gate_z,
        norm_gain.reshape(1, DV), after if empty else held, lengths if after is held else after,
    )


def own_chip():
    seq = lax.axis_index("seq")
    return seq // 2, seq % 2 == 1


def early_late(own, other, odd):
    return jnp.where(odd, other, own), jnp.where(odd, own, other)


def compose_maps(ins, outs):
    state_ref, trans_ref, state_other_ref, trans_other_ref = ins
    _, odd = own_chip()
    for n in range(state_ref.shape[0]):
        state_early, state_late = early_late(state_ref[n], state_other_ref[n], odd)
        trans_early, trans_late = early_late(trans_ref[n], trans_other_ref[n], odd)
        both = dot(trans_late, jnp.concatenate([state_early, trans_early], axis=1))
        outs[0][n] = (both[:, :DV] + state_late.astype(F32)).astype(BF16)
        outs[1][n] = both[:, DV:].astype(BF16)


def close_maps(chips, ins, outs):
    state_ref, trans_ref, state_other_ref, trans_other_ref = ins[:4]
    states, transes = ins[4 : 4 + chips], ins[4 + chips :]
    chip, odd = own_chip()

    def of_chip(refs, j, n):
        value = refs[0][n]
        for k in range(1, chips):
            value = jnp.where((chip + chips - k) % chips == j, refs[k][n], value)
        return value

    for n in range(state_ref.shape[0]):
        running = of_chip(states, 0, n)
        entering = jnp.zeros_like(running)
        for j in range(1, chips):
            entering = jnp.where(chip == j, running, entering)
            running = dot(of_chip(transes, j, n), running) + of_chip(states, j, n).astype(F32)
            running = running.astype(BF16)
        state_early, _ = early_late(state_ref[n], state_other_ref[n], odd)
        trans_early, _ = early_late(trans_ref[n], trans_other_ref[n], odd)
        second = (dot(trans_early, entering) + state_early.astype(F32)).astype(BF16)
        outs[0][n] = jnp.where(odd, second, entering)
        outs[1][n] = running


def choose_finals(group, placement_ref, finals, outs):
    refs = [(ref, n) for ref in finals for n in range(ref.shape[0] // group)]
    for r in range(placement_ref.shape[1]):
        prompt = placement_ref[0, r]
        for p, (ref, n) in enumerate(refs):
            @pl.when(prompt == p)
            def _(ref=ref, n=n):
                outs[0][r] = ref[n * group : (n + 1) * group]


def state_step(placement, group, compose, close, earlier, after):
    operands, shapes = [placement], []
    steps = []
    if compose is not None:
        steps.append(("compose", len(operands), len(compose), len(shapes)))
        operands += compose
        shapes += [compose[0], compose[1]]
    if close is not None:
        steps.append(("close", len(operands), len(close), len(shapes)))
        operands += close
        shapes += [close[0], close[0]]
        if earlier is not None:
            steps.append(("choose", len(operands), len(earlier), len(shapes)))
            operands += earlier
            shapes.append(jax.ShapeDtypeStruct((placement.shape[1], group, DK, DV), BF16))
    out_shape = [jax.ShapeDtypeStruct(x.shape, x.dtype) for x in shapes]

    def kernel(*refs):
        ins, outs = refs[: len(operands)], refs[len(operands) + 1 :]
        closed = None
        for kind, at, size, to in steps:
            part = ins[at : at + size]
            if kind == "compose":
                compose_maps(part, outs[to : to + 2])
            elif kind == "close":
                close_maps((size - 4) // 2, part, outs[to : to + 2])
                closed = outs[to + 1]
            else:
                choose_finals(group, ins[0], list(part) + [closed], outs[to:])

    vmem = pl.BlockSpec(memory_space=pltpu.VMEM)
    return pl.pallas_call(
        kernel,
        in_specs=[pl.BlockSpec(memory_space=pltpu.SMEM)]
        + [vmem] * (len(operands) - 1)
        + [pl.BlockSpec(memory_space=pl.ANY)],
        out_specs=[vmem] * len(out_shape),
        out_shape=out_shape,
        compiler_params=pltpu.CompilerParams(vmem_limit_bytes=VMEM_BYTES),
        cost_estimate=pl.CostEstimate(flops=10**9, bytes_accessed=2**20, transcendentals=0),
        name="state_step",
    )(*operands, after)


def deliver(parts):
    count, group = parts[0].shape[:2]

    def kernel(*refs):
        for n, ref in enumerate(refs[:-1]):
            refs[-1][0, n * group : (n + 1) * group] = ref[0].astype(F32)

    return pl.pallas_call(
        kernel,
        grid=(count,),
        in_specs=[pl.BlockSpec((1, group, DK, DV), lambda i: (i, 0, 0, 0))] * len(parts),
        out_specs=pl.BlockSpec((1, group * len(parts), DK, DV), lambda i: (i, 0, 0, 0)),
        out_shape=jax.ShapeDtypeStruct((count, group * len(parts), DK, DV), F32),
        compiler_params=pltpu.CompilerParams(vmem_limit_bytes=VMEM_BYTES),
        name="deliver",
    )(*parts)


def pair_swap(block):
    count = lax.axis_size("seq")
    return lax.ppermute(block, "seq", [(i, i ^ 1) for i in range(count)])


def from_chip_behind(block, distance, skip_first):
    count = lax.axis_size("seq")
    chips = count // 2
    route = [
        (i, ((i // 2 + distance) % chips) * 2 + i % 2)
        for i in range(count)
        if not (skip_first and i < 2)
    ]
    return lax.ppermute(block, "seq", route)


def shards(
    qk_in, v_in, gate_z, conv_qk, conv_v, log_decay, write_gain, norm_gain, prompt_lengths, placement,
):
    prompts, tok = qk_in.shape[:2]
    key_heads = qk_in.shape[3] // DK
    value_heads = v_in.shape[2] // DV
    rim = CONV - 1
    seq_count = lax.axis_size("seq")
    head_count = lax.axis_size("head")

    def by_head(x):
        x = x.reshape(x.shape[0], x.shape[1], 2, key_heads, DK)
        return jnp.transpose(x, (0, 1, 3, 2, 4)).reshape(x.shape[0], -1, DK)

    qk_rows = by_head(qk_in)
    qk_taps = by_head(conv_qk[None])[0]
    qk_tail = qk_rows[:, (tok - rim) * 2 * key_heads :]
    v_tail = v_in[:, tok - rim :].reshape(prompts, rim * value_heads, DV)
    front = 2 * EDGE - qk_tail.shape[1]
    back = 2 * EDGE - v_tail.shape[1]
    tails = jnp.concatenate(
        [
            jnp.zeros((prompts, front, DK), BF16),
            qk_tail,
            v_tail,
            jnp.zeros((prompts, back, DK), BF16),
        ],
        axis=1,
    )
    halo = lax.ppermute(tails, "seq", [(i, i + 1) for i in range(seq_count - 1)])
    group = value_heads // key_heads
    chips = seq_count // 2
    half = prompts // 2
    jobs = [(head, 0, prompts) for head in range(key_heads - 1)]
    jobs += [(key_heads - 1, 0, half), (key_heads - 1, half, prompts - half)]
    total = len(jobs)

    made, maps, chip_maps, entered, finals, sent = {}, {}, {}, {}, {}, {}
    waiting = []
    attended = None
    last = v_in

    def emit(attended, last):
        job, piece = waiting.pop(0)
        kn, wu, starts = made[job]
        attended = outputs(
            jobs[job], piece, prompt_lengths, qk_rows, halo, qk_taps, kn, wu, starts, log_decay, write_gain,
            entered[job], gate_z, norm_gain, key_heads, attended, last,
        )
        return attended, attended

    for t in range(total + 2):
        if t < total:
            kn, wu, starts, state, trans = prepare(
                jobs[t], prompt_lengths, qk_rows, v_in, halo, qk_taps, conv_v, log_decay, write_gain, key_heads, last
            )
            made[t] = kn, wu, starts
            maps[t] = [state, trans, pair_swap(state), pair_swap(trans)]
            last = state
        elif waiting:
            attended, last = emit(attended, last)
        compose = maps[t - 1] if 0 <= t - 1 < total else None
        close, earlier = None, None
        if 0 <= t - 2 < total:
            close = maps[t - 2] + chip_maps[t - 2]
            head = jobs[t - 2][0]
            if t - 2 == max(n for n in range(total) if jobs[n][0] == head):
                earlier = [finals[n] for n in range(t - 2) if jobs[n][0] == head]
        if compose is None and close is None:
            continue
        results = state_step(placement, group, compose, close, earlier, last)
        last = results[0]
        if compose is not None:
            state, trans = results[:2]
            results = results[2:]
            states, transes = [state], [trans]
            for k in range(1, chips):
                states.append(from_chip_behind(state, k, False))
                transes.append(from_chip_behind(trans, k, True))
            chip_maps[t - 1] = states + transes
        if close is not None:
            entered[t - 2], finals[t - 2] = results[:2]
            if earlier is not None:
                sent[jobs[t - 2][0]] = lax.all_to_all(results[2], "head", 0, 0)
            _, begin, count = jobs[t - 2]
            while count > 0:
                waiting.append((t - 2, (begin, min(half, count))))
                begin, count = begin + half, count - half
    while waiting:
        attended, last = emit(attended, last)
    rollout = deliver([sent[head] for head in range(key_heads)])
    return attended, rollout.reshape(1, 1, head_count * value_heads, DK, DV)


def solution(mesh):
    return jax.shard_map(
        shards,
        mesh=mesh,
        in_specs=(
            P(None, "seq", None, "head"),
            P(None, "seq", "head"),
            P(None, "seq", "head"),
            P(None, None, "head"),
            P(None, "head"),
            P(None, "head", "seq"),
            P(None, "head", "seq"),
            P(),
            P(),
            P("seq", None),
        ),
        out_specs=(P(None, "seq", "head"), P("seq", "head", None, None, None)),
        check_vma=False,
    )
```

time: 128 us -> 160 us (1.25)
  local copies, waits for them, and re-layouts: 2.9 us -> 37.9 us
  waiting for transfers between devices: 16.4 us -> 0.88 us
  starting transfers between devices: 15.2 us -> 30.5 us
  other arithmetic: 5.14 us -> 0.02 us
  Pallas kernels: 83.6 us -> 88.3 us
  matrix products: 3.81 us -> 0 us
    unnamed x10 -> x78, local copies, waits for them, and re-layouts: 0.62 us -> 36.4 us
    all_to_all x1 -> x2, waiting for transfers between devices: 12 us -> 0.01 us  [shards(): sent[jobs[t - 2][0]] = lax.all_to_all(results[2], 'head', 0, 0)]
    ppermute x2 -> x6, starting transfers between devices: 4.01 us -> 12.4 us  [from_chip_behind(): return lax.ppermute(block, 'seq', route)]
    all_to_all x1 -> x2, starting transfers between devices: 5.84 us -> 11.8 us  [shards(): sent[jobs[t - 2][0]] = lax.all_to_all(results[2], 'head', 0, 0)]
    pallas_call x3 -> x12, Pallas kernels: 83.6 us -> 88.3 us  [the longest x3 45.5 us: prepare(): pl.pallas_call(functools.partial(prepare_kernel, first, count, head, grou...]
    dot_general x4 -> x0, matrix products: 3.81 us -> none  [apply_map(): return jnp.einsum('nij,njv->niv', trans, state, preferred_element_type=F32)]
    ppermute x3 -> x6, waiting for transfers between devices: 3.52 us -> 0.02 us  [pair_swap(): return lax.ppermute(block, 'seq', [(i, i ^ 1) for i in range(count)])]
    select_n x5 -> x0, other arithmetic: 3.42 us -> none  [the longest x2 1.14 us: shards(): outgoing = jnp.take(final, placement[0], axis=0)]
  transfers between devices with their start and end apart: 7 -> 15, of which waited for: 4 -> 1; matrix products, arithmetic and copies ran while one was open for 5% -> 0% of each run, Pallas kernels for 28% -> 40%
where the time goes in v1:
time: 160 us; the launch traced here: 159 us
  Pallas kernels  88.3 us (55%)
  local copies, waits for them, and re-layouts  37.9 us (24%)
  starting transfers between devices  30.5 us (19%)
    pallas_call x3, Pallas kernels, prepare(): pl.pallas_call(functools.partial(prepare_kernel, first, count, head, grou...  45.5 us
    unnamed x78, local copies, waits for them, and re-layouts  36.4 us
    pallas_call x4, Pallas kernels, outputs(): pl.pallas_call(functools.partial(outputs_kernel, begin, head, group, chun...  34 us
    ppermute x6, starting transfers between devices, from_chip_behind(): return lax.ppermute(block, 'seq', route)  12.4 us
    all_to_all x2, starting transfers between devices, shards(): sent[jobs[t - 2][0]] = lax.all_to_all(results[2], 'head', 0, 0)  11.8 us
    pallas_call x4, Pallas kernels, state_step(): pl.pallas_call(kernel, in_specs=[pl.BlockSpec(memory_space=pltpu.SMEM)] +...  5.8 us
    ppermute x6, starting transfers between devices, pair_swap(): return lax.ppermute(block, 'seq', [(i, i ^ 1) for i in range(count)])  3.91 us
  transfers between devices with their start and end apart: 15, of which 1 were waited for; matrix products, arithmetic and copies ran while one was open for 0% of the time, Pallas kernels for 40%

profile of v1, /device:TPU:0, one launch (start us, length us, event | category | flops | bytes accessed | tf_op | source)
XLA Modules:
  0.0 158.5 jit_solution(364057136908977090)
XLA Ops:
  0.6 0.7 slice.8
  1.4 0.8 slice.7
  2.2 2.4 %collective-permute-start = (bf16[4,32,128]{2,1,0:T(8,128)(2,1)S(1)}, bf16[4,32,128]{2,1,0:T(8,128)(2,1)S(1)}, u32[]{:S(2)}, u32[]{:S(2)}) collective-permute-start(bf16[4,32,128]{2,1,0:T(8,128)(2,1)S(1)} %pad_maximum_fusion), channel_id=1, source_target_pairs={{0,8},{8,16},{16,24},{1,9},{9,17},{17,25},{2,10},{10,18},{18,26},{... | collective-permute-start | bytes 98312 | tf_op jit(solution)/shard_map/ppermute | solution.py:599
  4.6 0.8 collective-permute-done.halo_ref
  5.4 2.2 %copy-done.2 = bf16[4,1024,2,256]{3,2,1,0:T(2,128)(2,1)S(1)} copy-done((bf16[4,1024,2,256]{3,2,1,0:T(2,128)(2,1)S(1)}, bf16[4,1024,2,256]{3,2,1,0:T(2,128)(2,1)}, u32[]{:S(2)}) %copy-start.2) | copy-done | bytes 4194328
  7.6 0.8 copy-done.15
  8.4 0.8 copy-done.17
  9.3 0.7 copy-done.19
  10.0 0.7 copy-done.21
  10.6 2.2 %copy-done.25 = bf16[4,1024,512]{2,1,0:T(8,128)(2,1)S(1)} copy-done((bf16[4,1024,512]{2,1,0:T(8,128)(2,1)S(1)}, bf16[4,1024,512]{2,1,0:T(8,128)(2,1)}, u32[]{:S(2)}) %copy-start.25) | copy-done | bytes 4194328
  12.8 0.7 copy-done.26
  13.5 21.8 %prepare.3 = (bf16[4,1024,128]{2,1,0:T(8,128)(2,1)S(1)}, bf16[4,16,128,256]{3,2,1,0:T(8,128)(2,1)S(1)}, bf16[4,8,2,128,256]{4,3,2,1,0:T(8,128)(2,1)S(1)}, bf16[8...) custom-call(s32[4]{0:T(128)S(1)} %copy-done.21, bf16[4,4096,128]{2,1,0:T(8,128)(2,1)S(1)} %bitcast.13, ...), custom_call_target="tpu_custom_call" | custom-call | flops 20000000000 | bytes 16777216 | tf_op jit(solution)/shard_map/prepare/pallas_call | solution.py:283
  35.3 2.0 %copy-done.10 = bf16[4,16,128,256]{3,2,1,0:T(8,128)(2,1)} copy-done((bf16[4,16,128,256]{3,2,1,0:T(8,128)(2,1)}, bf16[4,16,128,256]{3,2,1,0:T(8,128)(2,1)S(1)}, u32[]{:S(2)}) %copy-start.10) | copy-done | bytes 4194328
  37.3 2.0 %copy-done.13 = bf16[4,8,2,128,256]{4,3,2,1,0:T(8,128)(2,1)} copy-done((bf16[4,8,2,128,256]{4,3,2,1,0:T(8,128)(2,1)}, bf16[4,8,2,128,256]{4,3,2,1,0:T(8,128)(2,1)S(1)}, u32[]{:S(2)}) %copy-start.13) | copy-done | bytes 4194328
  39.3 2.8 %collective-permute-start.2 = (bf16[8,128,128]{2,1,0:T(8,128)(2,1)S(1)}, bf16[8,128,128]{2,1,0:T(8,128)(2,1)S(1)}, u32[]{:S(2)}, u32[]{:S(2)}) collective-permute-start(bf16[8,128,128]{2,1,0:T(8,128)(2,1)S(1)} %get-tuple-element.30.refs_2_.refs_6_), channel_id=1, source_target_pairs={{0,8},{8,0},{16,24},{24,16},{1,9},{9,1},{17,25},{25,17},{2,10},{10... | collective-permute-start | bytes 786440 | tf_op jit(solution)/shard_map/ppermute | solution.py:556
  42.0 0.1 collective-permute-start.1
  42.1 11.9 %prepare.4 = (bf16[2,1024,128]{2,1,0:T(8,128)(2,1)S(1)}, bf16[2,16,128,256]{3,2,1,0:T(8,128)(2,1)S(1)}, bf16[2,8,2,128,256]{4,3,2,1,0:T(8,128)(2,1)S(1)}, bf16[4...) custom-call(s32[4]{0:T(128)S(1)} %copy-done.21, bf16[4,4096,128]{2,1,0:T(8,128)(2,1)S(1)} %bitcast.14, ...), custom_call_target="tpu_custom_call" | custom-call | flops 10000000000 | bytes 8388608 | tf_op jit(solution)/shard_map/prepare/pallas_call | solution.py:283
  54.0 1.4 copy-done.29
  55.4 0.8 copy-done.35
  56.2 0.4 collective-permute-start.6
  56.6 0.1 collective-permute-start.5
  56.7 0.9 state_step.4
  57.6 1.5 collective-permute-start.8
  59.1 2.7 %collective-permute-start.7 = (bf16[8,128,128]{2,1,0:T(8,128)(2,1)S(1)}, bf16[8,128,128]{2,1,0:T(8,128)(2,1)S(1)}, u32[]{:S(2)}, u32[]{:S(2)}) collective-permute-start(bf16[8,128,128]{2,1,0:T(8,128)(2,1)S(1)} %get-tuple-element.32.after_ref.refs_9_), channel_id=1, source_target_pairs={{0,16},{8,24},{16,0},{24,8},{1,17},{9,25},{17,1},{25,9},{2,18},{10... | collective-permute-start | bytes 786440 | tf_op jit(solution)/shard_map/ppermute | solution.py:567
  61.8 11.9 %prepare.5 = (bf16[2,1024,128]{2,1,0:T(8,128)(2,1)S(1)}, bf16[2,16,128,256]{3,2,1,0:T(8,128)(2,1)S(1)}, bf16[2,8,2,128,256]{4,3,2,1,0:T(8,128)(2,1)S(1)}, bf16[4...) custom-call(s32[4]{0:T(128)S(1)} %copy-done.22, bf16[4,4096,128]{2,1,0:T(8,128)(2,1)S(1)} %bitcast.15, ...), custom_call_target="tpu_custom_call" | custom-call | flops 10000000000 | bytes 8388608 | tf_op jit(solution)/shard_map/prepare/pallas_call | solution.py:283
  73.8 1.4 copy-done.33
  75.2 0.0 copy-start.20
  75.2 0.0 copy-start.23
  75.2 0.1 collective-permute-start.4
  75.3 0.5 collective-permute-start.3
  75.8 0.0 collective-permute-done.5.refs_3_.refs_7_
  75.8 0.0 collective-permute-done.8.refs_12_
  75.8 0.0 collective-permute-done.7.refs_10_
  75.8 2.2 %state_step.5 = (bf16[4,128,128]{2,1,0:T(8,128)(2,1)S(1)}, bf16[4,128,128]{2,1,0:T(8,128)(2,1)S(1)}, bf16[8,128,128]{2,1,0:T(8,128)(2,1)S(1)}, bf16[8,128,128]{2,1,0:T(8,128)(2,1)}, bf16[8,2,128,128]{3,2,1,0:T(8,128)(2,1)}) custom-call(s32[1,8]{1,0:T(1,128)S(1)} %copy-done.24, bf16[4,128,128]{2,1,0:T(8,128)(2,1)S(1)} %get-tuple-element.31.refs_5_.refs_1_, ...), custom_call_target="tpu_custom_call" | custom-call | flops 1000000000 | bytes 1048576 | tf_op jit(solution)/shard_map/state_step/pallas_call | solution.py:523
  78.0 5.8 %all-to-all-start = ((bf16[8,2,128,128]{3,2,1,0:T(8,128)(2,1)}), bf16[8,2,128,128]{3,2,1,0:T(8,128)(2,1)S(1)}, u32[]{:S(2)}, u32[]{:S(2)}) async-start(bf16[8,2,128,128]{3,2,1,0:T(8,128)(2,1)} %get-tuple-element.54), calls=%async_computation | async-start | bytes 1048576 | tf_op jit(solution)/shard_map/all_to_all | solution.py:653
  83.8 1.3 collective-permute-start.10
  85.1 2.7 %collective-permute-start.9 = (bf16[4,128,128]{2,1,0:T(8,128)(2,1)S(1)}, bf16[4,128,128]{2,1,0:T(8,128)(2,1)S(1)}, u32[]{:S(2)}, u32[]{:S(2)}) collective-permute-start(bf16[4,128,128]{2,1,0:T(8,128)(2,1)S(1)} %get-tuple-element.40.held_ref.after_ref.refs_9_), channel_id=1, source_target_pairs={{0,16},{8,24},{16,0},{24,8},{1,17},{9,25},{17,1},{25,9},{2,18},{10... | collective-permute-start | bytes 393224 | tf_op jit(solution)/shard_map/ppermute | solution.py:567
  87.8 0.0 copy-start.4
  87.8 2.2 %copy-done.4 = bf16[4,1024,2,256]{3,2,1,0:T(2,128)(2,1)S(1)} copy-done((bf16[4,1024,2,256]{3,2,1,0:T(2,128)(2,1)S(1)}, bf16[4,1024,2,256]{3,2,1,0:T(2,128)(2,1)}, u32[]{:S(2)}) %copy-start.4) | copy-done | bytes 4194328
  90.0 2.2 %copy-done.7 = bf16[4,1024,512]{2,1,0:T(8,128)(2,1)S(1)} copy-done((bf16[4,1024,512]{2,1,0:T(8,128)(2,1)S(1)}, bf16[4,1024,512]{2,1,0:T(8,128)(2,1)}, u32[]{:S(2)}) %copy-start.7) | copy-done | bytes 4194328
  92.2 2.2 %copy-done.11 = bf16[4,16,128,256]{3,2,1,0:T(8,128)(2,1)S(1)} copy-done((bf16[4,16,128,256]{3,2,1,0:T(8,128)(2,1)S(1)}, bf16[4,16,128,256]{3,2,1,0:T(8,128)(2,1)}, u32[]{:S(2)}) %copy-start.11) | copy-done | bytes 4194328
  94.4 2.2 %copy-done.14 = bf16[4,8,2,128,256]{4,3,2,1,0:T(8,128)(2,1)S(1)} copy-done((bf16[4,8,2,128,256]{4,3,2,1,0:T(8,128)(2,1)S(1)}, bf16[4,8,2,128,256]{4,3,2,1,0:T(8,128)(2,1)}, u32[]{:S(2)}) %copy-start.14) | copy-done | bytes 4194328
  96.6 8.5 %outputs.4.refs_13_.held_ref = bf16[4,1024,512]{2,1,0:T(8,128)(2,1)} custom-call(s32[4]{0:T(128)S(1)} %copy-done.22, bf16[4,4096,128]{2,1,0:T(8,128)(2,1)S(1)} %bitcast.16, bf16[4,32,128]{2,1,0:T(8,128)(2,1)S(1)} %collective-permute-done.halo_ref, bf16[16,128]{1,0:T(8,128)(2,1)S(1)} %bitcast.23, bf16[4,1024,128]{2,1,0:T(8,128)(2,1)S(1)} %get-tuple-element.42.kn_ref, ...), custom_call_target="tpu_custom_call" | custom-call | flops 6000000000 | bytes 8388608 | tf_op jit(solution)/shard_map/outputs/pallas_call | solution.py:403
  105.1 0.0 collective-permute-done.4.refs_4_
  105.1 0.0 collective-permute-done.3.refs_3_
  105.1 0.0 collective-permute-done.10.refs_12_
  105.1 0.0 collective-permute-done.9.refs_10_
  105.1 0.0 copy-start
  105.1 2.2 %copy-done = bf16[4,1024,512]{2,1,0:T(8,128)(2,1)S(1)} copy-done((bf16[4,1024,512]{2,1,0:T(8,128)(2,1)S(1)}, bf16[4,1024,512]{2,1,0:T(8,128)(2,1)}, u32[]{:S(2)}) %copy-start) | copy-done | bytes 4194328
  107.3 0.9 state_step.6
  108.2 1.5 collective-permute-start.12
  109.7 2.7 %collective-permute-start.11 = (bf16[4,128,128]{2,1,0:T(8,128)(2,1)S(1)}, bf16[4,128,128]{2,1,0:T(8,128)(2,1)S(1)}, u32[]{:S(2)}, u32[]{:S(2)}) collective-permute-start(bf16[4,128,128]{2,1,0:T(8,128)(2,1)S(1)} %get-tuple-element.46.after_ref.refs_5_), channel_id=1, source_target_pairs={{0,16},{8,24},{16,0},{24,8},{1,17},{9,25},{17,1},{25,9},{2,18},{10... | collective-permute-start | bytes 393224 | tf_op jit(solution)/shard_map/ppermute | solution.py:567
  112.5 8.5 %outputs.5.refs_10_.held_ref = bf16[4,1024,512]{2,1,0:T(8,128)(2,1)} custom-call(s32[4]{0:T(128)S(1)} %copy-done.22, bf16[4,4096,128]{2,1,0:T(8,128)(2,1)S(1)} %bitcast.17, bf16[4,32,128]{2,1,0:T(8,128)(2,1)S(1)} %collective-permute-done.halo_ref, bf16[16,128]{1,0:T(8,128)(2,1)S(1)} %bitcast.24, ...), custom_call_target="tpu_custom_call", output_to_operand_aliasing={{}: (12, {})} | custom-call | flops 6000000000 | bytes 8388608 | tf_op jit(solution)/shard_map/outputs/pallas_call | solution.py:403
  121.0 2.2 %copy-done.1 = bf16[4,1024,512]{2,1,0:T(8,128)(2,1)S(1)} copy-done((bf16[4,1024,512]{2,1,0:T(8,128)(2,1)S(1)}, bf16[4,1024,512]{2,1,0:T(8,128)(2,1)}, u32[]{:S(2)}) %copy-start.1) | copy-done | bytes 4194328
  123.2 1.8 %state_step.7 = (bf16[4,128,128]{2,1,0:T(8,128)(2,1)S(1)}, bf16[4,128,128]{2,1,0:T(8,128)(2,1)}, bf16[8,2,128,128]{3,2,1,0:T(8,128)(2,1)}) custom-call(s32[1,8]{1,0:T(1,128)S(1)} %copy-done.24, bf16[4,128,128]{2,1,0:T(8,128)(2,1)S(1)} %get-tuple-element.36.refs_13_.refs_1_, bf16[4,128,128]{2,1,0:T(8,128)(2,1)S(1)} %get-tuple-element.37.refs_2_, ...), custom_call_target="tpu_custom_call" | custom-call | flops 1000000000 | bytes 1048576 | tf_op jit(solution)/shard_map/state_step/pallas_call | solution.py:523
  125.0 6.0 %all-to-all-start.1 = ((bf16[8,2,128,128]{3,2,1,0:T(8,128)(2,1)}), bf16[8,2,128,128]{3,2,1,0:T(8,128)(2,1)S(1)}, u32[]{:S(2)}, u32[]{:S(2)}) async-start(bf16[8,2,128,128]{3,2,1,0:T(8,128)(2,1)} %get-tuple-element.55), calls=%async_computation.1 | async-start | bytes 1048576 | tf_op jit(solution)/shard_map/all_to_all | solution.py:653
  131.0 0.0 copy-start.6
  131.0 2.2 %copy-done.6 = bf16[4,1024,2,256]{3,2,1,0:T(2,128)(2,1)S(1)} copy-done((bf16[4,1024,2,256]{3,2,1,0:T(2,128)(2,1)S(1)}, bf16[4,1024,2,256]{3,2,1,0:T(2,128)(2,1)}, u32[]{:S(2)}) %copy-start.6) | copy-done | bytes 4194328
  133.2 2.2 %copy-done.9 = bf16[4,1024,512]{2,1,0:T(8,128)(2,1)S(1)} copy-done((bf16[4,1024,512]{2,1,0:T(8,128)(2,1)S(1)}, bf16[4,1024,512]{2,1,0:T(8,128)(2,1)}, u32[]{:S(2)}) %copy-start.9) | copy-done | bytes 4194328
  135.4 1.6 %copy-done.28 = bf16[2,16,128,256]{3,2,1,0:T(8,128)(2,1)S(1)} copy-done((bf16[2,16,128,256]{3,2,1,0:T(8,128)(2,1)S(1)}, bf16[2,16,128,256]{3,2,1,0:T(8,128)(2,1)}, u32[]{:S(2)}) %copy-start.28) | copy-done | bytes 2097176
  137.0 1.6 %copy-done.30 = bf16[2,8,2,128,256]{4,3,2,1,0:T(8,128)(2,1)S(1)} copy-done((bf16[2,8,2,128,256]{4,3,2,1,0:T(8,128)(2,1)S(1)}, bf16[2,8,2,128,256]{4,3,2,1,0:T(8,128)(2,1)}, u32[]{:S(2)}) %copy-start.30) | copy-done | bytes 2097176
  138.6 8.5 %outputs.6.held_ref = bf16[4,1024,512]{2,1,0:T(8,128)(2,1)} custom-call(s32[4]{0:T(128)S(1)} %copy-done.22, bf16[4,4096,128]{2,1,0:T(8,128)(2,1)S(1)} %bitcast.18, bf16[4,32,128]{2,1,0:T(8,128)(2,1)S(1)} %collective-permute-done.halo_ref, bf16[16,128]{1,0:T(8,128)(2,1)S(1)} %bitcast.25, ...), custom_call_target="tpu_custom_call", output_to_operand_aliasing={{}: (12, {})} | custom-call | flops 6000000000 | bytes 8388608 | tf_op jit(solution)/shard_map/outputs/pallas_call | solution.py:403
  147.1 8.5 %outputs.7 = bf16[4,1024,512]{2,1,0:T(8,128)(2,1)} custom-call(s32[4]{0:T(128)S(1)} %copy-done.22, bf16[4,4096,128]{2,1,0:T(8,128)(2,1)S(1)} %bitcast.19, bf16[4,32,128]{2,1,0:T(8,128)(2,1)S(1)} %collective-permute-done.halo_ref, bf16[16,128]{1,0:T(8,128)(2,1)S(1)} %bitcast.26, ...), custom_call_target="tpu_custom_call", output_to_operand_aliasing={{}: (12, {})} | custom-call | flops 6000000000 | bytes 8388608 | tf_op jit(solution)/shard_map/outputs/pallas_call | solution.py:403
  155.6 3.0 %deliver.1 = f32[8,4,128,128]{3,2,1,0:T(8,128)} custom-call(bf16[8,2,128,128]{3,2,1,0:T(8,128)(2,1)S(1)} %all-to-all-done.refs_0_, bf16[8,2,128,128]{3,2,1,0:T(8,128)(2,1)S(1)} %all-to-all-done.1.refs_1_), custom_call_target="tpu_custom_call" | custom-call | tf_op jit(solution)/shard_map/deliver/pallas_call | solution.py:543
  (61 shorter events, 0.2 us)
Async XLA Ops:
  2.2 3.2 %collective-permute-start = (bf16[4,32,128]{2,1,0:T(8,128)(2,1)S(1)}, bf16[4,32,128]{2,1,0:T(8,128)(2,1)S(1)}, u32[]{:S(2)}, u32[]{:S(2)}) collective-permute-start(bf16[4,32,128]{2,1,0:T(8,128)(2,1)S(1)} %pad_maximum_fusion), channel_id=1, source_target_pairs={{0,8},{8,16},{16,24},{1,9},{9,17},{17,25},{2,10},{10,18},{18,26},{... | collective-permute-start | bytes 98312 | tf_op jit(solution)/shard_map/ppermute | solution.py:599
  5.4 2.2 %copy-start.2 = (bf16[4,1024,2,256]{3,2,1,0:T(2,128)(2,1)S(1)}, bf16[4,1024,2,256]{3,2,1,0:T(2,128)(2,1)}, u32[]{:S(2)}) copy-start(bf16[4,1024,2,256]{3,2,1,0:T(2,128)(2,1)} %param.10) | copy-start | bytes 12582916
  7.6 0.8 copy-start.15
  8.4 0.8 copy-start.17
  9.3 0.7 copy-start.19
  10.0 0.7 copy-start.21
  10.6 2.2 %copy-start.25 = (bf16[4,1024,512]{2,1,0:T(8,128)(2,1)S(1)}, bf16[4,1024,512]{2,1,0:T(8,128)(2,1)}, u32[]{:S(2)}) copy-start(bf16[4,1024,512]{2,1,0:T(8,128)(2,1)} %v_ref.5) | copy-start | bytes 12582916
  12.8 0.7 copy-start.26
  35.3 2.0 %copy-start.10 = (bf16[4,16,128,256]{3,2,1,0:T(8,128)(2,1)}, bf16[4,16,128,256]{3,2,1,0:T(8,128)(2,1)S(1)}, u32[]{:S(2)}) copy-start(bf16[4,16,128,256]{3,2,1,0:T(8,128)(2,1)S(1)} %get-tuple-element.43.wu_ref) | copy-start | bytes 12582916
  37.3 2.0 %copy-start.13 = (bf16[4,8,2,128,256]{4,3,2,1,0:T(8,128)(2,1)}, bf16[4,8,2,128,256]{4,3,2,1,0:T(8,128)(2,1)S(1)}, u32[]{:S(2)}) copy-start(bf16[4,8,2,128,256]{4,3,2,1,0:T(8,128)(2,1)S(1)} %get-tuple-element.44.start_ref) | copy-start | bytes 12582916
  39.3 17.4 %collective-permute-start.2 = (bf16[8,128,128]{2,1,0:T(8,128)(2,1)S(1)}, bf16[8,128,128]{2,1,0:T(8,128)(2,1)S(1)}, u32[]{:S(2)}, u32[]{:S(2)}) collective-permute-start(bf16[8,128,128]{2,1,0:T(8,128)(2,1)S(1)} %get-tuple-element.30.refs_2_.refs_6_), channel_id=1, source_target_pairs={{0,8},{8,0},{16,24},{24,16},{1,9},{9,1},{17,25},{25,17},{2,10},{10... | collective-permute-start | bytes 786440 | tf_op jit(solution)/shard_map/ppermute | solution.py:556
  42.0 14.7 %copy-start.24 = (s32[1,8]{1,0:T(1,128)S(1)}, s32[1,8]{1,0:T(1,128)}, u32[]{:S(2)}) copy-start(s32[1,8]{1,0:T(1,128)} %refs_0_.7) | copy-start | bytes 100
  42.0 19.8 %copy-start.3 = (bf16[4,1024,2,256]{3,2,1,0:T(2,128)(2,1)S(1)}, bf16[4,1024,2,256]{3,2,1,0:T(2,128)(2,1)}, u32[]{:S(2)}) copy-start(bf16[4,1024,2,256]{3,2,1,0:T(2,128)(2,1)} %param.10) | copy-start | bytes 12582916
  42.0 19.8 %copy-start.22 = (s32[4]{0:T(128)S(1)}, s32[4]{0:T(128)}, u32[]{:S(2)}) copy-start(s32[4]{0:T(128)} %after_ref.3) | copy-start | bytes 52
  42.0 14.7 %collective-permute-start.1 = (bf16[8,128,128]{2,1,0:T(8,128)(2,1)S(1)}, bf16[8,128,128]{2,1,0:T(8,128)(2,1)S(1)}, u32[]{:S(2)}, u32[]{:S(2)}) collective-permute-start(bf16[8,128,128]{2,1,0:T(8,128)(2,1)S(1)} %get-tuple-element.29.after_ref.refs_1_.refs_5_), channel_id=1, source_target_pairs={{0,8},{8,0},{16,24},{24,16},{1,9},{9,1},{17,25},{25,17},{2,10},{10... | collective-permute-start | bytes 786440 | tf_op jit(solution)/shard_map/ppermute | solution.py:556
  54.0 1.4 copy-start.29
  55.4 0.8 copy-start.35
  56.2 2.9 %copy-start.27 = (bf16[2,16,128,256]{3,2,1,0:T(8,128)(2,1)}, bf16[2,16,128,256]{3,2,1,0:T(8,128)(2,1)S(1)}, u32[]{:S(2)}) copy-start(bf16[2,16,128,256]{3,2,1,0:T(8,128)(2,1)S(1)} %get-tuple-element.51.wu_ref) | copy-start | bytes 6291460
  56.2 19.1 %collective-permute-start.6 = (bf16[4,128,128]{2,1,0:T(8,128)(2,1)S(1)}, bf16[4,128,128]{2,1,0:T(8,128)(2,1)S(1)}, u32[]{:S(2)}, u32[]{:S(2)}) collective-permute-start(bf16[4,128,128]{2,1,0:T(8,128)(2,1)S(1)} %get-tuple-element.38.refs_2_.refs_6_), channel_id=1, source_target_pairs={{0,8},{8,0},{16,24},{24,16},{1,9},{9,1},{17,25},{25,17},{2,10},{10... | collective-permute-start | bytes 393224 | tf_op jit(solution)/shard_map/ppermute | solution.py:556
  56.6 19.1 %collective-permute-start.5 = (bf16[4,128,128]{2,1,0:T(8,128)(2,1)S(1)}, bf16[4,128,128]{2,1,0:T(8,128)(2,1)S(1)}, u32[]{:S(2)}, u32[]{:S(2)}) collective-permute-start(bf16[4,128,128]{2,1,0:T(8,128)(2,1)S(1)} %get-tuple-element.31.refs_5_.refs_1_), channel_id=1, source_target_pairs={{0,8},{8,0},{16,24},{24,16},{1,9},{9,1},{17,25},{25,17},{2,10},{10... | collective-permute-start | bytes 393224 | tf_op jit(solution)/shard_map/ppermute | solution.py:556
  57.6 18.1 %collective-permute-start.8 = (bf16[8,128,128]{2,1,0:T(8,128)(2,1)S(1)}, bf16[8,128,128]{2,1,0:T(8,128)(2,1)S(1)}, u32[]{:S(2)}, u32[]{:S(2)}) collective-permute-start(bf16[8,128,128]{2,1,0:T(8,128)(2,1)S(1)} %get-tuple-element.39.refs_11_), channel_id=1, source_target_pairs={{16,0},{24,8},{17,1},{25,9},{18,2},{26,10},{19,3},{27,11},{20,4},{... | collective-permute-start | bytes 786440 | tf_op jit(solution)/shard_map/ppermute | solution.py:567
  59.1 16.7 %collective-permute-start.7 = (bf16[8,128,128]{2,1,0:T(8,128)(2,1)S(1)}, bf16[8,128,128]{2,1,0:T(8,128)(2,1)S(1)}, u32[]{:S(2)}, u32[]{:S(2)}) collective-permute-start(bf16[8,128,128]{2,1,0:T(8,128)(2,1)S(1)} %get-tuple-element.32.after_ref.refs_9_), channel_id=1, source_target_pairs={{0,16},{8,24},{16,0},{24,8},{1,17},{9,25},{17,1},{25,9},{2,18},{10... | collective-permute-start | bytes 786440 | tf_op jit(solution)/shard_map/ppermute | solution.py:567
  73.7 1.4 copy-start.33
  75.1 2.8 %copy-start.31 = (bf16[2,16,128,256]{3,2,1,0:T(8,128)(2,1)}, bf16[2,16,128,256]{3,2,1,0:T(8,128)(2,1)S(1)}, u32[]{:S(2)}) copy-start(bf16[2,16,128,256]{3,2,1,0:T(8,128)(2,1)S(1)} %get-tuple-element.34.wu_ref) | copy-start | bytes 6291460
  75.1 2.8 %copy-start.37 = (bf16[2,1024,128]{2,1,0:T(8,128)(2,1)}, bf16[2,1024,128]{2,1,0:T(8,128)(2,1)S(1)}, u32[]{:S(2)}) copy-start(bf16[2,1024,128]{2,1,0:T(8,128)(2,1)S(1)} %get-tuple-element.33.kn_ref) | copy-start | bytes 1572868
  75.1 12.7 %copy-start.16 = (f32[4,4,1024]{2,1,0:T(4,128)S(1)}, f32[4,4,1024]{2,1,0:T(4,128)}, u32[]{:S(2)}) copy-start(f32[4,4,1024]{2,1,0:T(4,128)} %log_ref.13) | copy-start | bytes 196612
  75.1 12.7 %copy-start.18 = (f32[4,4,1024]{2,1,0:T(4,128)S(1)}, f32[4,4,1024]{2,1,0:T(4,128)}, u32[]{:S(2)}) copy-start(f32[4,4,1024]{2,1,0:T(4,128)} %gain_ref.13) | copy-start | bytes 196612
  75.2 12.7 %copy-start.20 = (bf16[4,2,256]{2,1,0:T(2,128)(2,1)S(1)}, bf16[4,2,256]{2,1,0:T(2,128)(2,1)}, u32[]{:S(2)}) copy-start(bf16[4,2,256]{2,1,0:T(2,128)(2,1)} %param.13) | copy-start | bytes 12292
  75.2 12.7 %copy-start.23 = (f32[128]{0:T(128)S(1)}, f32[128]{0:T(128)}, u32[]{:S(2)}) copy-start(f32[128]{0:T(128)} %param.17) | copy-start | bytes 1540
  75.2 29.9 %collective-permute-start.4 = (bf16[4,128,128]{2,1,0:T(8,128)(2,1)S(1)}, bf16[4,128,128]{2,1,0:T(8,128)(2,1)S(1)}, u32[]{:S(2)}, u32[]{:S(2)}) collective-permute-start(bf16[4,128,128]{2,1,0:T(8,128)(2,1)S(1)} %get-tuple-element.37.refs_2_), channel_id=1, source_target_pairs={{0,8},{8,0},{16,24},{24,16},{1,9},{9,1},{17,25},{25,17},{2,10},{10... | collective-permute-start | bytes 393224 | tf_op jit(solution)/shard_map/ppermute | solution.py:556
  75.3 29.8 %collective-permute-start.3 = (bf16[4,128,128]{2,1,0:T(8,128)(2,1)S(1)}, bf16[4,128,128]{2,1,0:T(8,128)(2,1)S(1)}, u32[]{:S(2)}, u32[]{:S(2)}) collective-permute-start(bf16[4,128,128]{2,1,0:T(8,128)(2,1)S(1)} %get-tuple-element.36.refs_13_.refs_1_), channel_id=1, source_target_pairs={{0,8},{8,0},{16,24},{24,16},{1,9},{9,1},{17,25},{25,17},{2,10},{10... | collective-permute-start | bytes 393224 | tf_op jit(solution)/shard_map/ppermute | solution.py:556
  78.0 47.0 %all-to-all-start = ((bf16[8,2,128,128]{3,2,1,0:T(8,128)(2,1)}), bf16[8,2,128,128]{3,2,1,0:T(8,128)(2,1)S(1)}, u32[]{:S(2)}, u32[]{:S(2)}) async-start(bf16[8,2,128,128]{3,2,1,0:T(8,128)(2,1)} %get-tuple-element.54), calls=%async_computation | async-start | bytes 1048576 | tf_op jit(solution)/shard_map/all_to_all | solution.py:653
  83.8 21.3 %collective-permute-start.10 = (bf16[4,128,128]{2,1,0:T(8,128)(2,1)S(1)}, bf16[4,128,128]{2,1,0:T(8,128)(2,1)S(1)}, u32[]{:S(2)}, u32[]{:S(2)}) collective-permute-start(bf16[4,128,128]{2,1,0:T(8,128)(2,1)S(1)} %get-tuple-element.41.refs_11_), channel_id=1, source_target_pairs={{16,0},{24,8},{17,1},{25,9},{18,2},{26,10},{19,3},{27,11},{20,4},{... | collective-permute-start | bytes 393224 | tf_op jit(solution)/shard_map/ppermute | solution.py:567
  85.1 20.0 %collective-permute-start.9 = (bf16[4,128,128]{2,1,0:T(8,128)(2,1)S(1)}, bf16[4,128,128]{2,1,0:T(8,128)(2,1)S(1)}, u32[]{:S(2)}, u32[]{:S(2)}) collective-permute-start(bf16[4,128,128]{2,1,0:T(8,128)(2,1)S(1)} %get-tuple-element.40.held_ref.after_ref.refs_9_), channel_id=1, source_target_pairs={{0,16},{8,24},{16,0},{24,8},{1,17},{9,25},{17,1},{25,9},{2,18},{10... | collective-permute-start | bytes 393224 | tf_op jit(solution)/shard_map/ppermute | solution.py:567
  87.8 2.2 %copy-start.4 = (bf16[4,1024,2,256]{3,2,1,0:T(2,128)(2,1)S(1)}, bf16[4,1024,2,256]{3,2,1,0:T(2,128)(2,1)}, u32[]{:S(2)}) copy-start(bf16[4,1024,2,256]{3,2,1,0:T(2,128)(2,1)} %param.10) | copy-start | bytes 12582916
  90.0 2.2 %copy-start.7 = (bf16[4,1024,512]{2,1,0:T(8,128)(2,1)S(1)}, bf16[4,1024,512]{2,1,0:T(8,128)(2,1)}, u32[]{:S(2)}) copy-start(bf16[4,1024,512]{2,1,0:T(8,128)(2,1)} %z_ref.7) | copy-start | bytes 12582916
  92.2 2.2 %copy-start.11 = (bf16[4,16,128,256]{3,2,1,0:T(8,128)(2,1)S(1)}, bf16[4,16,128,256]{3,2,1,0:T(8,128)(2,1)}, u32[]{:S(2)}) copy-start(bf16[4,16,128,256]{3,2,1,0:T(8,128)(2,1)} %copy-done.10) | copy-start | bytes 12582916
  94.4 2.2 %copy-start.14 = (bf16[4,8,2,128,256]{4,3,2,1,0:T(8,128)(2,1)S(1)}, bf16[4,8,2,128,256]{4,3,2,1,0:T(8,128)(2,1)}, u32[]{:S(2)}) copy-start(bf16[4,8,2,128,256]{4,3,2,1,0:T(8,128)(2,1)} %copy-done.13) | copy-start | bytes 12582916
  96.6 15.9 %copy-start.5 = (bf16[4,1024,2,256]{3,2,1,0:T(2,128)(2,1)S(1)}, bf16[4,1024,2,256]{3,2,1,0:T(2,128)(2,1)}, u32[]{:S(2)}) copy-start(bf16[4,1024,2,256]{3,2,1,0:T(2,128)(2,1)} %param.10) | copy-start | bytes 12582916
  96.6 15.9 %copy-start.8 = (bf16[4,1024,512]{2,1,0:T(8,128)(2,1)S(1)}, bf16[4,1024,512]{2,1,0:T(8,128)(2,1)}, u32[]{:S(2)}) copy-start(bf16[4,1024,512]{2,1,0:T(8,128)(2,1)} %z_ref.7) | copy-start | bytes 12582916
  96.6 15.9 %copy-start.12 = (bf16[4,16,128,256]{3,2,1,0:T(8,128)(2,1)S(1)}, bf16[4,16,128,256]{3,2,1,0:T(8,128)(2,1)}, u32[]{:S(2)}) copy-start(bf16[4,16,128,256]{3,2,1,0:T(8,128)(2,1)} %copy-done.10) | copy-start | bytes 12582916
  105.1 2.2 %copy-start = (bf16[4,1024,512]{2,1,0:T(8,128)(2,1)S(1)}, bf16[4,1024,512]{2,1,0:T(8,128)(2,1)}, u32[]{:S(2)}) copy-start(bf16[4,1024,512]{2,1,0:T(8,128)(2,1)} %outputs.4.refs_13_.held_ref) | copy-start | bytes 12582916
  108.2 12.8 %collective-permute-start.12 = (bf16[4,128,128]{2,1,0:T(8,128)(2,1)S(1)}, bf16[4,128,128]{2,1,0:T(8,128)(2,1)S(1)}, u32[]{:S(2)}, u32[]{:S(2)}) collective-permute-start(bf16[4,128,128]{2,1,0:T(8,128)(2,1)S(1)} %get-tuple-element.47.refs_7_), channel_id=1, source_target_pairs={{16,0},{24,8},{17,1},{25,9},{18,2},{26,10},{19,3},{27,11},{20,4},{... | collective-permute-start | bytes 393224 | tf_op jit(solution)/shard_map/ppermute | solution.py:567
  109.7 11.2 %collective-permute-start.11 = (bf16[4,128,128]{2,1,0:T(8,128)(2,1)S(1)}, bf16[4,128,128]{2,1,0:T(8,128)(2,1)S(1)}, u32[]{:S(2)}, u32[]{:S(2)}) collective-permute-start(bf16[4,128,128]{2,1,0:T(8,128)(2,1)S(1)} %get-tuple-element.46.after_ref.refs_5_), channel_id=1, source_target_pairs={{0,16},{8,24},{16,0},{24,8},{1,17},{9,25},{17,1},{25,9},{2,18},{10... | collective-permute-start | bytes 393224 | tf_op jit(solution)/shard_map/ppermute | solution.py:567
  112.4 18.5 %copy-start.36 = (bf16[2,1024,128]{2,1,0:T(8,128)(2,1)S(1)}, bf16[2,1024,128]{2,1,0:T(8,128)(2,1)}, u32[]{:S(2)}) copy-start(bf16[2,1024,128]{2,1,0:T(8,128)(2,1)} %copy-done.35) | copy-start | bytes 1572868
  121.0 2.2 %copy-start.1 = (bf16[4,1024,512]{2,1,0:T(8,128)(2,1)S(1)}, bf16[4,1024,512]{2,1,0:T(8,128)(2,1)}, u32[]{:S(2)}) copy-start(bf16[4,1024,512]{2,1,0:T(8,128)(2,1)} %outputs.5.refs_10_.held_ref) | copy-start | bytes 12582916
  125.0 30.6 %all-to-all-start.1 = ((bf16[8,2,128,128]{3,2,1,0:T(8,128)(2,1)}), bf16[8,2,128,128]{3,2,1,0:T(8,128)(2,1)S(1)}, u32[]{:S(2)}, u32[]{:S(2)}) async-start(bf16[8,2,128,128]{3,2,1,0:T(8,128)(2,1)} %get-tuple-element.55), calls=%async_computation.1 | async-start | bytes 1048576 | tf_op jit(solution)/shard_map/all_to_all | solution.py:653
  131.0 2.2 %copy-start.6 = (bf16[4,1024,2,256]{3,2,1,0:T(2,128)(2,1)S(1)}, bf16[4,1024,2,256]{3,2,1,0:T(2,128)(2,1)}, u32[]{:S(2)}) copy-start(bf16[4,1024,2,256]{3,2,1,0:T(2,128)(2,1)} %param.10) | copy-start | bytes 12582916
  133.2 2.2 %copy-start.9 = (bf16[4,1024,512]{2,1,0:T(8,128)(2,1)S(1)}, bf16[4,1024,512]{2,1,0:T(8,128)(2,1)}, u32[]{:S(2)}) copy-start(bf16[4,1024,512]{2,1,0:T(8,128)(2,1)} %z_ref.7) | copy-start | bytes 12582916
  135.4 1.6 %copy-start.28 = (bf16[2,16,128,256]{3,2,1,0:T(8,128)(2,1)S(1)}, bf16[2,16,128,256]{3,2,1,0:T(8,128)(2,1)}, u32[]{:S(2)}) copy-start(bf16[2,16,128,256]{3,2,1,0:T(8,128)(2,1)} %copy-done.27) | copy-start | bytes 6291460
  137.0 1.6 %copy-start.30 = (bf16[2,8,2,128,256]{4,3,2,1,0:T(8,128)(2,1)S(1)}, bf16[2,8,2,128,256]{4,3,2,1,0:T(8,128)(2,1)}, u32[]{:S(2)}) copy-start(bf16[2,8,2,128,256]{4,3,2,1,0:T(8,128)(2,1)} %copy-done.29) | copy-start | bytes 6291460
  138.6 8.5 %copy-start.32 = (bf16[2,16,128,256]{3,2,1,0:T(8,128)(2,1)S(1)}, bf16[2,16,128,256]{3,2,1,0:T(8,128)(2,1)}, u32[]{:S(2)}) copy-start(bf16[2,16,128,256]{3,2,1,0:T(8,128)(2,1)} %copy-done.31) | copy-start | bytes 6291460
  138.6 8.5 %copy-start.34 = (bf16[2,8,2,128,256]{4,3,2,1,0:T(8,128)(2,1)S(1)}, bf16[2,8,2,128,256]{4,3,2,1,0:T(8,128)(2,1)}, u32[]{:S(2)}) copy-start(bf16[2,8,2,128,256]{4,3,2,1,0:T(8,128)(2,1)} %copy-done.33) | copy-start | bytes 6291460
  138.6 8.5 %copy-start.38 = (bf16[2,1024,128]{2,1,0:T(8,128)(2,1)S(1)}, bf16[2,1024,128]{2,1,0:T(8,128)(2,1)}, u32[]{:S(2)}) copy-start(bf16[2,1024,128]{2,1,0:T(8,128)(2,1)} %copy-done.37) | copy-start | bytes 1572868

commit v2 on v1

--- a/solution.py
+++ b/solution.py
@@ -13,8 +13,9 @@
 BLOCK = 128
 TINY = 16
 EDGE = 8
+HALF = BLOCK // 2
 EPSILON = 1e-06
-VMEM_BYTES = 20 * 1024 * 1024
+VMEM_BYTES = 56 * 1024 * 1024
 F32 = jnp.float32
 BF16 = jnp.bfloat16
 
@@ -28,18 +29,11 @@
     return half + half * jnp.tanh(half)
 
 
-def load_padded(pad_ref, halo, raw_ref):
-    rim = halo.shape[0]
-    pad_ref[0:rim, :] = halo
-    pad_ref[rim:, :] = raw_ref[0].astype(F32)
-
-
-def mixed_rows(pad_ref, taps, rim, first, step, c):
+def mixed_rows(pad_ref, taps, c, columns):
     total = None
     for i in range(CONV):
-        start = rim + first + step * (c * BLOCK + i - (CONV - 1))
-        stride = None if step == 1 else step
-        term = pad_ref[pl.ds(start, BLOCK, stride), :] * taps[i]
+        start = EDGE - (CONV - 1) + i + c * BLOCK
+        term = pad_ref[start : start + BLOCK, columns] * taps[i]
         total = term if total is None else total + term
     return silu(total)
 
@@ -77,12 +71,38 @@
     return jnp.concatenate(parts, axis=0).T
 
 
-def prepare_kernel(
-    first, count, head, group, chunks, key_heads,
-    length_ref, qk_ref, v_ref, halo_ref, qk_taps_ref, v_taps_ref, log_ref, gain_ref, after_ref,
-    kn_ref, wu_ref, start_ref, state_ref, trans_ref,
-    qk_pad, v_pad, halo_scr, m_scr, b_scr, fade_scr, st_scr, a_scr, x_scr,
-):
+def mix(qk_ref, halo_ref, taps_ref, qn_ref, kn_ref, raw_scr, dense_scr, key_heads, chunks):
+    kinds = 2 * key_heads
+    tok = chunks * BLOCK
+    halo = halo_ref[0].astype(F32)
+    taps = taps_ref[...].astype(F32)
+    raw_scr[...] = qk_ref[0].astype(F32)
+    for kind in range(kinds):
+        columns = slice(kind * DK, (kind + 1) * DK)
+        for i in range(1, CONV):
+            source = 2 * EDGE - i * kinds + kind
+            dense_scr[EDGE - i : EDGE - i + 1, columns] = halo[source : source + 1]
+        dense_scr[EDGE:, columns] = raw_scr[pl.ds(kind, tok, kinds), :]
+    for c in range(chunks):
+        span = slice(c * BLOCK, (c + 1) * BLOCK)
+        for kind in range(kinds):
+            own = [taps[n : n + 1] for n in range(kind, taps.shape[0], kinds)]
+            rows = unit_rows(mixed_rows(dense_scr, own, c, slice(kind * DK, (kind + 1) * DK)))
+            to_ref = kn_ref if kind % 2 else qn_ref
+            to_ref[0, span, kind // 2 * DK : (kind // 2 + 1) * DK] = rows.astype(BF16)
+
+
+def prepare_kernel(first, count, head, group, chunks, key_heads, mixes, *refs):
+    length_ref, v_ref, halo_ref, v_taps_ref, log_ref, gain_ref, after_ref = refs[:7]
+    refs = refs[7:]
+    if mixes:
+        qk_ref, qk_taps_ref, wu_ref, start_ref, map_ref, qn_ref, kn_ref = refs[:7]
+        v_pad, m_scr, b_scr, fade_scr, st_scr, a_scr, x_scr, raw_scr, dense_scr = refs[7:]
+        key_columns = slice(head * DK, (head + 1) * DK)
+    else:
+        kn_ref, wu_ref, start_ref, map_ref = refs[:4]
+        v_pad, m_scr, b_scr, fade_scr, st_scr, a_scr, x_scr = refs[4:]
+        key_columns = slice(0, DK)
     step = pl.program_id(0)
     used = length_ref[first + jnp.minimum(step, count - 1)] - lax.axis_index("seq") * (chunks * BLOCK)
     units = [(h, c) for c in range(chunks) for h in range(group)]
@@ -99,7 +119,7 @@
         narrow, moved = [], []
         for h in range(group):
             narrow.append(st_scr[h].astype(BF16))
-            start_ref[0, c, h] = narrow[h]
+            start_ref[0, h, c * DK : (c + 1) * DK, :] = narrow[h]
         for h in range(group):
             moved.append(dot(m_scr[1 - slot, c, h], narrow[h]))
         for h in range(group):
@@ -110,8 +130,8 @@
                 st_scr[h, :, :DV] = state
                 st_scr[h, :, DV:] = trans
             else:
-                state_ref[h] = state.astype(BF16)
-                trans_ref[h] = trans.astype(BF16)
+                map_ref[h, :, :DV] = state.astype(BF16)
+                map_ref[h, :, DV:] = trans.astype(BF16)
 
     todo = [begin] + [functools.partial(advance, c) for c in range(chunks)]
 
@@ -129,7 +149,9 @@
 
         @pl.when(step < count)
         def _():
-            kn_ref[...] = jnp.zeros_like(kn_ref)
+            if mixes:
+                qn_ref[...] = jnp.zeros_like(qn_ref)
+                kn_ref[...] = jnp.zeros_like(kn_ref)
             wu_ref[...] = jnp.zeros_like(wu_ref)
             fade_scr[slot] = jnp.ones(fade_scr.shape[1:], F32)
             m_scr[slot] = jnp.zeros(m_scr.shape[1:], BF16)
@@ -137,18 +159,16 @@
 
     @pl.when(live)
     def _():
+        if mixes:
+            mix(qk_ref, halo_ref, qk_taps_ref, qn_ref, kn_ref, raw_scr, dense_scr, key_heads, chunks)
         halo = halo_ref[0].astype(F32)
-        halo_scr[...] = halo
-        load_padded(qk_pad, halo[: 2 * EDGE], qk_ref)
         v_pad[EDGE:, :] = v_ref[0].astype(F32)
         for i in range(CONV - 1):
             for h in range(group):
                 source = 2 * EDGE + (i * key_heads + head) * group + h
-                v_pad[EDGE - CONV + 1 + i : EDGE - CONV + 2 + i, h * DV : (h + 1) * DV] = halo_scr[
-                    source : source + 1, :
+                v_pad[EDGE - CONV + 1 + i : EDGE - CONV + 2 + i, h * DV : (h + 1) * DV] = halo[
+                    source : source + 1
                 ]
-        all_taps = qk_taps_ref[...].astype(F32)
-        k_taps = [all_taps[n : n + 1] for n in range(2 * head + 1, all_taps.shape[0], 2 * key_heads)]
         v_all_taps = v_taps_ref[...].astype(F32)
         v_taps = [v_all_taps[i : i + 1] for i in range(CONV)]
         run(1)
@@ -169,12 +189,7 @@
         part_of = small_lane // TINY
         tiny_eye = jnp.where(small_row == small_lane % TINY, 1.0, 0.0).astype(F32)
 
-        keys = []
-        for c in range(chunks):
-            kc = mixed_rows(qk_pad, k_taps, 2 * EDGE, 2 * head + 1, 2 * key_heads, c)
-            kc = unit_rows(kc).astype(BF16)
-            kn_ref[0, c * BLOCK : (c + 1) * BLOCK, :] = kc
-            keys.append(kc)
+        keys = [kn_ref[0, c * BLOCK : (c + 1) * BLOCK, key_columns] for c in range(chunks)]
         turned = [kc.T for kc in keys]
         run(1)
 
@@ -207,7 +222,7 @@
 
         run(1)
         size = TINY
-        while size < BLOCK:
+        while size < HALF:
             odd = [s for s in range(size, BLOCK, 2 * size)]
             half_lane = lax.broadcasted_iota(jnp.int32, (BLOCK // 2, BLOCK), 1)
             half_row = lax.broadcasted_iota(jnp.int32, (BLOCK // 2, BLOCK), 0)
@@ -233,20 +248,24 @@
             size *= 2
 
         for c in range(chunks):
-            vc = mixed_rows(v_pad, v_taps, EDGE, 0, 1, c).astype(BF16).astype(F32)
+            vc = mixed_rows(v_pad, v_taps, c, slice(0, group * DV)).astype(BF16).astype(F32)
             kc = keys[c].astype(F32)
             for h in range(group):
                 r = h * chunks + c
-                right = jnp.concatenate(
-                    [
-                        (kc * column(2, h, c)).astype(BF16),
-                        (vc[:, h * DV : (h + 1) * DV] * column(1, h, c)).astype(BF16),
-                    ],
-                    axis=1,
-                )
-                wu_ref[0, r] = dot(x_scr[r], right).astype(BF16)
-            if c == chunks // 2:
-                run(1)
+                wu_ref[0, r, :, :DK] = (kc * column(2, h, c)).astype(BF16)
+                wu_ref[0, r, :, DK:] = (vc[:, h * DV : (h + 1) * DV] * column(1, h, c)).astype(BF16)
+        run(1)
+        for h, c in units:
+            r = h * chunks + c
+            wu_ref[0, r, :HALF] = dot(x_scr[r, :HALF, :HALF], wu_ref[0, r, :HALF]).astype(BF16)
+        run(1)
+        for h, c in units:
+            r = h * chunks + c
+            rest = wu_ref[0, r, HALF:].astype(F32) - dot(a_scr[r, HALF:, :HALF], wu_ref[0, r, :HALF])
+            wu_ref[0, r, HALF:] = rest.astype(BF16)
+        for h, c in units:
+            r = h * chunks + c
+            wu_ref[0, r, HALF:] = dot(x_scr[r, HALF:, HALF:], wu_ref[0, r, HALF:]).astype(BF16)
         run(len(todo))
         for c in range(chunks):
             sums = cum[:, c * BLOCK : (c + 1) * BLOCK]
@@ -262,7 +281,7 @@
                 b_scr[slot, c, h] = both[:, DK:]
 
 
-def prepare(job, lengths, qk_rows, v_in, halo, qk_taps, v_taps, log_decay, write_gain, key_heads, after):
+def prepare(job, lengths, qk_rows, v_in, halo, qk_taps, v_taps, log_decay, write_gain, key_heads, mixed, after):
     head, first, count = job
     tok = v_in.shape[1]
     value_heads = v_in.shape[2] // DV
@@ -270,6 +289,7 @@
     chunks = tok // BLOCK
     rows = group * chunks
     wide = group * DV
+    mixes = mixed is None
 
     def now(i):
         return jnp.minimum(i, count - 1)
@@ -280,61 +300,73 @@
     def whole_of(i, lengths):
         return (first + now(i), 0, 0)
 
+    operands = [v_in, halo, v_taps, log_decay, write_gain, after]
+    in_specs = [
+        pl.BlockSpec((1, tok, wide), lambda i, lengths: (first + now(i), 0, head)),
+        pl.BlockSpec((1,) + halo.shape[1:], whole_of),
+        pl.BlockSpec((CONV, wide), lambda i, lengths: (0, head)),
+        pl.BlockSpec((1, value_heads, tok), whole_of),
+        pl.BlockSpec((1, value_heads, tok), whole_of),
+        pl.BlockSpec(memory_space=pltpu.HBM),
+    ]
+    out_specs = [
+        pl.BlockSpec((1, rows, BLOCK, DK + DV), lambda i, lengths: (now(i), 0, 0, 0)),
+        pl.BlockSpec((1, group, chunks * DK, DV + DK), lambda i, lengths: (before(i), 0, 0, 0)),
+        pl.BlockSpec((group, DK, DV + DK), lambda i, lengths: (before(i), 0, 0)),
+    ]
+    out_shape = [
+        jax.ShapeDtypeStruct((count, rows, BLOCK, DK + DV), BF16),
+        jax.ShapeDtypeStruct((count, group, chunks * DK, DV + DK), BF16),
+        jax.ShapeDtypeStruct((count * group, DK, DV + DK), BF16),
+    ]
+    scratch = [
+        pltpu.VMEM((tok + EDGE, wide), F32),
+        pltpu.VMEM((2, chunks, group, DK, DK), BF16),
+        pltpu.VMEM((2, chunks, group, DK, DV), F32),
+        pltpu.VMEM((2, chunks, group, BLOCK), F32),
+        pltpu.VMEM((group, DK, DV + DK), F32),
+        pltpu.VMEM((rows, BLOCK, BLOCK), BF16),
+        pltpu.VMEM((rows, BLOCK, BLOCK), BF16),
+    ]
+    if mixes:
+        operands += [qk_rows, qk_taps]
+        in_specs += [
+            pl.BlockSpec((1,) + qk_rows.shape[1:], whole_of),
+            pl.BlockSpec(qk_taps.shape, lambda i, lengths: (0, 0)),
+        ]
+        out_specs += [pl.BlockSpec((1, tok, key_heads * DK), lambda i, lengths: (now(i), 0, 0))] * 2
+        out_shape += [jax.ShapeDtypeStruct((count, tok, key_heads * DK), BF16)] * 2
+        scratch += [
+            pltpu.VMEM(qk_rows.shape[1:], F32),
+            pltpu.VMEM((tok + EDGE, 2 * key_heads * DK), F32),
+        ]
+    else:
+        operands.append(mixed)
+        in_specs.append(pl.BlockSpec((1, tok, DK), lambda i, lengths: (first + now(i), 0, head)))
     return pl.pallas_call(
-        functools.partial(prepare_kernel, first, count, head, group, chunks, key_heads),
+        functools.partial(prepare_kernel, first, count, head, group, chunks, key_heads, mixes),
         grid_spec=pltpu.PrefetchScalarGridSpec(
             num_scalar_prefetch=1,
             grid=(count + 1,),
-            in_specs=[
-                pl.BlockSpec((1,) + qk_rows.shape[1:], whole_of),
-                pl.BlockSpec((1, tok, wide), lambda i, lengths: (first + now(i), 0, head)),
-                pl.BlockSpec((1,) + halo.shape[1:], whole_of),
-                pl.BlockSpec(qk_taps.shape, lambda i, lengths: (0, 0)),
-                pl.BlockSpec((CONV, wide), lambda i, lengths: (0, head)),
-                pl.BlockSpec((1, value_heads, tok), whole_of),
-                pl.BlockSpec((1, value_heads, tok), whole_of),
-                pl.BlockSpec(memory_space=pl.ANY),
-            ],
-            out_specs=[
-                pl.BlockSpec((1, tok, DK), lambda i, lengths: (now(i), 0, 0)),
-                pl.BlockSpec((1, rows, BLOCK, DK + DV), lambda i, lengths: (now(i), 0, 0, 0)),
-                pl.BlockSpec((1, chunks, group, DK, DV + DK), lambda i, lengths: (before(i), 0, 0, 0, 0)),
-                pl.BlockSpec((group, DK, DV), lambda i, lengths: (before(i), 0, 0)),
-                pl.BlockSpec((group, DK, DK), lambda i, lengths: (before(i), 0, 0)),
-            ],
-            scratch_shapes=[
-                pltpu.VMEM((qk_rows.shape[1] + 2 * EDGE, DK), F32),
-                pltpu.VMEM((tok + EDGE, wide), F32),
-                pltpu.VMEM(halo.shape[1:], F32),
-                pltpu.VMEM((2, chunks, group, DK, DK), BF16),
-                pltpu.VMEM((2, chunks, group, DK, DV), F32),
-                pltpu.VMEM((2, chunks, group, BLOCK), F32),
-                pltpu.VMEM((group, DK, DV + DK), F32),
-                pltpu.VMEM((rows, BLOCK, BLOCK), BF16),
-                pltpu.VMEM((rows, BLOCK, BLOCK), BF16),
-            ],
+            in_specs=in_specs,
+            out_specs=out_specs,
+            scratch_shapes=scratch,
         ),
-        out_shape=[
-            jax.ShapeDtypeStruct((count, tok, DK), BF16),
-            jax.ShapeDtypeStruct((count, rows, BLOCK, DK + DV), BF16),
-            jax.ShapeDtypeStruct((count, chunks, group, DK, DV + DK), BF16),
-            jax.ShapeDtypeStruct((count * group, DK, DV), BF16),
-            jax.ShapeDtypeStruct((count * group, DK, DK), BF16),
-        ],
+        out_shape=out_shape,
         compiler_params=pltpu.CompilerParams(vmem_limit_bytes=VMEM_BYTES),
         cost_estimate=pl.CostEstimate(flops=5 * 10**9 * count, bytes_accessed=4 * 2**20 * count, transcendentals=10**6),
         name="prepare",
-    )(lengths, qk_rows, v_in, halo, qk_taps, v_taps, log_decay, write_gain, after)
+    )(lengths, *operands)
 
 
 def outputs_kernel(
-    first, head, group, chunks, key_heads,
-    length_ref, qk_ref, halo_ref, qk_taps_ref, kn_ref, wu_ref, start_ref, log_ref, gain_ref,
-    enter_ref, z_ref, norm_ref, held_ref, after_ref,
+    first, head, group, chunks,
+    length_ref, qn_ref, kn_ref, wu_ref, start_ref, log_ref, gain_ref, enter_ref, z_ref, norm_ref, held_ref, after_ref,
     out_ref,
-    qk_pad,
+    first_scr, score_scr, raw_scr,
 ):
     used = length_ref[first + pl.program_id(0)] - lax.axis_index("seq") * (chunks * BLOCK)
+    units = [(h, c) for c in range(chunks) for h in range(group)]
 
     @pl.when(used <= 0)
     def _():
@@ -342,9 +374,6 @@
 
     @pl.when(used > 0)
     def _():
-        load_padded(qk_pad, halo_ref[0].astype(F32)[: 2 * EDGE], qk_ref)
-        all_taps = qk_taps_ref[...].astype(F32)
-        q_taps = [all_taps[n : n + 1] for n in range(2 * head, all_taps.shape[0], 2 * key_heads)]
         cum, gain = gates_of_heads(log_ref, gain_ref, used, head, group)
         faded = jnp.exp(cum)
         columns = as_columns(jnp.concatenate([cum, faded, gain, gain], axis=0), chunks)
@@ -357,31 +386,37 @@
         lane = lax.broadcasted_iota(jnp.int32, (BLOCK, BLOCK), 1)
         upto = row >= lane
         norm_gain = norm_ref[...]
+
+        def span(c):
+            return slice(c * BLOCK, (c + 1) * BLOCK)
+
+        for h in range(group):
+            moved = dot(start_ref[0, h, :, DV:], enter_ref[h])
+            first_scr[h] = (moved + start_ref[0, h, :, :DV].astype(F32)).astype(BF16)
         for c in range(chunks):
-            span = slice(c * BLOCK, (c + 1) * BLOCK)
-            qc = mixed_rows(qk_pad, q_taps, 2 * EDGE, 2 * head, 2 * key_heads, c)
-            qc = unit_rows(qc).astype(BF16)
-            qk = dot(qc, kn_ref[0, span, :].T)
-            q_wide = qc.astype(F32)
-            valid = row + c * BLOCK < used
+            qk = dot(qn_ref[0, span(c), :], kn_ref[0, span(c), :].T)
             for h in range(group):
-                r = h * chunks + c
-                cols = slice(h * DV, (h + 1) * DV)
-                first_state = dot(start_ref[0, c, h, :, DV:], enter_ref[h])
-                first_state = (first_state + start_ref[0, c, h, :, :DV].astype(F32)).astype(BF16)
-                ratio = jnp.exp(column(0, h, c) - cum[h : h + 1, span])
-                scores = jnp.where(upto, ratio * qk, 0.0).astype(BF16)
-                both = dot(scores, wu_ref[0, r])
-                seen = (q_wide * column(1, h, c) - both[:, :DK]).astype(BF16)
-                raw = dot(seen, first_state) + both[:, DK:]
-                mean = jnp.sum(raw * raw, axis=-1, keepdims=True) * (1.0 / DV)
-                gated = raw * lax.rsqrt(mean + EPSILON) * norm_gain * silu(z_ref[0, span, cols].astype(F32))
-                out_ref[0, span, cols] = jnp.where(valid, gated, 0.0).astype(BF16)
+                ratio = jnp.exp(column(0, h, c) - cum[h : h + 1, span(c)])
+                score_scr[h * chunks + c] = jnp.where(upto, ratio * qk, 0.0).astype(BF16)
+        for h, c in units:
+            r = h * chunks + c
+            both = dot(score_scr[r], wu_ref[0, r])
+            seen = qn_ref[0, span(c), :].astype(F32) * column(1, h, c) - both[:, :DK]
+            score_scr[r] = seen.astype(BF16)
+            raw_scr[r] = both[:, DK:]
+        for h, c in units:
+            r = h * chunks + c
+            raw_scr[r] += dot(score_scr[r], first_scr[h, span(c), :])
+        for h, c in units:
+            raw = raw_scr[h * chunks + c]
+            cols = slice(h * DV, (h + 1) * DV)
+            mean = jnp.sum(raw * raw, axis=-1, keepdims=True) * (1.0 / DV)
+            gated = raw * lax.rsqrt(mean + EPSILON) * norm_gain * silu(z_ref[0, span(c), cols].astype(F32))
+            out_ref[0, span(c), cols] = jnp.where(row + c * BLOCK < used, gated, 0.0).astype(BF16)
 
 
 def outputs(
-    job, piece, lengths, qk_rows, halo, qk_taps, kn, wu, starts, log_decay, write_gain, enter, gate_z, norm_gain,
-    key_heads, held, after,
+    job, piece, lengths, qn, kn, wu, starts, log_decay, write_gain, enter, gate_z, norm_gain, key_heads, held, after,
 ):
     head, first, _ = job
     begin, count = piece
@@ -392,6 +427,7 @@
     wide = group * DV
     value_heads = key_heads * group
     shift = begin - first
+    from_mix = begin if qn.shape[0] == prompts else shift
 
     def whole_of(i, lengths):
         return (begin + i, 0, 0)
@@ -399,37 +435,42 @@
     def wide_of(i, lengths):
         return (begin + i, 0, head)
 
+    def mixed_of(i, lengths):
+        return (from_mix + i, 0, head)
+
     empty = held is None
     return pl.pallas_call(
-        functools.partial(outputs_kernel, begin, head, group, chunks, key_heads),
+        functools.partial(outputs_kernel, begin, head, group, chunks),
         grid_spec=pltpu.PrefetchScalarGridSpec(
             num_scalar_prefetch=1,
             grid=(count,),
             in_specs=[
-                pl.BlockSpec((1,) + qk_rows.shape[1:], whole_of),
-                pl.BlockSpec((1,) + halo.shape[1:], whole_of),
-                pl.BlockSpec(qk_taps.shape, lambda i, lengths: (0, 0)),
-                pl.BlockSpec((1, tok, DK), lambda i, lengths: (shift + i, 0, 0)),
+                pl.BlockSpec((1, tok, DK), mixed_of),
+                pl.BlockSpec((1, tok, DK), mixed_of),
                 pl.BlockSpec((1, rows, BLOCK, DK + DV), lambda i, lengths: (shift + i, 0, 0, 0)),
-                pl.BlockSpec((1, chunks, group, DK, DV + DK), lambda i, lengths: (shift + i, 0, 0, 0, 0)),
+                pl.BlockSpec((1, group, chunks * DK, DV + DK), lambda i, lengths: (shift + i, 0, 0, 0)),
                 pl.BlockSpec((1, value_heads, tok), whole_of),
                 pl.BlockSpec((1, value_heads, tok), whole_of),
                 pl.BlockSpec((group, DK, DV), lambda i, lengths: (shift + i, 0, 0)),
                 pl.BlockSpec((1, tok, wide), wide_of),
                 pl.BlockSpec((1, DV), lambda i, lengths: (0, 0)),
-                pl.BlockSpec(memory_space=pl.ANY),
-                pl.BlockSpec(memory_space=pl.ANY),
+                pl.BlockSpec(memory_space=pltpu.HBM),
+                pl.BlockSpec(memory_space=pltpu.HBM),
             ],
             out_specs=pl.BlockSpec((1, tok, wide), wide_of),
-            scratch_shapes=[pltpu.VMEM((qk_rows.shape[1] + 2 * EDGE, DK), F32)],
+            scratch_shapes=[
+                pltpu.VMEM((group, chunks * DK, DV), BF16),
+                pltpu.VMEM((rows, BLOCK, BLOCK), BF16),
+                pltpu.VMEM((rows, BLOCK, DV), F32),
+            ],
         ),
         out_shape=jax.ShapeDtypeStruct((prompts, tok, width), BF16),
-        input_output_aliases={} if empty else {12: 0},
+        input_output_aliases={} if empty else {10: 0},
         compiler_params=pltpu.CompilerParams(vmem_limit_bytes=VMEM_BYTES),
         cost_estimate=pl.CostEstimate(flops=3 * 10**9 * count, bytes_accessed=4 * 2**20 * count, transcendentals=10**6),
         name="outputs",
     )(
-        lengths, qk_rows, halo, qk_taps, kn, wu, starts, log_decay, write_gain, enter, gate_z,
+        lengths, qn, kn, wu, starts, log_decay, write_gain, enter, gate_z,
         norm_gain.reshape(1, DV), after if empty else held, lengths if after is held else after,
     )
 
@@ -444,37 +485,36 @@
 
 
 def compose_maps(ins, outs):
-    state_ref, trans_ref, state_other_ref, trans_other_ref = ins
+    own_ref, other_ref = ins
     _, odd = own_chip()
-    for n in range(state_ref.shape[0]):
-        state_early, state_late = early_late(state_ref[n], state_other_ref[n], odd)
-        trans_early, trans_late = early_late(trans_ref[n], trans_other_ref[n], odd)
-        both = dot(trans_late, jnp.concatenate([state_early, trans_early], axis=1))
-        outs[0][n] = (both[:, :DV] + state_late.astype(F32)).astype(BF16)
-        outs[1][n] = both[:, DV:].astype(BF16)
-
-
-def close_maps(chips, ins, outs):
-    state_ref, trans_ref, state_other_ref, trans_other_ref = ins[:4]
-    states, transes = ins[4 : 4 + chips], ins[4 + chips :]
+    for n in range(own_ref.shape[0]):
+        early, late = early_late(own_ref[n], other_ref[n], odd)
+        both = dot(late[:, DV:], early)
+        outs[0][n, :, :DV] = (both[:, :DV] + late[:, :DV].astype(F32)).astype(BF16)
+        outs[0][n, :, DV:] = both[:, DV:].astype(BF16)
+
+
+def close_maps(ins, outs):
+    own_ref, other_ref = ins[:2]
+    refs = ins[2:]
+    chips = len(refs)
     chip, odd = own_chip()
 
-    def of_chip(refs, j, n):
+    def of_chip(j, n):
         value = refs[0][n]
         for k in range(1, chips):
             value = jnp.where((chip + chips - k) % chips == j, refs[k][n], value)
         return value
 
-    for n in range(state_ref.shape[0]):
-        running = of_chip(states, 0, n)
+    for n in range(own_ref.shape[0]):
+        running = of_chip(0, n)[:, :DV]
         entering = jnp.zeros_like(running)
         for j in range(1, chips):
             entering = jnp.where(chip == j, running, entering)
-            running = dot(of_chip(transes, j, n), running) + of_chip(states, j, n).astype(F32)
-            running = running.astype(BF16)
-        state_early, _ = early_late(state_ref[n], state_other_ref[n], odd)
-        trans_early, _ = early_late(trans_ref[n], trans_other_ref[n], odd)
-        second = (dot(trans_early, entering) + state_early.astype(F32)).astype(BF16)
+            there = of_chip(j, n)
+            running = (dot(there[:, DV:], running) + there[:, :DV].astype(F32)).astype(BF16)
+        early, _ = early_late(own_ref[n], other_ref[n], odd)
+        second = (dot(early[:, DV:], entering) + early[:, :DV].astype(F32)).astype(BF16)
         outs[0][n] = jnp.where(odd, second, entering)
         outs[1][n] = running
 
@@ -495,11 +535,11 @@
     if compose is not None:
         steps.append(("compose", len(operands), len(compose), len(shapes)))
         operands += compose
-        shapes += [compose[0], compose[1]]
+        shapes += [compose[0]]
     if close is not None:
         steps.append(("close", len(operands), len(close), len(shapes)))
         operands += close
-        shapes += [close[0], close[0]]
+        shapes += [jax.ShapeDtypeStruct((close[0].shape[0], DK, DV), BF16)] * 2
         if earlier is not None:
             steps.append(("choose", len(operands), len(earlier), len(shapes)))
             operands += earlier
@@ -512,9 +552,9 @@
         for kind, at, size, to in steps:
             part = ins[at : at + size]
             if kind == "compose":
-                compose_maps(part, outs[to : to + 2])
+                compose_maps(part, outs[to : to + 1])
             elif kind == "close":
-                close_maps((size - 4) // 2, part, outs[to : to + 2])
+                close_maps(part, outs[to : to + 2])
                 closed = outs[to + 1]
             else:
                 choose_finals(group, ins[0], list(part) + [closed], outs[to:])
@@ -524,7 +564,7 @@
         kernel,
         in_specs=[pl.BlockSpec(memory_space=pltpu.SMEM)]
         + [vmem] * (len(operands) - 1)
-        + [pl.BlockSpec(memory_space=pl.ANY)],
+        + [pl.BlockSpec(memory_space=pltpu.HBM)],
         out_specs=[vmem] * len(out_shape),
         out_shape=out_shape,
         compiler_params=pltpu.CompilerParams(vmem_limit_bytes=VMEM_BYTES),
@@ -556,14 +596,10 @@
     return lax.ppermute(block, "seq", [(i, i ^ 1) for i in range(count)])
 
 
-def from_chip_behind(block, distance, skip_first):
+def from_chip_behind(block, distance):
     count = lax.axis_size("seq")
     chips = count // 2
-    route = [
-        (i, ((i // 2 + distance) % chips) * 2 + i % 2)
-        for i in range(count)
-        if not (skip_first and i < 2)
-    ]
+    route = [(i, ((i // 2 + distance) % chips) * 2 + i % 2) for i in range(count)]
     return lax.ppermute(block, "seq", route)
 
 
@@ -611,21 +647,23 @@
 
     def emit(attended, last):
         job, piece = waiting.pop(0)
-        kn, wu, starts = made[job]
+        qn, kn, wu, starts = made[job]
         attended = outputs(
-            jobs[job], piece, prompt_lengths, qk_rows, halo, qk_taps, kn, wu, starts, log_decay, write_gain,
+            jobs[job], piece, prompt_lengths, qn, kn, wu, starts, log_decay, write_gain,
             entered[job], gate_z, norm_gain, key_heads, attended, last,
         )
         return attended, attended
 
     for t in range(total + 2):
         if t < total:
-            kn, wu, starts, state, trans = prepare(
-                jobs[t], prompt_lengths, qk_rows, v_in, halo, qk_taps, conv_v, log_decay, write_gain, key_heads, last
+            mixed = None if jobs[t][0] == 0 else made[0][:2]
+            wu, starts, own_map, *new = prepare(
+                jobs[t], prompt_lengths, qk_rows, v_in, halo, qk_taps, conv_v, log_decay, write_gain, key_heads,
+                mixed and mixed[1], last,
             )
-            made[t] = kn, wu, starts
-            maps[t] = [state, trans, pair_swap(state), pair_swap(trans)]
-            last = state
+            made[t] = (*(mixed or new), wu, starts)
+            maps[t] = [own_map, pair_swap(own_map)]
+            last = own_map
         elif waiting:
             attended, last = emit(attended, last)
         compose = maps[t - 1] if 0 <= t - 1 < total else None
@@ -640,13 +678,8 @@
         results = state_step(placement, group, compose, close, earlier, last)
         last = results[0]
         if compose is not None:
-            state, trans = results[:2]
-            results = results[2:]
-            states, transes = [state], [trans]
-            for k in range(1, chips):
-                states.append(from_chip_behind(state, k, False))
-                transes.append(from_chip_behind(trans, k, True))
-            chip_maps[t - 1] = states + transes
+            chip_map, results = results[0], results[1:]
+            chip_maps[t - 1] = [chip_map] + [from_chip_behind(chip_map, k) for k in range(1, chips)]
         if close is not None:
             entered[t - 2], finals[t - 2] = results[:2]
             if earlier is not None:

time: 160 us -> 142 us (0.89)
  local copies, waits for them, and re-layouts: 37.9 us -> 7.32 us
  Pallas kernels: 88.3 us -> 114 us
  starting transfers between devices: 30.5 us -> 17.3 us
    unnamed x78 -> x18, local copies, waits for them, and re-layouts: 36.4 us -> 5.79 us
    pallas_call x3, Pallas kernels: 45.5 us -> 66.8 us  [prepare(): pl.pallas_call(functools.partial(prepare_kernel, first, count, head, grou...]
    ppermute x6 -> x3, starting transfers between devices: 12.4 us -> 0.01 us  [from_chip_behind(): return lax.ppermute(block, 'seq', route)]
    pallas_call x4, Pallas kernels: 5.8 us -> 10.6 us  [state_step(): pl.pallas_call(kernel, in_specs=[pl.BlockSpec(memory_space=pltpu.SMEM)] +...]
    pallas_call x1, Pallas kernels: 2.97 us -> 5.25 us  [deliver(): pl.pallas_call(kernel, grid=(count,), in_specs=[pl.BlockSpec((1, group, D...]
    pallas_call x4, Pallas kernels: 34 us -> 31.8 us  [outputs(): pl.pallas_call(functools.partial(outputs_kernel, begin, head, group, chun...]
    ppermute x6 -> x3, starting transfers between devices: 3.91 us -> 3.34 us  [pair_swap(): return lax.ppermute(block, 'seq', [(i, i ^ 1) for i in range(count)])]
  transfers between devices with their start and end apart: 15 -> 9, of which waited for: 1 -> 2; matrix products, arithmetic and copies ran while one was open for 0% -> 0% of each run, Pallas kernels for 40% -> 52%
where the time goes in v2:
time: 142 us; the launch traced here: 141 us
  Pallas kernels  114 us (80%)
  starting transfers between devices  17.3 us (12%)
  local copies, waits for them, and re-layouts  7.32 us (5%)
    pallas_call x3, Pallas kernels, prepare(): pl.pallas_call(functools.partial(prepare_kernel, first, count, head, grou...  66.8 us
    pallas_call x4, Pallas kernels, outputs(): pl.pallas_call(functools.partial(outputs_kernel, begin, head, group, chun...  31.8 us
    all_to_all x2, starting transfers between devices, shards(): sent[jobs[t - 2][0]] = lax.all_to_all(results[2], 'head', 0, 0)  11.6 us
    pallas_call x4, Pallas kernels, state_step(): pl.pallas_call(kernel, in_specs=[pl.BlockSpec(memory_space=pltpu.SMEM)] +...  10.6 us
    unnamed x18, local copies, waits for them, and re-layouts  5.79 us
    pallas_call x1, Pallas kernels, deliver(): pl.pallas_call(kernel, grid=(count,), in_specs=[pl.BlockSpec((1, group, D...  5.25 us
    ppermute x3, starting transfers between devices, pair_swap(): return lax.ppermute(block, 'seq', [(i, i ^ 1) for i in range(count)])  3.34 us
  transfers between devices with their start and end apart: 9, of which 2 were waited for; matrix products, arithmetic and copies ran while one was open for 0% of the time, Pallas kernels for 52%

profile of v2, /device:TPU:0, one launch (start us, length us, event | category | flops | bytes accessed | tf_op | source)
XLA Modules:
  0.0 140.9 jit_solution(6861324203563538559)
XLA Ops:
  0.6 0.7 slice.8
  1.4 0.8 slice.7
  2.2 2.4 %collective-permute-start = (bf16[4,32,128]{2,1,0:T(8,128)(2,1)S(1)}, bf16[4,32,128]{2,1,0:T(8,128)(2,1)S(1)}, u32[]{:S(2)}, u32[]{:S(2)}) collective-permute-start(bf16[4,32,128]{2,1,0:T(8,128)(2,1)S(1)} %pad_maximum_fusion), channel_id=1, source_target_pairs={{0,8},{8,16},{16,24},{1,9},{9,17},{17,25},{2,10},{10,18},{18,26},{... | collective-permute-start | bytes 98312 | tf_op jit(solution)/shard_map/ppermute | solution.py:635
  4.6 0.8 collective-permute-done.refs_2_
  5.4 0.0 copy-start.8
  5.4 0.6 copy-done.8
  6.0 36.0 %prepare.3 = (bf16[4,16,128,256]{3,2,1,0:T(8,128)(2,1)}, bf16[4,2,1024,256]{3,2,1,0:T(8,128)(2,1)}, bf16[8,128,256]{2,1,0:T(8,128)(2,1)}, bf16[4,1024,256]{2,1,0:T(8,128)(2,1)}, bf16[4,1024,256]{2,1,0:T(8,128)(2,1)}) custom-call(s32[4]{0:T(128)} %after_ref.1, bf16[4,1024,512]{2,1,0:T(8,128)(2,1)} %refs_1_.5, bf16[4,32,128]{2,1,0:T(8,128)(2,1)} %copy-done.8, ...), custom_call_target="tpu_custom_call" | custom-call | flops 20000000000 | bytes 16777216 | tf_op jit(solution)/shard_map/prepare/pallas_call | solution.py:346
  42.1 2.8 %collective-permute-start.1 = (bf16[8,128,256]{2,1,0:T(8,128)(2,1)}, bf16[8,128,256]{2,1,0:T(8,128)(2,1)S(1)}, u32[]{:S(2)}, u32[]{:S(2)}) collective-permute-start(bf16[8,128,256]{2,1,0:T(8,128)(2,1)} %get-tuple-element.23.refs_6_.refs_1_.refs_3_), channel_id=1, source_target_pairs={{0,8},{8,0},{16,24},{24,16},{1,9},{9,1},{17,25},{25,17},{2,10},{10... | collective-permute-start | bytes 1572872 | tf_op jit(solution)/shard_map/ppermute | solution.py:596
  44.9 15.5 %prepare.4 = (bf16[2,16,128,256]{3,2,1,0:T(8,128)(2,1)}, bf16[2,2,1024,256]{3,2,1,0:T(8,128)(2,1)}, bf16[4,128,256]{2,1,0:T(8,128)(2,1)}) custom-call(s32[4]{0:T(128)} %after_ref.1, bf16[4,1024,512]{2,1,0:T(8,128)(2,1)} %refs_1_.5, bf16[4,32,128]{2,1,0:T(8,128)(2,1)} %copy-done.8, bf16[4,512]{1,0:T(4,128)(2,1)} %refs_3_.5, f32[4,4,1024]{2,1,0:T(4,128)} %log_ref.7, ...), custom_call_target="tpu_custom_call" | custom-call | flops 10000000000 | bytes 8388608 | tf_op jit(solution)/shard_map/prepare/pallas_call | solution.py:346
  60.3 0.0 collective-permute-start.3
  60.4 0.0 collective-permute-done.1.refs_2_.refs_4_
  60.4 0.0 copy-start.6
  60.4 0.8 copy-done.6
  61.2 2.3 %state_step.4.refs_6_.refs_5_ = bf16[8,128,256]{2,1,0:T(8,128)(2,1)} custom-call(s32[1,8]{1,0:T(1,128)} %refs_0_.13, bf16[8,128,256]{2,1,0:T(8,128)(2,1)} %get-tuple-element.23.refs_6_.refs_1_.refs_3_, bf16[8,128,256]{2,1,0:T(8,128)(2,1)} %copy-done.6, bf16[4,128,256]{2,1,0:T(8,128)(2,1)} %get-tuple-element.24.refs_3_.refs_1_), custom_call_target="tpu_custom_call" | custom-call | flops 1000000000 | bytes 1048576 | tf_op jit(solution)/shard_map/state_step/pallas_call | solution.py:563
  63.5 0.0 collective-permute-start.4
  63.5 15.3 %prepare.5 = (bf16[2,16,128,256]{3,2,1,0:T(8,128)(2,1)}, bf16[2,2,1024,256]{3,2,1,0:T(8,128)(2,1)}, bf16[4,128,256]{2,1,0:T(8,128)(2,1)}) custom-call(s32[4]{0:T(128)} %after_ref.1, bf16[4,1024,512]{2,1,0:T(8,128)(2,1)} %refs_1_.5, bf16[4,32,128]{2,1,0:T(8,128)(2,1)} %copy-done.8, bf16[4,512]{1,0:T(4,128)(2,1)} %refs_3_.5, f32[4,4,1024]{2,1,0:T(4,128)} %log_ref.7, ...), custom_call_target="tpu_custom_call" | custom-call | flops 10000000000 | bytes 8388608 | tf_op jit(solution)/shard_map/prepare/pallas_call | solution.py:346
  78.7 0.5 collective-permute-start.2
  79.2 0.0 collective-permute-done.3.refs_2_.refs_4_
  79.2 0.0 copy-start.3
  79.2 0.0 collective-permute-done.4.refs_6_
  79.2 0.7 copy-done.3
  79.9 0.0 copy-start.7
  79.9 0.8 copy-done.7
  80.7 3.4 %state_step.5 = (bf16[4,128,256]{2,1,0:T(8,128)(2,1)}, bf16[8,128,128]{2,1,0:T(8,128)(2,1)}, bf16[8,128,128]{2,1,0:T(8,128)(2,1)}, bf16[8,2,128,128]{3,2,1,0:T(8,128)(2,1)}) custom-call(s32[1,8]{1,0:T(1,128)} %refs_0_.13, bf16[4,128,256]{2,1,0:T(8,128)(2,1)} %get-tuple-element.24.refs_3_.refs_1_, bf16[4,128,256]{2,1,0:T(8,128)(2,1)} %copy-done.3, ...), custom_call_target="tpu_custom_call" | custom-call | flops 1000000000 | bytes 1048576 | tf_op jit(solution)/shard_map/state_step/pallas_call | solution.py:563
  84.1 5.8 %all-to-all-start = ((bf16[8,2,128,128]{3,2,1,0:T(8,128)(2,1)}), bf16[8,2,128,128]{3,2,1,0:T(8,128)(2,1)S(1)}, u32[]{:S(2)}, u32[]{:S(2)}) async-start(bf16[8,2,128,128]{3,2,1,0:T(8,128)(2,1)} %get-tuple-element.38), calls=%async_computation | async-start | bytes 1048576 | tf_op jit(solution)/shard_map/all_to_all | solution.py:686
  89.9 0.0 collective-permute-start.5
  89.9 8.2 %outputs.4.refs_7_.held_ref = bf16[4,1024,512]{2,1,0:T(8,128)(2,1)} custom-call(s32[4]{0:T(128)} %after_ref.1, bf16[4,1024,256]{2,1,0:T(8,128)(2,1)} %get-tuple-element.21.qn_ref, bf16[4,1024,256]{2,1,0:T(8,128)(2,1)} %get-tuple-element.22.refs_7_.kn_ref, bf16[4,16,128,256]{3,2,1,0:T(8,128)(2,1)} %get-tuple-element.29.wu_ref, ...), custom_call_target="tpu_custom_call" | custom-call | flops 6000000000 | bytes 8388608 | tf_op jit(solution)/shard_map/outputs/pallas_call | solution.py:442
  98.1 0.0 collective-permute-done.2.refs_2_
  98.1 0.0 copy-start.2
  98.2 0.0 collective-permute-done.5.refs_6_
  98.2 0.7 copy-done.2
  98.9 0.0 copy-start.4
  98.9 0.7 copy-done.4
  99.6 2.4 %state_step.6 = (bf16[4,128,256]{2,1,0:T(8,128)(2,1)}, bf16[4,128,128]{2,1,0:T(8,128)(2,1)}, bf16[4,128,128]{2,1,0:T(8,128)(2,1)}) custom-call(s32[1,8]{1,0:T(1,128)} %refs_0_.13, bf16[4,128,256]{2,1,0:T(8,128)(2,1)} %get-tuple-element.27.refs_7_.refs_1_, bf16[4,128,256]{2,1,0:T(8,128)(2,1)} %copy-done.2, ...), custom_call_target="tpu_custom_call" | custom-call | flops 1000000000 | bytes 1048576 | tf_op jit(solution)/shard_map/state_step/pallas_call | solution.py:563
  102.0 0.0 collective-permute-start.6
  102.0 7.8 %outputs.5.refs_6_.held_ref = bf16[4,1024,512]{2,1,0:T(8,128)(2,1)} custom-call(s32[4]{0:T(128)} %after_ref.1, bf16[4,1024,256]{2,1,0:T(8,128)(2,1)} %get-tuple-element.21.qn_ref, bf16[4,1024,256]{2,1,0:T(8,128)(2,1)} %get-tuple-element.22.refs_7_.kn_ref, bf16[4,16,128,256]{3,2,1,0:T(8,128)(2,1)} %get-tuple-element.29.wu_ref, ...), custom_call_target="tpu_custom_call", output_to_operand_aliasing={{}: (10, {})} | custom-call | flops 6000000000 | bytes 8388608 | tf_op jit(solution)/shard_map/outputs/pallas_call | solution.py:442
  109.8 0.3 collective-permute-done.6.refs_4_
  110.1 0.0 copy-start.5
  110.1 0.7 copy-done.5
  110.8 2.5 %state_step.7 = (bf16[4,128,128]{2,1,0:T(8,128)(2,1)}, bf16[4,128,128]{2,1,0:T(8,128)(2,1)}, bf16[8,2,128,128]{3,2,1,0:T(8,128)(2,1)}) custom-call(s32[1,8]{1,0:T(1,128)} %refs_0_.13, bf16[4,128,256]{2,1,0:T(8,128)(2,1)} %get-tuple-element.27.refs_7_.refs_1_, bf16[4,128,256]{2,1,0:T(8,128)(2,1)} %copy-done.2, ...), custom_call_target="tpu_custom_call" | custom-call | flops 1000000000 | bytes 1048576 | tf_op jit(solution)/shard_map/state_step/pallas_call | solution.py:563
  113.4 0.0 all-to-all-done.refs_0_
  113.4 0.0 copy-start
  113.4 5.7 %all-to-all-start.1 = ((bf16[8,2,128,128]{3,2,1,0:T(8,128)(2,1)}), bf16[8,2,128,128]{3,2,1,0:T(8,128)(2,1)S(1)}, u32[]{:S(2)}, u32[]{:S(2)}) async-start(bf16[8,2,128,128]{3,2,1,0:T(8,128)(2,1)} %get-tuple-element.39), calls=%async_computation.1 | async-start | bytes 1048576 | tf_op jit(solution)/shard_map/all_to_all | solution.py:686
  119.1 7.9 %outputs.6.held_ref = bf16[4,1024,512]{2,1,0:T(8,128)(2,1)} custom-call(s32[4]{0:T(128)} %after_ref.1, bf16[4,1024,256]{2,1,0:T(8,128)(2,1)} %get-tuple-element.21.qn_ref, bf16[4,1024,256]{2,1,0:T(8,128)(2,1)} %get-tuple-element.22.refs_7_.kn_ref, bf16[2,16,128,256]{3,2,1,0:T(8,128)(2,1)} %get-tuple-element.35.wu_ref, ...), custom_call_target="tpu_custom_call", output_to_operand_aliasing={{}: (10, {})} | custom-call | flops 6000000000 | bytes 8388608 | tf_op jit(solution)/shard_map/outputs/pallas_call | solution.py:442
  127.0 0.0 copy-done
  127.0 7.9 %outputs.7 = bf16[4,1024,512]{2,1,0:T(8,128)(2,1)} custom-call(s32[4]{0:T(128)} %after_ref.1, bf16[4,1024,256]{2,1,0:T(8,128)(2,1)} %get-tuple-element.21.qn_ref, bf16[4,1024,256]{2,1,0:T(8,128)(2,1)} %get-tuple-element.22.refs_7_.kn_ref, bf16[2,16,128,256]{3,2,1,0:T(8,128)(2,1)} %get-tuple-element.25.wu_ref, ...), custom_call_target="tpu_custom_call", output_to_operand_aliasing={{}: (10, {})} | custom-call | flops 6000000000 | bytes 8388608 | tf_op jit(solution)/shard_map/outputs/pallas_call | solution.py:442
  134.9 0.0 all-to-all-done.1.refs_1_
  134.9 0.0 copy-start.1
  134.9 0.8 copy-done.1
  135.7 5.3 %deliver.1 = f32[8,4,128,128]{3,2,1,0:T(8,128)} custom-call(bf16[8,2,128,128]{3,2,1,0:T(8,128)(2,1)} %copy-done, bf16[8,2,128,128]{3,2,1,0:T(8,128)(2,1)} %copy-done.1), custom_call_target="tpu_custom_call" | custom-call | tf_op jit(solution)/shard_map/deliver/pallas_call | solution.py:583
  (3 shorter events, 0.0 us)
Async XLA Ops:
  2.2 3.2 %collective-permute-start = (bf16[4,32,128]{2,1,0:T(8,128)(2,1)S(1)}, bf16[4,32,128]{2,1,0:T(8,128)(2,1)S(1)}, u32[]{:S(2)}, u32[]{:S(2)}) collective-permute-start(bf16[4,32,128]{2,1,0:T(8,128)(2,1)S(1)} %pad_maximum_fusion), channel_id=1, source_target_pairs={{0,8},{8,16},{16,24},{1,9},{9,17},{17,25},{2,10},{10,18},{18,26},{... | collective-permute-start | bytes 98312 | tf_op jit(solution)/shard_map/ppermute | solution.py:635
  5.4 0.6 copy-start.8
  42.1 18.3 %collective-permute-start.1 = (bf16[8,128,256]{2,1,0:T(8,128)(2,1)}, bf16[8,128,256]{2,1,0:T(8,128)(2,1)S(1)}, u32[]{:S(2)}, u32[]{:S(2)}) collective-permute-start(bf16[8,128,256]{2,1,0:T(8,128)(2,1)} %get-tuple-element.23.refs_6_.refs_1_.refs_3_), channel_id=1, source_target_pairs={{0,8},{8,0},{16,24},{24,16},{1,9},{9,1},{17,25},{25,17},{2,10},{10... | collective-permute-start | bytes 1572872 | tf_op jit(solution)/shard_map/ppermute | solution.py:596
  60.3 18.9 %collective-permute-start.3 = (bf16[4,128,256]{2,1,0:T(8,128)(2,1)}, bf16[4,128,256]{2,1,0:T(8,128)(2,1)S(1)}, u32[]{:S(2)}, u32[]{:S(2)}) collective-permute-start(bf16[4,128,256]{2,1,0:T(8,128)(2,1)} %get-tuple-element.24.refs_3_.refs_1_), channel_id=1, source_target_pairs={{0,8},{8,0},{16,24},{24,16},{1,9},{9,1},{17,25},{25,17},{2,10},{10... | collective-permute-start | bytes 786440 | tf_op jit(solution)/shard_map/ppermute | solution.py:596
  60.4 0.8 copy-start.6
  63.5 15.7 %collective-permute-start.4 = (bf16[8,128,256]{2,1,0:T(8,128)(2,1)}, bf16[8,128,256]{2,1,0:T(8,128)(2,1)S(1)}, u32[]{:S(2)}, u32[]{:S(2)}) collective-permute-start(bf16[8,128,256]{2,1,0:T(8,128)(2,1)} %state_step.4.refs_6_.refs_5_), channel_id=1, source_target_pairs={{0,16},{8,24},{16,0},{24,8},{1,17},{9,25},{17,1},{25,9},{2,18},{10... | collective-permute-start | bytes 1572872 | tf_op jit(solution)/shard_map/ppermute | solution.py:603
  78.7 19.4 %collective-permute-start.2 = (bf16[4,128,256]{2,1,0:T(8,128)(2,1)}, bf16[4,128,256]{2,1,0:T(8,128)(2,1)S(1)}, u32[]{:S(2)}, u32[]{:S(2)}) collective-permute-start(bf16[4,128,256]{2,1,0:T(8,128)(2,1)} %get-tuple-element.27.refs_7_.refs_1_), channel_id=1, source_target_pairs={{0,8},{8,0},{16,24},{24,16},{1,9},{9,1},{17,25},{25,17},{2,10},{10... | collective-permute-start | bytes 786440 | tf_op jit(solution)/shard_map/ppermute | solution.py:596
  79.2 0.7 copy-start.3
  79.9 0.8 copy-start.7
  84.1 29.3 %all-to-all-start = ((bf16[8,2,128,128]{3,2,1,0:T(8,128)(2,1)}), bf16[8,2,128,128]{3,2,1,0:T(8,128)(2,1)S(1)}, u32[]{:S(2)}, u32[]{:S(2)}) async-start(bf16[8,2,128,128]{3,2,1,0:T(8,128)(2,1)} %get-tuple-element.38), calls=%async_computation | async-start | bytes 1048576 | tf_op jit(solution)/shard_map/all_to_all | solution.py:686
  89.9 8.2 %collective-permute-start.5 = (bf16[4,128,256]{2,1,0:T(8,128)(2,1)}, bf16[4,128,256]{2,1,0:T(8,128)(2,1)S(1)}, u32[]{:S(2)}, u32[]{:S(2)}) collective-permute-start(bf16[4,128,256]{2,1,0:T(8,128)(2,1)} %get-tuple-element.28.held_ref.after_ref.refs_5_), channel_id=1, source_target_pairs={{0,16},{8,24},{16,0},{24,8},{1,17},{9,25},{17,1},{25,9},{2,18},{10... | collective-permute-start | bytes 786440 | tf_op jit(solution)/shard_map/ppermute | solution.py:603
  98.1 0.7 copy-start.2
  98.9 0.7 copy-start.4
  102.0 8.2 %collective-permute-start.6 = (bf16[4,128,256]{2,1,0:T(8,128)(2,1)}, bf16[4,128,256]{2,1,0:T(8,128)(2,1)S(1)}, u32[]{:S(2)}, u32[]{:S(2)}) collective-permute-start(bf16[4,128,256]{2,1,0:T(8,128)(2,1)} %get-tuple-element.32.after_ref.refs_3_), channel_id=1, source_target_pairs={{0,16},{8,24},{16,0},{24,8},{1,17},{9,25},{17,1},{25,9},{2,18},{10... | collective-permute-start | bytes 786440 | tf_op jit(solution)/shard_map/ppermute | solution.py:603
  110.1 0.7 copy-start.5
  113.4 13.6 %copy-start = (bf16[8,2,128,128]{3,2,1,0:T(8,128)(2,1)}, bf16[8,2,128,128]{3,2,1,0:T(8,128)(2,1)S(1)}, u32[]{:S(2)}) copy-start(bf16[8,2,128,128]{3,2,1,0:T(8,128)(2,1)S(1)} %all-to-all-done.refs_0_) | copy-start | bytes 1572868
  113.4 21.5 %all-to-all-start.1 = ((bf16[8,2,128,128]{3,2,1,0:T(8,128)(2,1)}), bf16[8,2,128,128]{3,2,1,0:T(8,128)(2,1)S(1)}, u32[]{:S(2)}, u32[]{:S(2)}) async-start(bf16[8,2,128,128]{3,2,1,0:T(8,128)(2,1)} %get-tuple-element.39), calls=%async_computation.1 | async-start | bytes 1048576 | tf_op jit(solution)/shard_map/all_to_all | solution.py:686
  134.9 0.8 copy-start.1

commit v3 on v2

--- a/solution.py
+++ b/solution.py
@@ -13,11 +13,15 @@
 BLOCK = 128
 TINY = 16
 EDGE = 8
-HALF = BLOCK // 2
 EPSILON = 1e-06
-VMEM_BYTES = 56 * 1024 * 1024
+VMEM_BYTES = 40 * 1024 * 1024
+SMALL_VMEM_BYTES = 8 * 1024 * 1024
 F32 = jnp.float32
 BF16 = jnp.bfloat16
+
+
+def far(x):
+    return pltpu.with_memory_space_constraint(x, pltpu.HBM)
 
 
 def dot(a, b):
@@ -63,12 +67,32 @@
     return cum, gain
 
 
-def as_columns(rows, chunks):
-    parts = [rows[:, c * BLOCK : (c + 1) * BLOCK] for c in range(chunks)]
-    short = BLOCK - 8 * chunks
-    if short:
-        parts.append(jnp.zeros((short, BLOCK), F32))
-    return jnp.concatenate(parts, axis=0).T
+def block_bases(parts, chunks):
+    rows = jnp.concatenate(parts, axis=0)
+    short = 7 - rows.shape[0]
+    fill = [jnp.zeros((short, rows.shape[1]), F32)] if short else []
+    rows = jnp.concatenate([rows] + fill + [jnp.ones((1, rows.shape[1]), F32)], axis=0)
+    return [rows[:, c * BLOCK : (c + 1) * BLOCK] for c in range(chunks)]
+
+
+def spread_squares(base, group, kinds):
+    high = base.astype(BF16).astype(F32)
+    middle = (base - high).astype(BF16).astype(F32)
+    low = base - high - middle
+    parts = [high, middle, low]
+    row = lax.broadcasted_iota(jnp.int32, (32, BLOCK), 0)
+    which = row % 8
+    real = row < 24
+    stacked = jnp.concatenate(parts + [jnp.zeros_like(high)], axis=0)
+    left = jnp.where(jnp.logical_and(which == 7, real), 1.0, stacked).T.astype(BF16)
+    blocks = []
+    for h in range(group):
+        minus = jnp.concatenate([jnp.broadcast_to(-part[h : h + 1], (8, BLOCK)) for part in parts + [low]], axis=0)
+        blocks.append(jnp.where(which == h, 1.0, jnp.where(which == 7, minus, 0.0)))
+    for n in range(group, group * kinds):
+        blocks.append(jnp.where(which == n, 1.0, 0.0).astype(F32))
+    every = dot(left, jnp.concatenate(blocks, axis=1).astype(BF16))
+    return [every[:, n * BLOCK : (n + 1) * BLOCK] for n in range(group * kinds)]
 
 
 def mix(qk_ref, halo_ref, taps_ref, qn_ref, kn_ref, raw_scr, dense_scr, key_heads, chunks):
@@ -175,11 +199,7 @@
 
         cum, gain = gates_of_heads(log_ref, gain_ref, used, head, group)
         faded = jnp.exp(cum)
-        columns = as_columns(jnp.concatenate([cum, gain, gain * faded, faded], axis=0), chunks)
-
-        def column(which, h, c):
-            n = c * 8 + which * group + h
-            return columns[:, n : n + 1]
+        bases = block_bases([cum, gain, gain * faded], chunks)
 
         row = lax.broadcasted_iota(jnp.int32, (BLOCK, BLOCK), 0)
         lane = lax.broadcasted_iota(jnp.int32, (BLOCK, BLOCK), 1)
@@ -196,11 +216,15 @@
         compact = {}
         for c in range(chunks):
             kk = dot(keys[c], turned[c])
+            squares = spread_squares(bases[c], group, 3)
+            vc = mixed_rows(v_pad, v_taps, c, slice(0, group * DV)).astype(BF16).astype(F32)
+            kc = keys[c].astype(F32)
             for h in range(group):
                 r = h * chunks + c
-                span = slice(c * BLOCK, (c + 1) * BLOCK)
-                ratio = jnp.exp(column(0, h, c) - cum[h : h + 1, span])
-                strict = jnp.where(below, column(1, h, c) * ratio * kk, 0.0)
+                gain_square, fade_square = squares[group + h], squares[2 * group + h]
+                wu_ref[0, r, :, :DK] = (kc * fade_square).astype(BF16)
+                wu_ref[0, r, :, DK:] = (vc[:, h * DV : (h + 1) * DV] * gain_square).astype(BF16)
+                strict = jnp.where(below, gain_square * jnp.exp(squares[h]) * kk, 0.0)
                 a_scr[r] = strict.astype(BF16)
                 tiny = strict[0:TINY]
                 for b in range(1, BLOCK // TINY):
@@ -222,7 +246,7 @@
 
         run(1)
         size = TINY
-        while size < HALF:
+        while size < BLOCK:
             odd = [s for s in range(size, BLOCK, 2 * size)]
             half_lane = lax.broadcasted_iota(jnp.int32, (BLOCK // 2, BLOCK), 1)
             half_row = lax.broadcasted_iota(jnp.int32, (BLOCK // 2, BLOCK), 0)
@@ -247,25 +271,15 @@
             run(1)
             size *= 2
 
-        for c in range(chunks):
-            vc = mixed_rows(v_pad, v_taps, c, slice(0, group * DV)).astype(BF16).astype(F32)
-            kc = keys[c].astype(F32)
-            for h in range(group):
-                r = h * chunks + c
-                wu_ref[0, r, :, :DK] = (kc * column(2, h, c)).astype(BF16)
-                wu_ref[0, r, :, DK:] = (vc[:, h * DV : (h + 1) * DV] * column(1, h, c)).astype(BF16)
         run(1)
+        solved_rows = {}
         for h, c in units:
             r = h * chunks + c
-            wu_ref[0, r, :HALF] = dot(x_scr[r, :HALF, :HALF], wu_ref[0, r, :HALF]).astype(BF16)
-        run(1)
-        for h, c in units:
-            r = h * chunks + c
-            rest = wu_ref[0, r, HALF:].astype(F32) - dot(a_scr[r, HALF:, :HALF], wu_ref[0, r, :HALF])
-            wu_ref[0, r, HALF:] = rest.astype(BF16)
-        for h, c in units:
-            r = h * chunks + c
-            wu_ref[0, r, HALF:] = dot(x_scr[r, HALF:, HALF:], wu_ref[0, r, HALF:]).astype(BF16)
+            solved_rows[r] = dot(x_scr[r], wu_ref[0, r]).astype(BF16)
+            if len(solved_rows) == len(units) // 2:
+                run(1)
+        for r in solved_rows:
+            wu_ref[0, r] = solved_rows[r]
         run(len(todo))
         for c in range(chunks):
             sums = cum[:, c * BLOCK : (c + 1) * BLOCK]
@@ -276,7 +290,7 @@
                 r = h * chunks + c
                 fade_scr[slot, c, h : h + 1, :] = fade[h : h + 1]
                 scaled = (turned[c].astype(F32) * tail[h : h + 1, :]).astype(BF16)
-                both = dot(scaled, wu_ref[0, r])
+                both = dot(scaled, solved_rows[r])
                 m_scr[slot, c, h] = (-both[:, :DK]).astype(BF16)
                 b_scr[slot, c, h] = both[:, DK:]
 
@@ -300,7 +314,7 @@
     def whole_of(i, lengths):
         return (first + now(i), 0, 0)
 
-    operands = [v_in, halo, v_taps, log_decay, write_gain, after]
+    operands = [far(v_in), halo, far(v_taps), far(log_decay), far(write_gain), far(after)]
     in_specs = [
         pl.BlockSpec((1, tok, wide), lambda i, lengths: (first + now(i), 0, head)),
         pl.BlockSpec((1,) + halo.shape[1:], whole_of),
@@ -315,8 +329,8 @@
         pl.BlockSpec((group, DK, DV + DK), lambda i, lengths: (before(i), 0, 0)),
     ]
     out_shape = [
-        jax.ShapeDtypeStruct((count, rows, BLOCK, DK + DV), BF16),
-        jax.ShapeDtypeStruct((count, group, chunks * DK, DV + DK), BF16),
+        pltpu.HBM((count, rows, BLOCK, DK + DV), BF16),
+        pltpu.HBM((count, group, chunks * DK, DV + DK), BF16),
         jax.ShapeDtypeStruct((count * group, DK, DV + DK), BF16),
     ]
     scratch = [
@@ -329,19 +343,19 @@
         pltpu.VMEM((rows, BLOCK, BLOCK), BF16),
     ]
     if mixes:
-        operands += [qk_rows, qk_taps]
+        operands += [far(qk_rows), far(qk_taps)]
         in_specs += [
             pl.BlockSpec((1,) + qk_rows.shape[1:], whole_of),
             pl.BlockSpec(qk_taps.shape, lambda i, lengths: (0, 0)),
         ]
         out_specs += [pl.BlockSpec((1, tok, key_heads * DK), lambda i, lengths: (now(i), 0, 0))] * 2
-        out_shape += [jax.ShapeDtypeStruct((count, tok, key_heads * DK), BF16)] * 2
+        out_shape += [pltpu.HBM((count, tok, key_heads * DK), BF16)] * 2
         scratch += [
             pltpu.VMEM(qk_rows.shape[1:], F32),
             pltpu.VMEM((tok + EDGE, 2 * key_heads * DK), F32),
         ]
     else:
-        operands.append(mixed)
+        operands.append(far(mixed))
         in_specs.append(pl.BlockSpec((1, tok, DK), lambda i, lengths: (first + now(i), 0, head)))
     return pl.pallas_call(
         functools.partial(prepare_kernel, first, count, head, group, chunks, key_heads, mixes),
@@ -363,7 +377,7 @@
     first, head, group, chunks,
     length_ref, qn_ref, kn_ref, wu_ref, start_ref, log_ref, gain_ref, enter_ref, z_ref, norm_ref, held_ref, after_ref,
     out_ref,
-    first_scr, score_scr, raw_scr,
+    first_scr, score_scr, seen_scr,
 ):
     used = length_ref[first + pl.program_id(0)] - lax.axis_index("seq") * (chunks * BLOCK)
     units = [(h, c) for c in range(chunks) for h in range(group)]
@@ -376,11 +390,7 @@
     def _():
         cum, gain = gates_of_heads(log_ref, gain_ref, used, head, group)
         faded = jnp.exp(cum)
-        columns = as_columns(jnp.concatenate([cum, faded, gain, gain], axis=0), chunks)
-
-        def column(which, h, c):
-            n = c * 8 + which * group + h
-            return columns[:, n : n + 1]
+        bases = block_bases([cum, faded], chunks)
 
         row = lax.broadcasted_iota(jnp.int32, (BLOCK, BLOCK), 0)
         lane = lax.broadcasted_iota(jnp.int32, (BLOCK, BLOCK), 1)
@@ -395,20 +405,22 @@
             first_scr[h] = (moved + start_ref[0, h, :, :DV].astype(F32)).astype(BF16)
         for c in range(chunks):
             qk = dot(qn_ref[0, span(c), :], kn_ref[0, span(c), :].T)
+            squares = spread_squares(bases[c], group, 2)
+            q_wide = qn_ref[0, span(c), :].astype(F32)
             for h in range(group):
-                ratio = jnp.exp(column(0, h, c) - cum[h : h + 1, span(c)])
-                score_scr[h * chunks + c] = jnp.where(upto, ratio * qk, 0.0).astype(BF16)
+                r = h * chunks + c
+                score_scr[r] = jnp.where(upto, jnp.exp(squares[h]) * qk, 0.0).astype(BF16)
+                seen_scr[r] = q_wide * squares[group + h]
+        both, raws = {}, {}
         for h, c in units:
             r = h * chunks + c
-            both = dot(score_scr[r], wu_ref[0, r])
-            seen = qn_ref[0, span(c), :].astype(F32) * column(1, h, c) - both[:, :DK]
-            score_scr[r] = seen.astype(BF16)
-            raw_scr[r] = both[:, DK:]
+            both[r] = dot(score_scr[r], wu_ref[0, r])
         for h, c in units:
             r = h * chunks + c
-            raw_scr[r] += dot(score_scr[r], first_scr[h, span(c), :])
+            seen = (seen_scr[r] - both[r][:, :DK]).astype(BF16)
+            raws[r] = dot(seen, first_scr[h, span(c), :]) + both[r][:, DK:]
         for h, c in units:
-            raw = raw_scr[h * chunks + c]
+            raw = raws[h * chunks + c]
             cols = slice(h * DV, (h + 1) * DV)
             mean = jnp.sum(raw * raw, axis=-1, keepdims=True) * (1.0 / DV)
             gated = raw * lax.rsqrt(mean + EPSILON) * norm_gain * silu(z_ref[0, span(c), cols].astype(F32))
@@ -464,14 +476,14 @@
                 pltpu.VMEM((rows, BLOCK, DV), F32),
             ],
         ),
-        out_shape=jax.ShapeDtypeStruct((prompts, tok, width), BF16),
+        out_shape=pltpu.HBM((prompts, tok, width), BF16),
         input_output_aliases={} if empty else {10: 0},
         compiler_params=pltpu.CompilerParams(vmem_limit_bytes=VMEM_BYTES),
         cost_estimate=pl.CostEstimate(flops=3 * 10**9 * count, bytes_accessed=4 * 2**20 * count, transcendentals=10**6),
         name="outputs",
     )(
-        lengths, qn, kn, wu, starts, log_decay, write_gain, enter, gate_z,
-        norm_gain.reshape(1, DV), after if empty else held, lengths if after is held else after,
+        lengths, far(qn), far(kn), far(wu), far(starts), far(log_decay), far(write_gain), enter, far(gate_z),
+        far(norm_gain.reshape(1, DV)), far(after if empty else held), far(wu if after is held else after),
     )
 
 
@@ -567,10 +579,10 @@
         + [pl.BlockSpec(memory_space=pltpu.HBM)],
         out_specs=[vmem] * len(out_shape),
         out_shape=out_shape,
-        compiler_params=pltpu.CompilerParams(vmem_limit_bytes=VMEM_BYTES),
+        compiler_params=pltpu.CompilerParams(vmem_limit_bytes=SMALL_VMEM_BYTES),
         cost_estimate=pl.CostEstimate(flops=10**9, bytes_accessed=2**20, transcendentals=0),
         name="state_step",
-    )(*operands, after)
+    )(*operands, far(after))
 
 
 def deliver(parts):
@@ -578,13 +590,13 @@
 
     def kernel(*refs):
         for n, ref in enumerate(refs[:-1]):
-            refs[-1][0, n * group : (n + 1) * group] = ref[0].astype(F32)
+            refs[-1][:, n * group : (n + 1) * group] = ref[...].astype(F32)
 
     return pl.pallas_call(
         kernel,
-        grid=(count,),
-        in_specs=[pl.BlockSpec((1, group, DK, DV), lambda i: (i, 0, 0, 0))] * len(parts),
-        out_specs=pl.BlockSpec((1, group * len(parts), DK, DV), lambda i: (i, 0, 0, 0)),
+        grid=(2,),
+        in_specs=[pl.BlockSpec((count // 2, group, DK, DV), lambda i: (i, 0, 0, 0))] * len(parts),
+        out_specs=pl.BlockSpec((count // 2, group * len(parts), DK, DV), lambda i: (i, 0, 0, 0)),
         out_shape=jax.ShapeDtypeStruct((count, group * len(parts), DK, DV), F32),
         compiler_params=pltpu.CompilerParams(vmem_limit_bytes=VMEM_BYTES),
         name="deliver",

time: 142 us -> 133 us (0.937)
  Pallas kernels: 114 us -> 103 us
  starting transfers between devices: 17.3 us -> 19.9 us
    pallas_call x4, Pallas kernels: 10.6 us -> 6.46 us  [state_step(): pl.pallas_call(kernel, in_specs=[pl.BlockSpec(memory_space=pltpu.SMEM)] +...]
    pallas_call x1, Pallas kernels: 5.25 us -> 1.41 us  [deliver(): pl.pallas_call(kernel, grid=(2,), in_specs=[pl.BlockSpec((count // 2, gro...]
    pallas_call x3, Pallas kernels: 66.8 us -> 63.5 us  [prepare(): pl.pallas_call(functools.partial(prepare_kernel, first, count, head, grou...]
    ppermute x3, starting transfers between devices: 0.01 us -> 2.09 us  [from_chip_behind(): return lax.ppermute(block, 'seq', route)]
    unnamed x18 -> x32, local copies, waits for them, and re-layouts: 5.79 us -> 6.62 us
  transfers between devices with their start and end apart: 9 -> 9, of which waited for: 2 -> 1; matrix products, arithmetic and copies ran while one was open for 0% -> 0% of each run, Pallas kernels for 52% -> 52%
where the time goes in v3:
time: 133 us; the launch traced here: 132 us
  Pallas kernels  103 us (77%)
  starting transfers between devices  19.9 us (15%)
  local copies, waits for them, and re-layouts  8.15 us (6%)
    pallas_call x3, Pallas kernels, prepare(): pl.pallas_call(functools.partial(prepare_kernel, first, count, head, grou...  63.5 us
    pallas_call x4, Pallas kernels, outputs(): pl.pallas_call(functools.partial(outputs_kernel, begin, head, group, chun...  31.3 us
    all_to_all x2, starting transfers between devices, shards(): sent[jobs[t - 2][0]] = lax.all_to_all(results[2], 'head', 0, 0)  11.8 us
    unnamed x32, local copies, waits for them, and re-layouts  6.62 us
    pallas_call x4, Pallas kernels, state_step(): pl.pallas_call(kernel, in_specs=[pl.BlockSpec(memory_space=pltpu.SMEM)] +...  6.46 us
    ppermute x3, starting transfers between devices, pair_swap(): return lax.ppermute(block, 'seq', [(i, i ^ 1) for i in range(count)])  3.64 us
  transfers between devices with their start and end apart: 9, of which 1 were waited for; matrix products, arithmetic and copies ran while one was open for 0% of the time, Pallas kernels for 52%

profile of v3, /device:TPU:0, one launch (start us, length us, event | category | flops | bytes accessed | tf_op | source)
XLA Modules:
  0.0 132.4 jit_solution(8744878530988749664)
XLA Ops:
  0.6 0.7 slice.8
  1.4 0.8 slice.7
  2.2 2.4 %collective-permute-start = (bf16[4,32,128]{2,1,0:T(8,128)(2,1)S(1)}, bf16[4,32,128]{2,1,0:T(8,128)(2,1)S(1)}, u32[]{:S(2)}, u32[]{:S(2)}) collective-permute-start(bf16[4,32,128]{2,1,0:T(8,128)(2,1)S(1)} %pad_maximum_fusion), channel_id=1, source_target_pairs={{0,8},{8,16},{16,24},{1,9},{9,17},{17,25},{2,10},{10,18},{18,26},{... | collective-permute-start | bytes 98312 | tf_op jit(solution)/shard_map/ppermute | solution.py:647
  4.6 0.8 collective-permute-done.refs_2_
  5.4 0.0 copy-start.8
  5.4 0.7 copy-done.8
  6.1 32.6 %prepare.3 = (bf16[4,16,128,256]{3,2,1,0:T(8,128)(2,1)}, bf16[4,2,1024,256]{3,2,1,0:T(8,128)(2,1)}, bf16[8,128,256]{2,1,0:T(8,128)(2,1)S(1)}, bf16[4,1024,256]{2,1,0:T(8,128)(2,1)}, bf16[4,1024,256]{2,1,0:T(8,128)(2,1)}) custom-call(s32[4]{0:T(128)S(1)} %copy-done.8, bf16[4,1024,512]{2,1,0:T(8,128)(2,1)} %refs_1_.5, ...), custom_call_target="tpu_custom_call" | custom-call | flops 20000000000 | bytes 16777216 | tf_op jit(solution)/shard_map/prepare/pallas_call | solution.py:360
  38.7 0.0 copy-start.11
  38.7 2.8 %collective-permute-start.1 = (bf16[8,128,256]{2,1,0:T(8,128)(2,1)S(1)}, bf16[8,128,256]{2,1,0:T(8,128)(2,1)S(1)}, u32[]{:S(2)}, u32[]{:S(2)}) collective-permute-start(bf16[8,128,256]{2,1,0:T(8,128)(2,1)S(1)} %get-tuple-element.23.refs_6_.refs_1_.refs_3_), channel_id=1, source_target_pairs={{0,8},{8,0},{16,24},{24,16},{1,9},{9,1},{17,25},{25,17},{2,10},{10... | collective-permute-start | bytes 1572872 | tf_op jit(solution)/shard_map/ppermute | solution.py:608
  41.5 0.0 copy-done.11
  41.5 0.0 copy-start.10
  41.5 15.5 %prepare.4 = (bf16[2,16,128,256]{3,2,1,0:T(8,128)(2,1)}, bf16[2,2,1024,256]{3,2,1,0:T(8,128)(2,1)}, bf16[4,128,256]{2,1,0:T(8,128)(2,1)}) custom-call(s32[4]{0:T(128)S(1)} %copy-done.8, bf16[4,1024,512]{2,1,0:T(8,128)(2,1)} %refs_1_.5, bf16[4,32,128]{2,1,0:T(8,128)(2,1)S(1)} %collective-permute-done.refs_2_, bf16[4,512]{1,0:T(4,128)(2,1)} %refs_3_.5, ...), custom_call_target="tpu_custom_call" | custom-call | flops 10000000000 | bytes 8388608 | tf_op jit(solution)/shard_map/prepare/pallas_call | solution.py:360
  57.0 0.7 collective-permute-start.3
  57.8 0.0 collective-permute-done.1.refs_2_.refs_4_
  57.8 0.0 copy-done.10
  57.8 0.0 copy-start.12
  57.8 1.0 copy-done.12
  58.8 0.9 state_step.4.refs_6_.refs_5_
  59.7 0.0 copy-start.14
  59.7 0.0 copy-start.13
  59.7 0.1 collective-permute-start.4
  59.8 0.7 copy-done.14
  60.5 15.4 %prepare.5 = (bf16[2,16,128,256]{3,2,1,0:T(8,128)(2,1)}, bf16[2,2,1024,256]{3,2,1,0:T(8,128)(2,1)}, bf16[4,128,256]{2,1,0:T(8,128)(2,1)S(1)}) custom-call(s32[4]{0:T(128)S(1)} %copy-done.8, bf16[4,1024,512]{2,1,0:T(8,128)(2,1)} %refs_1_.5, bf16[4,32,128]{2,1,0:T(8,128)(2,1)S(1)} %collective-permute-done.refs_2_, bf16[4,512]{1,0:T(4,128)(2,1)} %refs_3_.5, ...), custom_call_target="tpu_custom_call" | custom-call | flops 10000000000 | bytes 8388608 | tf_op jit(solution)/shard_map/prepare/pallas_call | solution.py:360
  75.8 0.0 copy-start.2
  75.9 0.0 copy-start.9
  75.9 0.1 collective-permute-start.2
  75.9 0.0 collective-permute-done.3.refs_2_.refs_4_
  75.9 0.0 collective-permute-done.4.refs_6_
  76.0 0.6 copy-done.2
  76.6 0.0 copy-done.13
  76.6 0.0 copy-start.15
  76.6 1.0 copy-done.15
  77.6 2.5 %state_step.5 = (bf16[4,128,256]{2,1,0:T(8,128)(2,1)S(1)}, bf16[8,128,128]{2,1,0:T(8,128)(2,1)S(1)}, bf16[8,128,128]{2,1,0:T(8,128)(2,1)}, bf16[8,2,128,128]{3,2,1,0:T(8,128)(2,1)}) custom-call(s32[1,8]{1,0:T(1,128)S(1)} %copy-done.10, bf16[4,128,256]{2,1,0:T(8,128)(2,1)} %get-tuple-element.24.refs_3_.refs_1_, ...), custom_call_target="tpu_custom_call" | custom-call | flops 1000000000 | bytes 1048576 | tf_op jit(solution)/shard_map/state_step/pallas_call | solution.py:575
  80.1 0.0 copy-start.4
  80.1 5.8 %all-to-all-start = ((bf16[8,2,128,128]{3,2,1,0:T(8,128)(2,1)}), bf16[8,2,128,128]{3,2,1,0:T(8,128)(2,1)S(1)}, u32[]{:S(2)}, u32[]{:S(2)}) async-start(bf16[8,2,128,128]{3,2,1,0:T(8,128)(2,1)} %get-tuple-element.38), calls=%async_computation | async-start | bytes 1048576 | tf_op jit(solution)/shard_map/all_to_all | solution.py:698
  85.9 0.0 collective-permute-start.5
  86.0 0.0 copy-done.4
  86.0 0.0 copy-done.9
  86.0 0.0 copy-start.3
  86.0 7.9 %outputs.4.refs_7_.held_ref = bf16[4,1024,512]{2,1,0:T(8,128)(2,1)} custom-call(s32[4]{0:T(128)S(1)} %copy-done.9, bf16[4,1024,256]{2,1,0:T(8,128)(2,1)} %get-tuple-element.21.qn_ref, bf16[4,1024,256]{2,1,0:T(8,128)(2,1)} %get-tuple-element.22.refs_7_.kn_ref, bf16[4,16,128,256]{3,2,1,0:T(8,128)(2,1)} %get-tuple-element.29.wu_ref, ...), custom_call_target="tpu_custom_call" | custom-call | flops 6000000000 | bytes 8388608 | tf_op jit(solution)/shard_map/outputs/pallas_call | solution.py:454
  93.8 0.0 collective-permute-done.2.refs_2_
  93.8 0.1 collective-permute-done.5.refs_6_
  93.9 0.0 copy-done.3
  93.9 0.0 copy-start.5
  93.9 0.9 copy-done.5
  94.9 1.3 state_step.6
  96.1 0.0 copy-start
  96.1 2.0 %collective-permute-start.6 = (bf16[4,128,256]{2,1,0:T(8,128)(2,1)S(1)}, bf16[4,128,256]{2,1,0:T(8,128)(2,1)S(1)}, u32[]{:S(2)}, u32[]{:S(2)}) collective-permute-start(bf16[4,128,256]{2,1,0:T(8,128)(2,1)S(1)} %get-tuple-element.32.after_ref.refs_3_), channel_id=1, source_target_pairs={{0,16},{8,24},{16,0},{24,8},{1,17},{9,25},{17,1},{25,9},{2,18},{10... | collective-permute-start | bytes 786440 | tf_op jit(solution)/shard_map/ppermute | solution.py:615
  98.2 0.0 copy-done
  98.2 7.8 %outputs.5.refs_6_.held_ref = bf16[4,1024,512]{2,1,0:T(8,128)(2,1)} custom-call(s32[4]{0:T(128)S(1)} %copy-done.9, bf16[4,1024,256]{2,1,0:T(8,128)(2,1)} %get-tuple-element.21.qn_ref, bf16[4,1024,256]{2,1,0:T(8,128)(2,1)} %get-tuple-element.22.refs_7_.kn_ref, bf16[4,16,128,256]{3,2,1,0:T(8,128)(2,1)} %get-tuple-element.29.wu_ref, ...), custom_call_target="tpu_custom_call", output_to_operand_aliasing={{}: (10, {})} | custom-call | flops 6000000000 | bytes 8388608 | tf_op jit(solution)/shard_map/outputs/pallas_call | solution.py:454
  106.0 0.0 collective-permute-done.6.refs_4_
  106.0 0.0 copy-start.1
  106.0 0.9 copy-done.1
  107.0 1.8 %state_step.7 = (bf16[4,128,128]{2,1,0:T(8,128)(2,1)S(1)}, bf16[4,128,128]{2,1,0:T(8,128)(2,1)}, bf16[8,2,128,128]{3,2,1,0:T(8,128)(2,1)}) custom-call(s32[1,8]{1,0:T(1,128)S(1)} %copy-done.10, bf16[4,128,256]{2,1,0:T(8,128)(2,1)S(1)} %copy-done.3, bf16[4,128,256]{2,1,0:T(8,128)(2,1)S(1)} %collective-permute-done.2.refs_2_, ...), custom_call_target="tpu_custom_call" | custom-call | flops 1000000000 | bytes 1048576 | tf_op jit(solution)/shard_map/state_step/pallas_call | solution.py:575
  108.8 0.0 copy-start.6
  108.8 0.6 copy-done.6
  109.4 0.0 all-to-all-done.refs_0_
  109.4 6.0 %all-to-all-start.1 = ((bf16[8,2,128,128]{3,2,1,0:T(8,128)(2,1)}), bf16[8,2,128,128]{3,2,1,0:T(8,128)(2,1)S(1)}, u32[]{:S(2)}, u32[]{:S(2)}) async-start(bf16[8,2,128,128]{3,2,1,0:T(8,128)(2,1)} %get-tuple-element.39), calls=%async_computation.1 | async-start | bytes 1048576 | tf_op jit(solution)/shard_map/all_to_all | solution.py:698
  115.4 0.0 copy-start.7
  115.5 7.8 %outputs.6.held_ref = bf16[4,1024,512]{2,1,0:T(8,128)(2,1)} custom-call(s32[4]{0:T(128)S(1)} %copy-done.9, bf16[4,1024,256]{2,1,0:T(8,128)(2,1)} %get-tuple-element.21.qn_ref, bf16[4,1024,256]{2,1,0:T(8,128)(2,1)} %get-tuple-element.22.refs_7_.kn_ref, bf16[2,16,128,256]{3,2,1,0:T(8,128)(2,1)} %get-tuple-element.35.wu_ref, ...), custom_call_target="tpu_custom_call", output_to_operand_aliasing={{}: (10, {})} | custom-call | flops 6000000000 | bytes 8388608 | tf_op jit(solution)/shard_map/outputs/pallas_call | solution.py:454
  123.2 0.0 copy-done.7
  123.2 7.8 %outputs.7 = bf16[4,1024,512]{2,1,0:T(8,128)(2,1)} custom-call(s32[4]{0:T(128)S(1)} %copy-done.9, bf16[4,1024,256]{2,1,0:T(8,128)(2,1)} %get-tuple-element.21.qn_ref, bf16[4,1024,256]{2,1,0:T(8,128)(2,1)} %get-tuple-element.22.refs_7_.kn_ref, bf16[2,16,128,256]{3,2,1,0:T(8,128)(2,1)} %get-tuple-element.25.wu_ref.after_ref, ...), custom_call_target="tpu_custom_call", output_to_operand_aliasing={{}: (10, {})} | custom-call | flops 6000000000 | bytes 8388608 | tf_op jit(solution)/shard_map/outputs/pallas_call | solution.py:454
  131.0 0.0 all-to-all-done.1.refs_1_
  131.0 1.4 %deliver.1 = f32[8,4,128,128]{3,2,1,0:T(8,128)} custom-call(bf16[8,2,128,128]{3,2,1,0:T(8,128)(2,1)S(1)} %all-to-all-done.refs_0_, bf16[8,2,128,128]{3,2,1,0:T(8,128)(2,1)S(1)} %all-to-all-done.1.refs_1_), custom_call_target="tpu_custom_call" | custom-call | tf_op jit(solution)/shard_map/deliver/pallas_call | solution.py:595
  (3 shorter events, 0.0 us)
Async XLA Ops:
  2.2 3.2 %collective-permute-start = (bf16[4,32,128]{2,1,0:T(8,128)(2,1)S(1)}, bf16[4,32,128]{2,1,0:T(8,128)(2,1)S(1)}, u32[]{:S(2)}, u32[]{:S(2)}) collective-permute-start(bf16[4,32,128]{2,1,0:T(8,128)(2,1)S(1)} %pad_maximum_fusion), channel_id=1, source_target_pairs={{0,8},{8,16},{16,24},{1,9},{9,17},{17,25},{2,10},{10,18},{18,26},{... | collective-permute-start | bytes 98312 | tf_op jit(solution)/shard_map/ppermute | solution.py:647
  5.4 0.7 copy-start.8
  38.7 2.8 %copy-start.11 = (bf16[8,128,256]{2,1,0:T(8,128)(2,1)}, bf16[8,128,256]{2,1,0:T(8,128)(2,1)S(1)}, u32[]{:S(2)}) copy-start(bf16[8,128,256]{2,1,0:T(8,128)(2,1)S(1)} %get-tuple-element.23.refs_6_.refs_1_.refs_3_) | copy-start | bytes 1572868
  38.7 19.1 %collective-permute-start.1 = (bf16[8,128,256]{2,1,0:T(8,128)(2,1)S(1)}, bf16[8,128,256]{2,1,0:T(8,128)(2,1)S(1)}, u32[]{:S(2)}, u32[]{:S(2)}) collective-permute-start(bf16[8,128,256]{2,1,0:T(8,128)(2,1)S(1)} %get-tuple-element.23.refs_6_.refs_1_.refs_3_), channel_id=1, source_target_pairs={{0,8},{8,0},{16,24},{24,16},{1,9},{9,1},{17,25},{25,17},{2,10},{10... | collective-permute-start | bytes 1572872 | tf_op jit(solution)/shard_map/ppermute | solution.py:608
  41.5 16.3 %copy-start.10 = (s32[1,8]{1,0:T(1,128)S(1)}, s32[1,8]{1,0:T(1,128)}, u32[]{:S(2)}) copy-start(s32[1,8]{1,0:T(1,128)} %refs_0_.13) | copy-start | bytes 100
  57.0 18.9 %collective-permute-start.3 = (bf16[4,128,256]{2,1,0:T(8,128)(2,1)}, bf16[4,128,256]{2,1,0:T(8,128)(2,1)S(1)}, u32[]{:S(2)}, u32[]{:S(2)}) collective-permute-start(bf16[4,128,256]{2,1,0:T(8,128)(2,1)} %get-tuple-element.24.refs_3_.refs_1_), channel_id=1, source_target_pairs={{0,8},{8,0},{16,24},{24,16},{1,9},{9,1},{17,25},{25,17},{2,10},{10... | collective-permute-start | bytes 786440 | tf_op jit(solution)/shard_map/ppermute | solution.py:608
  57.8 1.0 copy-start.12
  59.7 0.8 copy-start.14
  59.7 16.9 %copy-start.13 = (bf16[8,128,256]{2,1,0:T(8,128)(2,1)S(1)}, bf16[8,128,256]{2,1,0:T(8,128)(2,1)}, u32[]{:S(2)}) copy-start(bf16[8,128,256]{2,1,0:T(8,128)(2,1)} %copy-done.11) | copy-start | bytes 1572868
  59.7 16.2 %collective-permute-start.4 = (bf16[8,128,256]{2,1,0:T(8,128)(2,1)S(1)}, bf16[8,128,256]{2,1,0:T(8,128)(2,1)S(1)}, u32[]{:S(2)}, u32[]{:S(2)}) collective-permute-start(bf16[8,128,256]{2,1,0:T(8,128)(2,1)S(1)} %state_step.4.refs_6_.refs_5_), channel_id=1, source_target_pairs={{0,16},{8,24},{16,0},{24,8},{1,17},{9,25},{17,1},{25,9},{2,18},{10... | collective-permute-start | bytes 1572872 | tf_op jit(solution)/shard_map/ppermute | solution.py:615
  75.8 0.7 copy-start.2
  75.9 10.1 %copy-start.9 = (s32[4]{0:T(128)S(1)}, s32[4]{0:T(128)}, u32[]{:S(2)}) copy-start(s32[4]{0:T(128)} %length_ref.7) | copy-start | bytes 52
  75.9 18.0 %collective-permute-start.2 = (bf16[4,128,256]{2,1,0:T(8,128)(2,1)S(1)}, bf16[4,128,256]{2,1,0:T(8,128)(2,1)S(1)}, u32[]{:S(2)}, u32[]{:S(2)}) collective-permute-start(bf16[4,128,256]{2,1,0:T(8,128)(2,1)S(1)} %get-tuple-element.27.refs_7_.refs_1_), channel_id=1, source_target_pairs={{0,8},{8,0},{16,24},{24,16},{1,9},{9,1},{17,25},{25,17},{2,10},{10... | collective-permute-start | bytes 786440 | tf_op jit(solution)/shard_map/ppermute | solution.py:608
  76.6 1.0 copy-start.15
  80.1 5.8 %copy-start.4 = (bf16[4,128,256]{2,1,0:T(8,128)(2,1)}, bf16[4,128,256]{2,1,0:T(8,128)(2,1)S(1)}, u32[]{:S(2)}) copy-start(bf16[4,128,256]{2,1,0:T(8,128)(2,1)S(1)} %get-tuple-element.28.held_ref.after_ref.refs_5_) | copy-start | bytes 786436
  80.1 29.3 %all-to-all-start = ((bf16[8,2,128,128]{3,2,1,0:T(8,128)(2,1)}), bf16[8,2,128,128]{3,2,1,0:T(8,128)(2,1)S(1)}, u32[]{:S(2)}, u32[]{:S(2)}) async-start(bf16[8,2,128,128]{3,2,1,0:T(8,128)(2,1)} %get-tuple-element.38), calls=%async_computation | async-start | bytes 1048576 | tf_op jit(solution)/shard_map/all_to_all | solution.py:698
  85.9 8.0 %collective-permute-start.5 = (bf16[4,128,256]{2,1,0:T(8,128)(2,1)S(1)}, bf16[4,128,256]{2,1,0:T(8,128)(2,1)S(1)}, u32[]{:S(2)}, u32[]{:S(2)}) collective-permute-start(bf16[4,128,256]{2,1,0:T(8,128)(2,1)S(1)} %get-tuple-element.28.held_ref.after_ref.refs_5_), channel_id=1, source_target_pairs={{0,16},{8,24},{16,0},{24,8},{1,17},{9,25},{17,1},{25,9},{2,18},{10... | collective-permute-start | bytes 786440 | tf_op jit(solution)/shard_map/ppermute | solution.py:615
  86.0 7.9 %copy-start.3 = (bf16[4,128,256]{2,1,0:T(8,128)(2,1)S(1)}, bf16[4,128,256]{2,1,0:T(8,128)(2,1)}, u32[]{:S(2)}) copy-start(bf16[4,128,256]{2,1,0:T(8,128)(2,1)} %copy-done.2) | copy-start | bytes 786436
  93.9 1.0 copy-start.5
  96.1 2.0 %copy-start = (bf16[4,128,256]{2,1,0:T(8,128)(2,1)}, bf16[4,128,256]{2,1,0:T(8,128)(2,1)S(1)}, u32[]{:S(2)}) copy-start(bf16[4,128,256]{2,1,0:T(8,128)(2,1)S(1)} %get-tuple-element.32.after_ref.refs_3_) | copy-start | bytes 786436
  96.1 9.9 %collective-permute-start.6 = (bf16[4,128,256]{2,1,0:T(8,128)(2,1)S(1)}, bf16[4,128,256]{2,1,0:T(8,128)(2,1)S(1)}, u32[]{:S(2)}, u32[]{:S(2)}) collective-permute-start(bf16[4,128,256]{2,1,0:T(8,128)(2,1)S(1)} %get-tuple-element.32.after_ref.refs_3_), channel_id=1, source_target_pairs={{0,16},{8,24},{16,0},{24,8},{1,17},{9,25},{17,1},{25,9},{2,18},{10... | collective-permute-start | bytes 786440 | tf_op jit(solution)/shard_map/ppermute | solution.py:615
  106.0 1.0 copy-start.1
  108.8 0.7 copy-start.6
  109.4 21.6 %all-to-all-start.1 = ((bf16[8,2,128,128]{3,2,1,0:T(8,128)(2,1)}), bf16[8,2,128,128]{3,2,1,0:T(8,128)(2,1)S(1)}, u32[]{:S(2)}, u32[]{:S(2)}) async-start(bf16[8,2,128,128]{3,2,1,0:T(8,128)(2,1)} %get-tuple-element.39), calls=%async_computation.1 | async-start | bytes 1048576 | tf_op jit(solution)/shard_map/all_to_all | solution.py:698
  115.4 7.8 %copy-start.7 = (bf16[4,128,128]{2,1,0:T(8,128)(2,1)S(1)}, bf16[4,128,128]{2,1,0:T(8,128)(2,1)}, u32[]{:S(2)}) copy-start(bf16[4,128,128]{2,1,0:T(8,128)(2,1)} %copy-done.6) | copy-start | bytes 393220
